TPU v7x, 128 devices: a whole 4x4x4 slice. The times are simulated.
128 devices in a mesh: src: 8 (over y, x_lo), rcv: 16 (over z, x_hi, core).
Axes of the slice: x: 4 (x_hi: 2, x_lo: 2; x = x_hi * 2 + x_lo), y: 4, z: 4, core: 2. Of those that a mesh axis runs over, the one named last changes fastest.
Arguments:
- raw: bfloat16 [128, 2048, 512], P(('src', 'rcv')), may hold values from -60 to 60
- quality: int32 [128, 2048], P(('src', 'rcv')), may hold values 0 or 1
- channel_order: int32 [2048], replicated, may hold values from 0 to 2047, each once
- slab_order: int32 [4], replicated, may hold values from 0 to 3, each once
Outputs:
- cross: float32 [2, 64, 2048, 2048], P(None, None, 'src', 'rcv')
All inputs are finite; a program needn't handle non-finite values. No bound on the sum of `quality` on one device may be relied on, other than what follows from the above.
Results may differ from a plain program's by a relative error of at most 0.0066.
Values may be sent and summed in bfloat16 or wider, within the bound.
No kernel may reach another device: no remote copies, remote signals or barrier semaphores. Data moves between devices by JAX's collectives and lax.ppermute only.
A program may use at most 128 MiB of HBM per device.

v0:
```python
import math

import jax
import jax.numpy as jnp
from jax import lax
from jax.sharding import PartitionSpec as P

F = 64
HALF = 12
BAND = 2
WIN_SLAB = 32


def band_matrix(length, half_width):
    rows = jnp.arange(length)[:, None]
    cols = jnp.arange(length)[None, :]
    inside = (jnp.abs(rows - cols) <= half_width).astype(jnp.float32)
    return inside / jnp.sum(inside, axis=0, keepdims=True)


def fourier_table(samples, bin_count):
    times = jnp.arange(samples, dtype=jnp.int32)[:, None]
    harmonic = jnp.arange(1, bin_count + 1, dtype=jnp.int32)[None, :]
    phase = 2.0 * math.pi / samples * (times * harmonic % samples).astype(jnp.float32)
    return jnp.concatenate([jnp.cos(phase), -jnp.sin(phase)], axis=1).astype(jnp.bfloat16)


def slab_amplitude(slab_order, window_ids):
    count = slab_order.shape[0]
    positions = jnp.arange(count, dtype=jnp.int32)
    slab_ages = jnp.sum(
        jnp.where(slab_order[:, None] == positions[None, :], positions[:, None], 0), axis=0
    )
    amplitude = 0.5 ** (slab_ages.astype(jnp.float32) / count)
    slab_of = window_ids // WIN_SLAB
    onehot = (slab_of[:, None] == positions[None, :]).astype(jnp.float32)
    return jnp.sum(onehot * amplitude[None, :], axis=1)


def running_mean(magnitude):
    samples = magnitude.shape[2]
    padded = jnp.pad(magnitude, ((0, 0), (0, 0), (HALF, HALF)))
    window_sum = padded[:, :, 0:samples]
    for lag_index in range(1, 2 * HALF + 1):
        window_sum = window_sum + padded[:, :, lag_index : lag_index + samples]
    places = jnp.arange(samples, dtype=jnp.int32)
    upper = jnp.minimum(places + HALF + 1, samples)
    lower = jnp.maximum(places - HALF, 0)
    return window_sum / (upper - lower).astype(jnp.float32)[None, None, :]


def whiten(windows, keep_mask, window_ids, slab_order):
    samples = windows.shape[2]
    centred = windows.astype(jnp.float32)
    centred = centred - jnp.mean(centred, axis=2, keepdims=True)
    magnitude = jnp.abs(centred)
    envelope = running_mean(magnitude)
    level = jnp.mean(magnitude, axis=2, keepdims=True) + 1e-06
    normed = (centred / (envelope + 0.25 * level)).astype(jnp.bfloat16)
    spectrum = jnp.einsum(
        "wcn,nk->wck", normed, fourier_table(samples, F), preferred_element_type=jnp.float32
    )
    real_part = spectrum[:, :, :F]
    imag_part = spectrum[:, :, F:]
    spectral_power = real_part * real_part + imag_part * imag_part
    smooth = jnp.einsum(
        "wck,kj->wcj", spectral_power, band_matrix(F, BAND), precision=lax.Precision.HIGHEST
    )
    total = jnp.mean(spectral_power, axis=2, keepdims=True) + 1e-06
    amplitude = slab_amplitude(slab_order, window_ids)
    weight = keep_mask.astype(jnp.float32) * amplitude[:, None]
    white_scale = weight[:, :, None] / jnp.sqrt(smooth + 0.1 * total)
    return (spectrum * jnp.concatenate([white_scale, white_scale], axis=2)).astype(jnp.bfloat16)


def cross_block(row_white, col_white):
    window_total, row_count, double_bins = row_white.shape
    col_count = col_white.shape[1]
    rows_four = row_white.reshape(window_total, row_count, 2, double_bins // 2)
    cols_four = col_white.reshape(window_total, col_count, 2, double_bins // 2)
    swapped = jnp.stack([rows_four[:, :, 1], -rows_four[:, :, 0]], axis=2)
    real_sum = jnp.einsum(
        "wapf,wbpf->fab", rows_four, cols_four, preferred_element_type=jnp.float32
    )
    imag_sum = jnp.einsum("wapf,wbpf->fab", swapped, cols_four, preferred_element_type=jnp.float32)
    return jnp.stack([real_sum, imag_sum]) * (1.0 / math.sqrt(window_total))


def body(raw, quality, channel_order, slab_order):
    ordered = jnp.take(raw, channel_order, axis=1)
    keep_local = jnp.take(quality, channel_order, axis=1)
    owner_raw, owner_keep = (
        lax.all_to_all(ordered, ("src", "rcv"), split_axis=1, concat_axis=0, tiled=True),
        lax.all_to_all(
            keep_local.astype(jnp.bfloat16), ("src", "rcv"), split_axis=1, concat_axis=0, tiled=True
        ),
    )
    window_total = owner_raw.shape[0]
    owner_white = whiten(
        owner_raw, owner_keep, jnp.arange(window_total, dtype=jnp.int32), slab_order
    )
    columns = lax.all_gather(owner_white, "src", axis=1, tiled=True)
    return cross_block(lax.all_gather(owner_white, "rcv", axis=1, tiled=True), columns)


def solution(mesh):
    in_specs = (P(("src", "rcv"), None, None), P(("src", "rcv"), None), P(), P())
    out_specs = P(None, None, "src", "rcv")
    return jax.shard_map(body, mesh=mesh, in_specs=in_specs, out_specs=out_specs, check_vma=False)
```

profile of v0, /device:TPU:1, one launch (start us, length us, event | category | flops | bytes accessed | tf_op | source)
XLA Modules:
  0.0 443.1 jit_solution(10840147500958241496)
XLA Ops:
  6.5 0.9 fusion.59
  7.4 11.8 %gather_fusion.1 = s32[2048]{0:T(1024)S(1)} fusion(s32[2048]{0:T(1024)S(1)} %bitcast.34, s32[2048]{0:T(1024)S(1)} %fusion.59), kind=kCustom, calls=%fused_computation.1 | custom fusion | bytes 24576 | tf_op jit(solution)/shard_map/jit(_take)/gather | solution.py:91
  19.2 0.7 reshape.196
  19.9 11.5 %all-to-all-start.1 = ((bf16[1,128,16]{2,0,1:T(2,128)(2,1)}), bf16[1,128,16]{2,0,1:T(2,128)(2,1)S(1)}, u32[]{:S(2)}, u32[]{:S(2)}) async-start(bf16[1,128,16]{2,0,1:T(2,128)(2,1)} %reshape.196), calls=%async_computation.1 | async-start | bytes 131072 | tf_op jit(solution)/shard_map/all_to_all | solution.py:94
  31.5 9.2 %gather_fusion = bf16[2048,512]{1,0:T(8,128)(2,1)} fusion(bf16[2048,512]{1,0:T(8,128)(2,1)S(1)} %bitcast.33, s32[2048]{0:T(1024)S(1)} %fusion.59), kind=kCustom, calls=%fused_computation | custom fusion | bytes 4202496 | tf_op jit(solution)/shard_map/jit(_take)/gather | solution.py:90
  40.7 1.8 bitcast_select_fusion
  42.4 18.5 %copy.80 = bf16[1,2048,512]{2,0,1:T(2,128)(2,1)} copy(bf16[1,2048,512]{2,1,0:T(8,128)(2,1)S(1)} %bitcast_select_fusion) | data formatting | bytes 4194304 | tf_op jit(solution)/shard_map/jit(_take)/select_n | solution.py:90
  61.5 14.0 %reduce.2 = bf16[2048,512]{1,0:T(8,128)(2,1)S(1)} reduce(bf16[2048,1,512]{2,1,0:T(2,128)(2,1)} %bitcast.41, bf16[]{:T(256)} %broadcast.218), dimensions={1}, to_apply=%bitcast.32.reduce_sub_computation | reduce | bytes 4194306
  75.6 2.8 reshape.197
  78.3 9.8 %all-to-all-start = ((bf16[128,2,4096]{2,1,0:T(2,128)(2,1)}), bf16[128,2,4096]{2,1,0:T(2,128)(2,1)S(1)}, u32[]{:S(2)}, u32[]{:S(2)}) async-start(bf16[128,2,4096]{2,1,0:T(2,128)(2,1)} %reshape.197), calls=%async_computation | async-start | bytes 4194304 | tf_op jit(solution)/shard_map/all_to_all | solution.py:93
  88.6 0.6 cosine_convert_fusion
  89.5 28.6 %all-to-all-done = bf16[128,2,4096]{2,1,0:T(2,128)(2,1)S(1)} async-done(((bf16[128,2,4096]{2,1,0:T(2,128)(2,1)}), bf16[128,2,4096]{2,1,0:T(2,128)(2,1)S(1)}, u32[]{:S(2)}, u32[]{:S(2)}) %all-to-all-start) | async-done | bytes 2097184 | tf_op jit(solution)/shard_map/all_to_all | solution.py:93
  118.1 6.7 %reshape.198 = bf16[2048,1,512]{2,1,0:T(2,128)(2,1)} reshape(bf16[128,2,4096]{2,1,0:T(2,128)(2,1)S(1)} %all-to-all-done) | data formatting | bytes 4194304
  124.8 16.9 %convert_reduce_fusion.1 = f32[2048]{0:T(1024)S(1)} fusion(bf16[2048,1,512]{2,1,0:T(2,128)(2,1)} %reshape.198), kind=kLoop, calls=%fused_computation.122 | loop fusion | flops 2095104 | bytes 2105344 | tf_op jit(solution)/shard_map/reduce_sum | solution.py:55
  141.8 29.4 %abs_reduce_fusion = f32[2048]{0:T(1024)S(1)} fusion(f32[2048]{0:T(1024)S(1)} %broadcast_multiply_fusion.1, bf16[2048,1,512]{2,1,0:T(2,128)(2,1)S(1)} %copy-done.4), kind=kLoop, calls=%fused_computation.58 | loop fusion | flops 4192256 | bytes 2113536 | tf_op jit(solution)/shard_map/reduce_sum | solution.py:58
  171.5 2.7 copy.60
  174.2 2.7 fusion.28
  177.0 27.4 %divide_convert_fusion.5 = bf16[128,16,512]{2,0,1:T(8,128)(2,1)S(1)} fusion(f32[128,16,512]{2,0,1:T(8,128)S(1)} %fusion.28, f32[128,16,512]{2,1,0:T(8,128)S(1)} %bitcast.37, f32[128,16]{0,1:T(8,128)S(1)} %copy.46, f32[512]{0:T(512)S(1)} %fusion.62, f32[128,16]{0,1:T(8,128)S(1)} %copy.44), kind=kLoop, calls=%fused_computation.57.clone.clone.2 | loop fusion | flops 30408704 | bytes 10504192 | tf_op jit(solution)/shard_map/wcn,nk->wck/dot_general | solution.py:60
  204.4 0.8 fusion.40
  205.3 0.7 fusion.42
  206.1 1.0 copy.49
  207.2 0.7 all-gather.3.cloned.1.call-update
  207.9 86.0 %all-gather.5.cloned.1.call-done = bf16[128,128,128]{2,0,1:T(8,128)(2,1)} async-done(((bf16[128,16,128]{2,0,1:T(8,128)(2,1)}), bf16[128,128,128]{2,0,1:T(8,128)(2,1)}) %all-gather.5.cloned.1.call-update) | async-done | bytes 4194320 | tf_op jit(solution)/shard_map/all_gather | solution.py:102
  293.9 6.9 %copy.52 = bf16[128,128,128]{1,2,0:T(8,128)(2,1)} copy(bf16[128,128,128]{2,0,1:T(8,128)(2,1)} %all-gather.5.cloned.1.call-done) | data formatting | bytes 8388608 | tf_op jit(solution)/shard_map/all_gather | solution.py:102
  300.9 69.3 %all-gather.3.cloned.1.call-done = bf16[128,256,128]{2,0,1:T(8,128)(2,1)} async-done(((bf16[128,16,128]{2,0,1:T(8,128)(2,1)}), bf16[128,256,128]{2,0,1:T(8,128)(2,1)}) %all-gather.3.cloned.1.call-update) | async-done | bytes 8388624 | tf_op jit(solution)/shard_map/all_gather | solution.py:103
  370.2 13.0 %copy.50 = bf16[128,256,128]{1,2,0:T(8,128)(2,1)} copy(bf16[128,256,128]{2,0,1:T(8,128)(2,1)} %all-gather.3.cloned.1.call-done) | data formatting | bytes 16777216 | tf_op jit(solution)/shard_map/all_gather | solution.py:103
  383.2 12.8 %copy.53 = bf16[128,256,2,64]{0,1,2,3:T(8,128)(2,1)} copy(bf16[128,256,2,64]{1,3,2,0:T(8,128)(2,1)} %bitcast.40) | data formatting | bytes 16777216 | tf_op jit(solution)/shard_map/reshape | solution.py:79
  396.0 6.9 %fusion.68 = (bf16[128,256,1,64]{0,1,2,3:T(8,128)(2,1)}, bf16[128,256,1,64]{0,1,2,3:T(8,128)(2,1)}) fusion(bf16[128,256,2,64]{0,1,2,3:T(8,128)(2,1)} %copy.53), kind=kLoop, calls=%fused_computation.125 | loop fusion | flops 2097152 | bytes 16777216 | tf_op jit(solution)/shard_map/slice | solution.py:81
  402.9 1.8 copy-done.3
  404.8 8.0 %fusion.32 = f32[1,64,256,128]{3,2,1,0:T(8,128)S(1)} fusion(bf16[128,256,2,64]{0,1,2,3:T(8,128)(2,1)S(1)} %copy-done.3, bf16[128,128,2,64]{1,3,2,0:T(8,128)(2,1)} %bitcast.38), kind=kOutput, calls=%fused_computation.63 | convolution fusion | flops 1073741824 | bytes 20971520 | tf_op jit(solution)/shard_map/wapf,wbpf->fab/dot_general | solution.py:82
  412.7 13.4 %fusion.35 = f32[1,64,256,128]{3,2,1,0:T(8,128)} fusion(bf16[128,128,2,64]{1,3,2,0:T(8,128)(2,1)} %bitcast.39, bf16[128,256,1,64]{0,1,2,3:T(8,128)(2,1)} %get-tuple-element.8, bf16[128,256,1,64]{0,1,2,3:T(8,128)(2,1)} %get-tuple-element.7), kind=kOutput, calls=%fused_computation.64 | convolution fusion | flops 1077936128 | bytes 20971520 | tf_op jit(solution)/shard_map/wapf,wbpf->fab/dot_general | solution.py:85
  426.2 10.1 %maximum_multiply_fusion = f32[2,64,256,128]{3,2,1,0:T(8,128)} fusion(f32[1,64,256,128]{3,2,1,0:T(8,128)} %fusion.35, f32[1,64,256,128]{3,2,1,0:T(8,128)S(1)} %fusion.32), kind=kLoop, calls=%fused_computation.2 | loop fusion | flops 8388608 | bytes 33554432 | tf_op jit(solution)/shard_map/mul | solution.py:86
  (38 shorter events, 1.9 us)
Async XLA Ops:
  6.5 24.9 %copy-start = (bf16[1,2048,512]{2,1,0:T(8,128)(2,1)S(1)}, bf16[1,2048,512]{2,1,0:T(8,128)(2,1)}, u32[]{:S(2)}) copy-start(bf16[1,2048,512]{2,1,0:T(8,128)(2,1)} %param.4) | copy-start | bytes 6291460
  6.5 0.9 copy-start.2
  7.4 11.8 %copy-start.5 = (s32[2048]{0:T(1024)S(1)}, s32[2048]{0:T(1024)}, u32[]{:S(2)}) copy-start(s32[2048]{0:T(1024)} %param.6) | copy-start | bytes 24580
  19.9 58.4 %all-to-all-start.1 = ((bf16[1,128,16]{2,0,1:T(2,128)(2,1)}), bf16[1,128,16]{2,0,1:T(2,128)(2,1)S(1)}, u32[]{:S(2)}, u32[]{:S(2)}) async-start(bf16[1,128,16]{2,0,1:T(2,128)(2,1)} %reshape.196), calls=%async_computation.1 | async-start | bytes 131072 | tf_op jit(solution)/shard_map/all_to_all | solution.py:94
  75.6 12.9 %copy-start.6 = (s32[4]{0:T(128)S(1)}, s32[4]{0:T(128)}, u32[]{:S(2)}) copy-start(s32[4]{0:T(128)} %param.7) | copy-start | bytes 52
  78.3 39.8 %all-to-all-start = ((bf16[128,2,4096]{2,1,0:T(2,128)(2,1)}), bf16[128,2,4096]{2,1,0:T(2,128)(2,1)S(1)}, u32[]{:S(2)}, u32[]{:S(2)}) async-start(bf16[128,2,4096]{2,1,0:T(2,128)(2,1)} %reshape.197), calls=%async_computation | async-start | bytes 4194304 | tf_op jit(solution)/shard_map/all_to_all | solution.py:93
  88.1 205.9 %all-gather.5.cloned.1.call-start = ((), (), s32[]{:S(2)}) async-start(), calls=%async_computation.3 | async-start | bytes 4718592 | tf_op jit(solution)/shard_map/all_gather | solution.py:102
  124.8 16.9 %copy-start.4 = (bf16[2048,1,512]{2,1,0:T(2,128)(2,1)S(1)}, bf16[2048,1,512]{2,1,0:T(2,128)(2,1)}, u32[]{:S(2)}) copy-start(bf16[2048,1,512]{2,1,0:T(2,128)(2,1)} %reshape.198) | copy-start | bytes 6291460
  207.2 163.0 %all-gather.3.cloned.1.call-start = ((), (), s32[]{:S(2)}) async-start(), calls=%async_computation.2 | async-start | bytes 8912896 | tf_op jit(solution)/shard_map/all_gather | solution.py:103
  396.0 8.8 %copy-start.3 = (bf16[128,256,2,64]{0,1,2,3:T(8,128)(2,1)S(1)}, bf16[128,256,2,64]{0,1,2,3:T(8,128)(2,1)}, u32[]{:S(2)}) copy-start(bf16[128,256,2,64]{0,1,2,3:T(8,128)(2,1)} %copy.53) | copy-start | bytes 25165828
  426.2 10.1 %copy-start.1 = (bf16[1,2048,512]{2,1,0:T(8,128)(2,1)S(1)}, bf16[1,2048,512]{2,1,0:T(8,128)(2,1)}, u32[]{:S(2)}) copy-start(bf16[1,2048,512]{2,1,0:T(8,128)(2,1)} %param.4) | copy-start | bytes 6291460
Sparse Core Ops, SparseCore 0:
  207.3 86.6 all-gather.4
  296.4 73.7 all-gather.2
where the time goes:
time: 444 us; the launch traced here: 443 us
  waiting for transfers between devices  185 us (42%)
  other arithmetic  111 us (25%)
  local copies, waits for them, and re-layouts  88.9 us (20%)
  matrix products  22.9 us (5%)
  starting transfers between devices  21.5 us (5%)
  between operations  13.6 us (3%)
    all_gather x1, waiting for transfers between devices, body(): columns = lax.all_gather(owner_white, 'src', axis=1, tiled=True)  86 us
    all_gather x1, waiting for transfers between devices, body(): lax.all_gather(owner_white, 'rcv', axis=1, tiled=True)  69.3 us
    reduce_sum x1, other arithmetic, whiten(): level = jnp.mean(magnitude, axis=2, keepdims=True) + 1e-06  29.4 us
    all_to_all x1, waiting for transfers between devices, body(): lax.all_to_all(ordered, ('src', 'rcv'), split_axis=1, concat_axis=0, tile...  28.6 us
    dot_general x1, other arithmetic, whiten(): jnp.einsum('wcn,nk->wck', normed, fourier_table(samples, F), preferred_el...  27.4 us
    select_n x1, local copies, waits for them, and re-layouts, body(): ordered = jnp.take(raw, channel_order, axis=1)  18.5 us
    reduce_sum x1, other arithmetic, whiten(): centred = centred - jnp.mean(centred, axis=2, keepdims=True)  16.9 us
    unnamed x18, local copies, waits for them, and re-layouts  14.6 us
  transfers between devices with their start and end apart: 4, of which 3 were waited for; matrix products, arithmetic and copies ran while one was open for 12% of the time, Pallas kernels for 0%

commit v1 on v0

v1 whole, which is shorter than its diff:
```python
import functools
import math

import jax
import jax.numpy as jnp
import ml_dtypes
import numpy as np
from jax import lax
from jax.experimental import pallas as pl
from jax.experimental.pallas import tpu as pltpu
from jax.sharding import PartitionSpec as P

C, WLEN, F, HALF, BAND, SLABS, WIN_SLAB, NW, CB = 2048, 512, 64, 12, 2, 4, 32, 128, 16
AXES = ("src", "rcv")
GRID = (4, 2, 4, 2, 2)
Y, XL, Z, XH, CORE = range(5)
BF16, F32 = jnp.bfloat16, jnp.float32
ROWS = 256
KC = 8


def tables():
    n = np.arange(WLEN)
    inside = np.abs(n[:, None] - n[None, :]) <= HALF
    harmonic = np.arange(1, F + 1)[None, :]
    phase = 2.0 * math.pi / WLEN * (n[:, None] * harmonic % WLEN)
    dft = np.concatenate([np.cos(phase), -np.sin(phase)], axis=1)
    k = np.arange(F)
    near = np.abs(k[:, None] - k[None, :]) <= BAND
    zero = np.zeros((F, F))
    smooth = np.block([[near, zero], [zero, near]])
    total = np.block([[np.ones((F, F)), zero], [zero, np.ones((F, F))]])
    sums = np.concatenate([smooth, total], axis=1)
    sums = np.concatenate([sums, sums], axis=0)
    bf = ml_dtypes.bfloat16
    return (
        inside.astype(bf),
        (1.0 / inside.sum(0, dtype=np.float64))[None, :].astype(np.float32),
        dft.astype(bf),
        sums.astype(bf),
        (1.0 / np.tile(near.sum(0), 2))[None, :].astype(np.float32),
    )


def whiten_kernel(
    order, slab, wid, raw, quality, inside, inv_count, dft, sums, inv_near, out, white, placed
):
    step = pl.program_id(0)
    x = raw[0].astype(F32)
    centred = x - jnp.sum(x, axis=1, keepdims=True) * (1.0 / WLEN)
    magnitude = jnp.abs(centred)
    level = jnp.sum(magnitude, axis=1, keepdims=True) * (1.0 / WLEN) + 1e-6
    window_sum = jnp.dot(magnitude.astype(BF16), inside[...], preferred_element_type=F32)
    normed = (centred / (window_sum * inv_count[...] + 0.25 * level)).astype(BF16)
    spectrum = jnp.dot(normed, dft[...], preferred_element_type=F32)
    squares = spectrum * spectrum
    power = squares + pltpu.roll(squares, F, 1)
    high = power.astype(BF16)
    low = (power - high.astype(F32)).astype(BF16)
    both = jnp.dot(
        jnp.concatenate([high, low], axis=1), sums[...], preferred_element_type=F32
    )
    total = both[:, 2 * F :] * (1.0 / F) + 1e-6
    amplitude = jnp.float32(0.0)
    for age in range(SLABS):
        amplitude += jnp.where(
            slab[age] == wid[0] // WIN_SLAB, jnp.float32(0.5 ** (age / SLABS)), jnp.float32(0.0)
        )
    eye = (
        lax.broadcasted_iota(jnp.int32, (128, 128), 0)
        == lax.broadcasted_iota(jnp.int32, (128, 128), 1)
    )
    weights = []
    for part in range(ROWS // 128):
        row = quality[pl.ds(step * (ROWS // 128) + part, 1), :].astype(F32)
        weights.append(jnp.sum(jnp.where(eye, row, 0.0), axis=1, keepdims=True))
    weight = jnp.concatenate(weights, axis=0) * amplitude
    scale = weight * lax.rsqrt(both[:, : 2 * F] * inv_near[...] + 0.1 * total)
    white[pl.ds(pl.multiple_of(step * ROWS, ROWS), ROWS), :] = spectrum * scale

    @pl.when(step == pl.num_programs(0) - 1)
    def _():
        def place(group, carry):
            base = pl.multiple_of(group * 16, 16)
            for j in range(16):
                placed[pl.ds(base + j, 1), :] = white[pl.ds(order[base + j], 1), :]
            return carry

        lax.fori_loop(0, C // 16, place, 0)
        out[...] = placed[...].astype(BF16)


def whiten(raw, quality, order, slab, wid):
    inside, inv_count, dft, sums, inv_near = tables()
    whole = lambda a: pl.BlockSpec(a.shape, lambda i, *_: (0, 0))
    consts = [inside, inv_count, dft, sums, inv_near]
    return pl.pallas_call(
        whiten_kernel,
        grid_spec=pltpu.PrefetchScalarGridSpec(
            num_scalar_prefetch=3,
            grid=(C // ROWS,),
            in_specs=[
                pl.BlockSpec((1, ROWS, WLEN), lambda i, *_: (0, i, 0)),
                whole(quality),
                *[whole(a) for a in consts],
            ],
            out_specs=pl.BlockSpec((C, 2 * F), lambda i, *_: (0, 0)),
            scratch_shapes=[pltpu.VMEM((C, 2 * F), F32), pltpu.VMEM((C, 2 * F), F32)],
        ),
        out_shape=jax.ShapeDtypeStruct((C, 2 * F), BF16),
        compiler_params=pltpu.CompilerParams(vmem_limit_bytes=32 << 20),
        name="whiten",
    )(order, slab, wid, raw, quality, *[jnp.asarray(a) for a in consts])


def turn_kernel(received, out, wide, turned):
    wide[...] = received[...].astype(F32)
    for p in range(CB):
        t = wide[pl.ds(p, NW, stride=CB), :].T
        turned[pl.ds(p, F, stride=2 * CB), :] = t[:F]
        turned[pl.ds(CB + p, F, stride=2 * CB), :] = t[F:]
    out[...] = turned[...].astype(BF16)


def turn(received):
    return pl.pallas_call(
        turn_kernel,
        in_specs=[pl.BlockSpec(memory_space=pltpu.VMEM)],
        out_specs=pl.BlockSpec(memory_space=pltpu.VMEM),
        out_shape=jax.ShapeDtypeStruct((F * 2 * CB, NW), BF16),
        scratch_shapes=[pltpu.VMEM((NW * CB, 2 * F), F32), pltpu.VMEM((F * 2 * CB, NW), F32)],
        compiler_params=pltpu.CompilerParams(vmem_limit_bytes=16 << 20),
        name="turn",
    )(received)


def shift(x, axis, amount):
    ids = np.arange(int(np.prod(GRID))).reshape(GRID)
    to = np.roll(ids, -amount, axis=axis)
    return lax.ppermute(x, AXES, [(int(a), int(b)) for a, b in zip(ids.ravel(), to.ravel())])


def gather_ring(x, ring, pair):
    half = x.shape[0] // 2
    other = shift(x, pair, 1)
    found = []
    for flip, block in ((0, x), (1, other)):
        after = shift(block, ring, 1)
        before = shift(block, ring, -1)
        low = shift(after[:half], ring, 1)
        high = shift(before[half:], ring, -1)
        found += [(0, flip, block), (1, flip, after), (3, flip, before), (2, flip, low, high)]
    return found


def product_kernel(meta, *refs, row_parts, col_parts):
    step = pl.program_id(0)
    n_in = sum(row_parts) + sum(col_parts)
    inputs, (out, a, b) = list(refs[:n_in]), refs[n_in:]
    half_steps = pl.num_programs(0) // 2

    def put_row(block, offset):
        a[:, pl.ds(offset, CB), 0:NW] = block[:, 0:CB, :]
        a[:, pl.ds(offset, CB), NW : 2 * NW] = block[:, CB : 2 * CB, :]

    def put_col(block, offset):
        re, im = block[:, 0:CB, :], block[:, CB : 2 * CB, :]
        b[:, pl.ds(offset, CB), 0:NW] = re
        b[:, pl.ds(offset, CB), NW : 2 * NW] = im
        b[:, pl.ds(128 + offset, CB), 0:NW] = -im
        b[:, pl.ds(128 + offset, CB), NW : 2 * NW] = re

    position = 0
    for put, parts in ((put_row, row_parts), (put_col, col_parts)):
        for count in parts:
            offset = pl.multiple_of(meta[position] * CB, CB)
            position += 1
            if count == 1:
                put(inputs.pop(0), offset)
            else:
                low, high = inputs.pop(0), inputs.pop(0)
                pl.when(step < half_steps)(functools.partial(put, low, offset))
                pl.when(step >= half_steps)(functools.partial(put, high, offset))
    factor = 1.0 / math.sqrt(NW)
    for k in range(KC):
        o = lax.dot_general(
            a[k], b[k], (((1,), (1,)), ((), ())), preferred_element_type=F32
        )
        out[0, k] = o[:, :128] * factor
        out[1, k] = o[:, 128:] * factor


def product(meta, rows, cols):
    steps = F // KC
    arrays, specs = [], []
    for group in rows + cols:
        for index, array in enumerate(group):
            array = array.reshape(-1, 2 * CB, NW)
            if len(group) == 1:
                index_map = lambda i, m: (i, 0, 0)
            elif index == 0:
                index_map = lambda i, m: (jnp.minimum(i, steps // 2 - 1), 0, 0)
            else:
                index_map = lambda i, m: (jnp.maximum(i - steps // 2, 0), 0, 0)
            arrays.append(array)
            specs.append(pl.BlockSpec((KC, 2 * CB, NW), index_map))
    return pl.pallas_call(
        functools.partial(
            product_kernel,
            row_parts=[len(g) for g in rows],
            col_parts=[len(g) for g in cols],
        ),
        grid_spec=pltpu.PrefetchScalarGridSpec(
            num_scalar_prefetch=1,
            grid=(steps,),
            in_specs=specs,
            out_specs=pl.BlockSpec((2, KC, 256, 128), lambda i, m: (0, i, 0, 0)),
            scratch_shapes=[pltpu.VMEM((KC, 256, 256), BF16), pltpu.VMEM((KC, 256, 256), BF16)],
        ),
        out_shape=jax.ShapeDtypeStruct((2, F, 256, 128), F32),
        compiler_params=pltpu.CompilerParams(vmem_limit_bytes=40 << 20),
        name="product",
    )(meta, *arrays)


def body(raw, quality, channel_order, slab_order):
    src, rcv = lax.axis_index("src"), lax.axis_index("rcv")
    wid = (src * 16 + rcv).astype(jnp.int32).reshape(1)
    spectra = whiten(raw, quality.reshape(16, 128), channel_order, slab_order, wid)
    received = lax.all_to_all(
        spectra.reshape(NW, CB, 2 * F), AXES, split_axis=0, concat_axis=0, tiled=True
    )
    mine = turn(received.reshape(NW * CB, 2 * F))

    y, xl = src // 2, src % 2
    z, xh, core = rcv // 4, rcv // 2 % 2, rcv % 2
    rows, cols, meta = [], [], []
    for ring, flip, *blocks in gather_ring(mine, Z, XH):
        at = (z - ring) % 4 * 4 + (xh + flip) % 2 * 2
        rows.append(blocks)
        meta.append(at + core)
        rows.append([shift(block, CORE, 1) for block in blocks])
        meta.append(at + 1 - core)
    for ring, flip, *blocks in gather_ring(mine, Y, XL):
        cols.append(blocks)
        meta.append((y - ring) % 4 * 2 + (xl + flip) % 2)
    return product(jnp.stack(meta).astype(jnp.int32), rows, cols)


def solution(mesh):
    in_specs = (P(("src", "rcv"), None, None), P(("src", "rcv"), None), P(), P())
    out_specs = P(None, None, "src", "rcv")
    return jax.shard_map(body, mesh=mesh, in_specs=in_specs, out_specs=out_specs, check_vma=False)
```

time: 444 us -> 142 us (0.32)
  waiting for transfers between devices: 185 us -> 28.3 us
  other arithmetic: 111 us -> 0 us
  local copies, waits for them, and re-layouts: 88.9 us -> 29 us
  blocking collectives: 0 us -> 24.9 us
  matrix products: 22.9 us -> 0 us
  Pallas kernels: 0 us -> 22.7 us
  starting transfers between devices: 21.5 us -> 35.9 us
  between operations: 13.6 us -> 0.19 us
    all_gather x2 -> x0, waiting for transfers between devices: 155 us -> none  [the longest x1 86 us: body(): columns = lax.all_gather(owner_white, 'src', axis=1, tiled=True)]
    reduce_sum x6 -> x0, other arithmetic: 46.7 us -> none  [the longest x1 29.4 us: whiten(): level = jnp.mean(magnitude, axis=2, keepdims=True) + 1e-06]
    ppermute x0 -> x28, starting transfers between devices: none -> 35.9 us  [shift(): lax.ppermute(x, AXES, [(int(a), int(b)) for a, b in zip(ids.ravel(), to.r...]
    all_to_all x2 -> x0, waiting for transfers between devices: 28.6 us -> none  [the longest x1 28.6 us: body(): lax.all_to_all(ordered, ('src', 'rcv'), split_axis=1, concat_axis=0, tile...]
    ppermute x0 -> x28, waiting for transfers between devices: none -> 28.3 us  [shift(): lax.ppermute(x, AXES, [(int(a), int(b)) for a, b in zip(ids.ravel(), to.r...]
    dot_general x1 -> x0, other arithmetic: 27.4 us -> none  [whiten(): jnp.einsum('wcn,nk->wck', normed, fourier_table(samples, F), preferred_el...]
    all_to_all x0 -> x1, blocking collectives: none -> 24.9 us  [body(): lax.all_to_all(spectra.reshape(NW, CB, 2 * F), AXES, split_axis=0, concat...]
    dot_general x4 -> x0, matrix products: 22.9 us -> none  [the longest x1 13.4 us: cross_block(): jnp.einsum('wapf,wbpf->fab', swapped, cols_four, preferred_element_type=j...]
  transfers between devices with their start and end apart: 4 -> 28, of which waited for: 3 -> 9; matrix products, arithmetic and copies ran while one was open for 12% -> 2% of each run, Pallas kernels for 0% -> 0%
where the time goes in v1:
time: 142 us; the launch traced here: 141 us
  starting transfers between devices  35.9 us (25%)
  local copies, waits for them, and re-layouts  29 us (20%)
  waiting for transfers between devices  28.3 us (20%)
  blocking collectives  24.9 us (18%)
  Pallas kernels  22.7 us (16%)
    ppermute x28, starting transfers between devices, shift(): lax.ppermute(x, AXES, [(int(a), int(b)) for a, b in zip(ids.ravel(), to.r...  35.9 us
    ppermute x28, waiting for transfers between devices, shift(): lax.ppermute(x, AXES, [(int(a), int(b)) for a, b in zip(ids.ravel(), to.r...  28.3 us
    unnamed x70, local copies, waits for them, and re-layouts  26.1 us
    all_to_all x1, blocking collectives, body(): lax.all_to_all(spectra.reshape(NW, CB, 2 * F), AXES, split_axis=0, concat...  24.9 us
    pallas_call x1, Pallas kernels, product(): pl.pallas_call(functools.partial(product_kernel, row_parts=[len(g) for g...  12.2 us
    pallas_call x1, Pallas kernels, whiten(): pl.pallas_call(whiten_kernel, grid_spec=pltpu.PrefetchScalarGridSpec(num_...  9.48 us
  transfers between devices with their start and end apart: 28, of which 9 were waited for; matrix products, arithmetic and copies ran while one was open for 2% of the time, Pallas kernels for 0%

profile of v1, /device:TPU:1, one launch (start us, length us, event | category | flops | bytes accessed | tf_op | source)
XLA Modules:
  0.0 141.0 jit_solution(8205947472748718540)
XLA Ops:
  0.0 1.6 %copy-done = bf16[1,2048,512]{2,1,0:T(8,128)(2,1)S(1)} copy-done((bf16[1,2048,512]{2,1,0:T(8,128)(2,1)S(1)}, bf16[1,2048,512]{2,1,0:T(8,128)(2,1)}, u32[]{:S(2)}) %copy-start) | copy-done | bytes 2097176
  1.6 1.0 copy-done.15
  7.8 9.5 %whiten.1 = bf16[2048,128]{1,0:T(8,128)(2,1)S(1)} custom-call(s32[2048]{0:T(1024)S(1)} %copy-done.30, s32[4]{0:T(128)S(1)} %copy-done.33, s32[1]{0:T(128)} %bitcast.24.wid, bf16[1,2048,512]{2,1,0:T(8,128)(2,1)S(1)} %copy-done, s32[16,128]{1,0:T(8,128)S(1)} %bitcast.80, bf16[512,512]{1,0:T(8,128)(2,1)S(1)} %copy-done.15, f32[1,512]{1,0:T(1,128)S(1)} %copy-done.32, ...), custom_call_target="tpu_custom_call" | custom-call | tf_op jit(solution)/shard_map/whiten/pallas_call | solution.py:97
  17.3 24.9 %all_to_all.5 = bf16[128,16,128]{2,1,0:T(8,128)(2,1)S(1)} all-to-all(bf16[128,16,128]{2,1,0:T(8,128)(2,1)S(1)} %bitcast.60), channel_id=1, replica_groups=mesh['src'=8,'rcv'=16] {'src','rcv'}, dimensions={0} | all-to-all | bytes 1048576 | tf_op jit(solution)/shard_map/all_to_all | solution.py:230
  45.8 2.0 %collective-permute-start.9 = (bf16[2048,128]{1,0:T(8,128)(2,1)S(1)}, bf16[2048,128]{1,0:T(8,128)(2,1)S(1)}, u32[]{:S(2)}, u32[]{:S(2)}) collective-permute-start(bf16[2048,128]{1,0:T(8,128)(2,1)S(1)} %turn.1), channel_id=1, source_target_pairs={{0,2},{1,3},{2,0},{3,1},{4,6},{5,7},{6,4},{7,5},{8,10},{9,11},{10,... | collective-permute-start | bytes 1572872 | tf_op jit(solution)/shard_map/ppermute | solution.py:140
  47.8 7.9 %collective-permute-done.20 = bf16[2048,128]{1,0:T(8,128)(2,1)S(1)} collective-permute-done((bf16[2048,128]{1,0:T(8,128)(2,1)S(1)}, bf16[2048,128]{1,0:T(8,128)(2,1)S(1)}, u32[]{:S(2)}, u32[]{:S(2)}) %collective-permute-start.20) | collective-permute-done | bytes 524320 | tf_op jit(solution)/shard_map/ppermute | solution.py:140
  55.7 1.2 collective-permute-done.19
  56.9 2.5 %collective-permute-start = (bf16[2048,128]{1,0:T(8,128)(2,1)S(1)}, bf16[2048,128]{1,0:T(8,128)(2,1)S(1)}, u32[]{:S(2)}, u32[]{:S(2)}) collective-permute-start(bf16[2048,128]{1,0:T(8,128)(2,1)S(1)} %turn.1), channel_id=1, source_target_pairs={{0,1},{1,0},{2,3},{3,2},{4,5},{5,4},{6,7},{7,6},{8,9},{9,8},{10,11... | collective-permute-start | bytes 1572872 | tf_op jit(solution)/shard_map/ppermute | solution.py:140
  61.1 8.4 %collective-permute-done.9 = bf16[2048,128]{1,0:T(8,128)(2,1)S(1)} collective-permute-done((bf16[2048,128]{1,0:T(8,128)(2,1)S(1)}, bf16[2048,128]{1,0:T(8,128)(2,1)S(1)}, u32[]{:S(2)}, u32[]{:S(2)}) %collective-permute-start.9) | collective-permute-done | bytes 524320 | tf_op jit(solution)/shard_map/ppermute | solution.py:140
  69.5 2.3 %collective-permute-start.25 = (bf16[2048,128]{1,0:T(8,128)(2,1)S(1)}, bf16[2048,128]{1,0:T(8,128)(2,1)S(1)}, u32[]{:S(2)}, u32[]{:S(2)}) collective-permute-start(bf16[2048,128]{1,0:T(8,128)(2,1)S(1)} %collective-permute-done.23), channel_id=1, source_target_pairs={{0,96},{1,97},{2,98},{3,99},{4,100},{5,101},{6,102},{7,103},{8,104... | collective-permute-start | bytes 1572872 | tf_op jit(solution)/shard_map/ppermute | solution.py:140
  72.8 1.4 collective-permute-start.5
  74.8 1.4 collective-permute-start.13
  76.2 1.1 collective-permute-done.6
  77.3 2.0 %collective-permute-done.5 = bf16[1024,128]{1,0:T(8,128)(2,1)S(1)} collective-permute-done((bf16[1024,128]{1,0:T(8,128)(2,1)S(1)}, bf16[1024,128]{1,0:T(8,128)(2,1)S(1)}, u32[]{:S(2)}, u32[]{:S(2)}) %collective-permute-start.5) | collective-permute-done | bytes 262176 | tf_op jit(solution)/shard_map/ppermute | solution.py:140
  79.3 5.4 %collective-permute-start.10 = (bf16[2048,128]{1,0:T(8,128)(2,1)S(1)}, bf16[2048,128]{1,0:T(8,128)(2,1)S(1)}, u32[]{:S(2)}, u32[]{:S(2)}) collective-permute-start(bf16[2048,128]{1,0:T(8,128)(2,1)S(1)} %collective-permute-done.9), channel_id=1, source_target_pairs={{0,1},{1,0},{2,3},{3,2},{4,5},{5,4},{6,7},{7,6},{8,9},{9,8},{10,11... | collective-permute-start | bytes 1572872 | tf_op jit(solution)/shard_map/ppermute | solution.py:140
  84.7 3.5 %collective-permute-start.2 = (bf16[2048,128]{1,0:T(8,128)(2,1)S(1)}, bf16[2048,128]{1,0:T(8,128)(2,1)S(1)}, u32[]{:S(2)}, u32[]{:S(2)}) collective-permute-start(bf16[2048,128]{1,0:T(8,128)(2,1)S(1)} %collective-permute-done.1), channel_id=1, source_target_pairs={{0,1},{1,0},{2,3},{3,2},{4,5},{5,4},{6,7},{7,6},{8,9},{9,8},{10,11... | collective-permute-start | bytes 1572872 | tf_op jit(solution)/shard_map/ppermute | solution.py:140
  88.9 3.0 %collective-permute-start.8 = (bf16[1024,128]{1,0:T(8,128)(2,1)S(1)}, bf16[1024,128]{1,0:T(8,128)(2,1)S(1)}, u32[]{:S(2)}, u32[]{:S(2)}) collective-permute-start(bf16[1024,128]{1,0:T(8,128)(2,1)S(1)} %collective-permute-done.6), channel_id=1, source_target_pairs={{0,1},{1,0},{2,3},{3,2},{4,5},{5,4},{6,7},{7,6},{8,9},{9,8},{10,11... | collective-permute-start | bytes 786440 | tf_op jit(solution)/shard_map/ppermute | solution.py:140
  91.9 2.6 %collective-permute-start.7 = (bf16[1024,128]{1,0:T(8,128)(2,1)S(1)}, bf16[1024,128]{1,0:T(8,128)(2,1)S(1)}, u32[]{:S(2)}, u32[]{:S(2)}) collective-permute-start(bf16[1024,128]{1,0:T(8,128)(2,1)S(1)} %collective-permute-done.5), channel_id=1, source_target_pairs={{0,1},{1,0},{2,3},{3,2},{4,5},{5,4},{6,7},{7,6},{8,9},{9,8},{10,11... | collective-permute-start | bytes 786440 | tf_op jit(solution)/shard_map/ppermute | solution.py:140
  96.5 3.0 %collective-permute-start.27 = (bf16[1024,128]{1,0:T(8,128)(2,1)S(1)}, bf16[1024,128]{1,0:T(8,128)(2,1)S(1)}, u32[]{:S(2)}, u32[]{:S(2)}) collective-permute-start(bf16[1024,128]{1,0:T(8,128)(2,1)S(1)} %slice.39), channel_id=1, source_target_pairs={{0,96},{1,97},{2,98},{3,99},{4,100},{5,101},{6,102},{7,103},{8,104... | collective-permute-start | bytes 786440 | tf_op jit(solution)/shard_map/ppermute | solution.py:140
  100.9 1.5 %collective-permute-start.15 = (bf16[1024,128]{1,0:T(8,128)(2,1)S(1)}, bf16[1024,128]{1,0:T(8,128)(2,1)}, u32[]{:S(2)}, u32[]{:S(2)}) collective-permute-start(bf16[1024,128]{1,0:T(8,128)(2,1)S(1)} %slice.34), channel_id=1, source_target_pairs={{0,4},{1,5},{2,6},{3,7},{4,8},{5,9},{6,10},{7,11},{8,12},{9,13},{1... | collective-permute-start | bytes 786440 | tf_op jit(solution)/shard_map/ppermute | solution.py:140
  106.3 1.6 %collective-permute-done.16 = bf16[1024,128]{1,0:T(8,128)(2,1)} collective-permute-done((bf16[1024,128]{1,0:T(8,128)(2,1)S(1)}, bf16[1024,128]{1,0:T(8,128)(2,1)}, u32[]{:S(2)}, u32[]{:S(2)}) %collective-permute-start.16) | collective-permute-done | bytes 262176 | tf_op jit(solution)/shard_map/ppermute | solution.py:140
  107.8 1.1 collective-permute-start.18
  109.9 1.1 collective-permute-start.17
  111.1 4.6 %collective-permute-done.26 = bf16[1024,128]{1,0:T(8,128)(2,1)} collective-permute-done((bf16[1024,128]{1,0:T(8,128)(2,1)}, bf16[1024,128]{1,0:T(8,128)(2,1)}, u32[]{:S(2)}, u32[]{:S(2)}) %collective-permute-start.26) | collective-permute-done | bytes 262176 | tf_op jit(solution)/shard_map/ppermute | solution.py:140
  115.8 1.0 copy-done.2
  116.8 1.0 copy-done.4
  117.8 1.0 copy-done.6
  118.9 1.0 copy-done.8
  119.9 1.0 copy-done.10
  121.0 1.0 copy-done.12
  122.0 1.0 copy-done.14
  128.7 12.2 %product.1 = f32[2,64,256,128]{3,2,1,0:T(8,128)} custom-call(s32[24]{0:T(128)S(1)} %stack.99.meta, bf16[64,32,128]{2,1,0:T(8,128)(2,1)S(1)} %bitcast.57, bf16[64,32,128]{2,1,0:T(8,128)(2,1)S(1)} %bitcast.69, bf16[64,32,128]{2,1,0:T(8,128)(2,1)S(1)} %bitcast.64, bf16[64,32,128]{2,1,0:T(8,128)(2,1)S(1)} %bitcast.72, bf16[64,32,128]{2,1,0:T(8,128)(2,1)S(1)} %bitcast.63, ...), custom_call_target="tpu_custom_call" | custom-call | tf_op jit(solution)/shard_map/product/pallas_call | solution.py:207
  (107 shorter events, 26.9 us)
Async XLA Ops:
  43.3 12.5 %collective-permute-start.20 = (bf16[2048,128]{1,0:T(8,128)(2,1)S(1)}, bf16[2048,128]{1,0:T(8,128)(2,1)S(1)}, u32[]{:S(2)}, u32[]{:S(2)}) collective-permute-start(bf16[2048,128]{1,0:T(8,128)(2,1)S(1)} %turn.1), channel_id=1, source_target_pairs={{0,96},{1,97},{2,98},{3,99},{4,100},{5,101},{6,102},{7,103},{8,104... | collective-permute-start | bytes 1572872 | tf_op jit(solution)/shard_map/ppermute | solution.py:140
  43.9 13.1 %collective-permute-start.19 = (bf16[2048,128]{1,0:T(8,128)(2,1)S(1)}, bf16[2048,128]{1,0:T(8,128)(2,1)S(1)}, u32[]{:S(2)}, u32[]{:S(2)}) collective-permute-start(bf16[2048,128]{1,0:T(8,128)(2,1)S(1)} %turn.1), channel_id=1, source_target_pairs={{0,32},{1,33},{2,34},{3,35},{4,36},{5,37},{6,38},{7,39},{8,40},{9,... | collective-permute-start | bytes 1572872 | tf_op jit(solution)/shard_map/ppermute | solution.py:140
  44.8 14.7 %collective-permute-start.3 = (bf16[2048,128]{1,0:T(8,128)(2,1)S(1)}, bf16[2048,128]{1,0:T(8,128)(2,1)S(1)}, u32[]{:S(2)}, u32[]{:S(2)}) collective-permute-start(bf16[2048,128]{1,0:T(8,128)(2,1)S(1)} %turn.1), channel_id=1, source_target_pairs={{0,12},{1,13},{2,14},{3,15},{4,0},{5,1},{6,2},{7,3},{8,4},{9,5},{1... | collective-permute-start | bytes 1572872 | tf_op jit(solution)/shard_map/ppermute | solution.py:140
  45.5 14.7 %collective-permute-start.23 = (bf16[2048,128]{1,0:T(8,128)(2,1)S(1)}, bf16[2048,128]{1,0:T(8,128)(2,1)S(1)}, u32[]{:S(2)}, u32[]{:S(2)}) collective-permute-start(bf16[2048,128]{1,0:T(8,128)(2,1)S(1)} %turn.1), channel_id=1, source_target_pairs={{0,16},{1,17},{2,18},{3,19},{4,20},{5,21},{6,22},{7,23},{8,24},{9,... | collective-permute-start | bytes 1572872 | tf_op jit(solution)/shard_map/ppermute | solution.py:140
  45.8 23.7 %collective-permute-start.9 = (bf16[2048,128]{1,0:T(8,128)(2,1)S(1)}, bf16[2048,128]{1,0:T(8,128)(2,1)S(1)}, u32[]{:S(2)}, u32[]{:S(2)}) collective-permute-start(bf16[2048,128]{1,0:T(8,128)(2,1)S(1)} %turn.1), channel_id=1, source_target_pairs={{0,2},{1,3},{2,0},{3,1},{4,6},{5,7},{6,4},{7,5},{8,10},{9,11},{10,... | collective-permute-start | bytes 1572872 | tf_op jit(solution)/shard_map/ppermute | solution.py:140
  55.7 16.0 %collective-permute-start.1 = (bf16[2048,128]{1,0:T(8,128)(2,1)S(1)}, bf16[2048,128]{1,0:T(8,128)(2,1)S(1)}, u32[]{:S(2)}, u32[]{:S(2)}) collective-permute-start(bf16[2048,128]{1,0:T(8,128)(2,1)S(1)} %turn.1), channel_id=1, source_target_pairs={{0,4},{1,5},{2,6},{3,7},{4,8},{5,9},{6,10},{7,11},{8,12},{9,13},{1... | collective-permute-start | bytes 1572872 | tf_op jit(solution)/shard_map/ppermute | solution.py:140
  56.9 15.0 %collective-permute-start = (bf16[2048,128]{1,0:T(8,128)(2,1)S(1)}, bf16[2048,128]{1,0:T(8,128)(2,1)S(1)}, u32[]{:S(2)}, u32[]{:S(2)}) collective-permute-start(bf16[2048,128]{1,0:T(8,128)(2,1)S(1)} %turn.1), channel_id=1, source_target_pairs={{0,1},{1,0},{2,3},{3,2},{4,5},{5,4},{6,7},{7,6},{8,9},{9,8},{10,11... | collective-permute-start | bytes 1572872 | tf_op jit(solution)/shard_map/ppermute | solution.py:140
  59.5 13.3 %collective-permute-start.22 = (bf16[1024,128]{1,0:T(8,128)(2,1)S(1)}, bf16[1024,128]{1,0:T(8,128)(2,1)S(1)}, u32[]{:S(2)}, u32[]{:S(2)}) collective-permute-start(bf16[1024,128]{1,0:T(8,128)(2,1)S(1)} %slice.37), channel_id=1, source_target_pairs={{0,96},{1,97},{2,98},{3,99},{4,100},{5,101},{6,102},{7,103},{8,104... | collective-permute-start | bytes 786440 | tf_op jit(solution)/shard_map/ppermute | solution.py:140
  60.2 45.3 %copy-start.3 = (bf16[2048,128]{1,0:T(8,128)(2,1)}, bf16[2048,128]{1,0:T(8,128)(2,1)S(1)}, u32[]{:S(2)}) copy-start(bf16[2048,128]{1,0:T(8,128)(2,1)S(1)} %collective-permute-done.23) | copy-start | bytes 1572868
  60.2 13.9 %collective-permute-start.21 = (bf16[1024,128]{1,0:T(8,128)(2,1)S(1)}, bf16[1024,128]{1,0:T(8,128)(2,1)S(1)}, u32[]{:S(2)}, u32[]{:S(2)}) collective-permute-start(bf16[1024,128]{1,0:T(8,128)(2,1)S(1)} %slice.36), channel_id=1, source_target_pairs={{0,32},{1,33},{2,34},{3,35},{4,36},{5,37},{6,38},{7,39},{8,40},{9,... | collective-permute-start | bytes 786440 | tf_op jit(solution)/shard_map/ppermute | solution.py:140
  69.5 36.1 %copy-start.5 = (bf16[2048,128]{1,0:T(8,128)(2,1)}, bf16[2048,128]{1,0:T(8,128)(2,1)S(1)}, u32[]{:S(2)}) copy-start(bf16[2048,128]{1,0:T(8,128)(2,1)S(1)} %collective-permute-done.9) | copy-start | bytes 1572868
  69.5 15.2 %collective-permute-start.25 = (bf16[2048,128]{1,0:T(8,128)(2,1)S(1)}, bf16[2048,128]{1,0:T(8,128)(2,1)S(1)}, u32[]{:S(2)}, u32[]{:S(2)}) collective-permute-start(bf16[2048,128]{1,0:T(8,128)(2,1)S(1)} %collective-permute-done.23), channel_id=1, source_target_pairs={{0,96},{1,97},{2,98},{3,99},{4,100},{5,101},{6,102},{7,103},{8,104... | collective-permute-start | bytes 1572872 | tf_op jit(solution)/shard_map/ppermute | solution.py:140
  71.7 5.5 %collective-permute-start.6 = (bf16[1024,128]{1,0:T(8,128)(2,1)S(1)}, bf16[1024,128]{1,0:T(8,128)(2,1)S(1)}, u32[]{:S(2)}, u32[]{:S(2)}) collective-permute-start(bf16[1024,128]{1,0:T(8,128)(2,1)S(1)} %slice.33), channel_id=1, source_target_pairs={{0,12},{1,13},{2,14},{3,15},{4,0},{5,1},{6,2},{7,3},{8,4},{9,5},{1... | collective-permute-start | bytes 786440 | tf_op jit(solution)/shard_map/ppermute | solution.py:140
  72.7 12.0 %collective-permute-start.24 = (bf16[2048,128]{1,0:T(8,128)(2,1)S(1)}, bf16[2048,128]{1,0:T(8,128)(2,1)S(1)}, u32[]{:S(2)}, u32[]{:S(2)}) collective-permute-start(bf16[2048,128]{1,0:T(8,128)(2,1)S(1)} %collective-permute-done.23), channel_id=1, source_target_pairs={{0,32},{1,33},{2,34},{3,35},{4,36},{5,37},{6,38},{7,39},{8,40},{9,... | collective-permute-start | bytes 1572872 | tf_op jit(solution)/shard_map/ppermute | solution.py:140
  72.8 6.5 %collective-permute-start.5 = (bf16[1024,128]{1,0:T(8,128)(2,1)S(1)}, bf16[1024,128]{1,0:T(8,128)(2,1)S(1)}, u32[]{:S(2)}, u32[]{:S(2)}) collective-permute-start(bf16[1024,128]{1,0:T(8,128)(2,1)S(1)} %slice.32), channel_id=1, source_target_pairs={{0,4},{1,5},{2,6},{3,7},{4,8},{5,9},{6,10},{7,11},{8,12},{9,13},{1... | collective-permute-start | bytes 786440 | tf_op jit(solution)/shard_map/ppermute | solution.py:140
  74.8 14.0 %collective-permute-start.13 = (bf16[2048,128]{1,0:T(8,128)(2,1)S(1)}, bf16[2048,128]{1,0:T(8,128)(2,1)}, u32[]{:S(2)}, u32[]{:S(2)}) collective-permute-start(bf16[2048,128]{1,0:T(8,128)(2,1)S(1)} %collective-permute-done.9), channel_id=1, source_target_pairs={{0,12},{1,13},{2,14},{3,15},{4,0},{5,1},{6,2},{7,3},{8,4},{9,5},{1... | collective-permute-start | bytes 1572872 | tf_op jit(solution)/shard_map/ppermute | solution.py:140
  77.3 30.6 %copy-start.18 = (bf16[1024,128]{1,0:T(8,128)(2,1)}, bf16[1024,128]{1,0:T(8,128)(2,1)S(1)}, u32[]{:S(2)}) copy-start(bf16[1024,128]{1,0:T(8,128)(2,1)S(1)} %collective-permute-done.6) | copy-start | bytes 786436
  77.3 14.6 %collective-permute-start.11 = (bf16[2048,128]{1,0:T(8,128)(2,1)S(1)}, bf16[2048,128]{1,0:T(8,128)(2,1)}, u32[]{:S(2)}, u32[]{:S(2)}) collective-permute-start(bf16[2048,128]{1,0:T(8,128)(2,1)S(1)} %collective-permute-done.9), channel_id=1, source_target_pairs={{0,4},{1,5},{2,6},{3,7},{4,8},{5,9},{6,10},{7,11},{8,12},{9,13},{1... | collective-permute-start | bytes 1572872 | tf_op jit(solution)/shard_map/ppermute | solution.py:140
  79.3 29.7 %copy-start.20 = (bf16[1024,128]{1,0:T(8,128)(2,1)}, bf16[1024,128]{1,0:T(8,128)(2,1)S(1)}, u32[]{:S(2)}) copy-start(bf16[1024,128]{1,0:T(8,128)(2,1)S(1)} %collective-permute-done.5) | copy-start | bytes 786436
  79.3 17.2 %collective-permute-start.10 = (bf16[2048,128]{1,0:T(8,128)(2,1)S(1)}, bf16[2048,128]{1,0:T(8,128)(2,1)S(1)}, u32[]{:S(2)}, u32[]{:S(2)}) collective-permute-start(bf16[2048,128]{1,0:T(8,128)(2,1)S(1)} %collective-permute-done.9), channel_id=1, source_target_pairs={{0,1},{1,0},{2,3},{3,2},{4,5},{5,4},{6,7},{7,6},{8,9},{9,8},{10,11... | collective-permute-start | bytes 1572872 | tf_op jit(solution)/shard_map/ppermute | solution.py:140
  84.6 15.5 %collective-permute-start.4 = (bf16[2048,128]{1,0:T(8,128)(2,1)S(1)}, bf16[2048,128]{1,0:T(8,128)(2,1)S(1)}, u32[]{:S(2)}, u32[]{:S(2)}) collective-permute-start(bf16[2048,128]{1,0:T(8,128)(2,1)S(1)} %collective-permute-done.3), channel_id=1, source_target_pairs={{0,1},{1,0},{2,3},{3,2},{4,5},{5,4},{6,7},{7,6},{8,9},{9,8},{10,11... | collective-permute-start | bytes 1572872 | tf_op jit(solution)/shard_map/ppermute | solution.py:140
  84.7 19.2 %collective-permute-start.2 = (bf16[2048,128]{1,0:T(8,128)(2,1)S(1)}, bf16[2048,128]{1,0:T(8,128)(2,1)S(1)}, u32[]{:S(2)}, u32[]{:S(2)}) collective-permute-start(bf16[2048,128]{1,0:T(8,128)(2,1)S(1)} %collective-permute-done.1), channel_id=1, source_target_pairs={{0,1},{1,0},{2,3},{3,2},{4,5},{5,4},{6,7},{7,6},{8,9},{9,8},{10,11... | collective-permute-start | bytes 1572872 | tf_op jit(solution)/shard_map/ppermute | solution.py:140
  88.9 10.5 %collective-permute-start.8 = (bf16[1024,128]{1,0:T(8,128)(2,1)S(1)}, bf16[1024,128]{1,0:T(8,128)(2,1)S(1)}, u32[]{:S(2)}, u32[]{:S(2)}) collective-permute-start(bf16[1024,128]{1,0:T(8,128)(2,1)S(1)} %collective-permute-done.6), channel_id=1, source_target_pairs={{0,1},{1,0},{2,3},{3,2},{4,5},{5,4},{6,7},{7,6},{8,9},{9,8},{10,11... | collective-permute-start | bytes 786440 | tf_op jit(solution)/shard_map/ppermute | solution.py:140
  91.9 10.5 %collective-permute-start.7 = (bf16[1024,128]{1,0:T(8,128)(2,1)S(1)}, bf16[1024,128]{1,0:T(8,128)(2,1)S(1)}, u32[]{:S(2)}, u32[]{:S(2)}) collective-permute-start(bf16[1024,128]{1,0:T(8,128)(2,1)S(1)} %collective-permute-done.5), channel_id=1, source_target_pairs={{0,1},{1,0},{2,3},{3,2},{4,5},{5,4},{6,7},{7,6},{8,9},{9,8},{10,11... | collective-permute-start | bytes 786440 | tf_op jit(solution)/shard_map/ppermute | solution.py:140
  96.5 9.1 %collective-permute-start.27 = (bf16[1024,128]{1,0:T(8,128)(2,1)S(1)}, bf16[1024,128]{1,0:T(8,128)(2,1)S(1)}, u32[]{:S(2)}, u32[]{:S(2)}) collective-permute-start(bf16[1024,128]{1,0:T(8,128)(2,1)S(1)} %slice.39), channel_id=1, source_target_pairs={{0,96},{1,97},{2,98},{3,99},{4,100},{5,101},{6,102},{7,103},{8,104... | collective-permute-start | bytes 786440 | tf_op jit(solution)/shard_map/ppermute | solution.py:140
  100.1 7.7 %collective-permute-start.16 = (bf16[1024,128]{1,0:T(8,128)(2,1)S(1)}, bf16[1024,128]{1,0:T(8,128)(2,1)}, u32[]{:S(2)}, u32[]{:S(2)}) collective-permute-start(bf16[1024,128]{1,0:T(8,128)(2,1)S(1)} %slice.35), channel_id=1, source_target_pairs={{0,12},{1,13},{2,14},{3,15},{4,0},{5,1},{6,2},{7,3},{8,4},{9,5},{1... | collective-permute-start | bytes 786440 | tf_op jit(solution)/shard_map/ppermute | solution.py:140
  100.9 8.9 %collective-permute-start.15 = (bf16[1024,128]{1,0:T(8,128)(2,1)S(1)}, bf16[1024,128]{1,0:T(8,128)(2,1)}, u32[]{:S(2)}, u32[]{:S(2)}) collective-permute-start(bf16[1024,128]{1,0:T(8,128)(2,1)S(1)} %slice.34), channel_id=1, source_target_pairs={{0,4},{1,5},{2,6},{3,7},{4,8},{5,9},{6,10},{7,11},{8,12},{9,13},{1... | collective-permute-start | bytes 786440 | tf_op jit(solution)/shard_map/ppermute | solution.py:140
  103.1 12.6 %collective-permute-start.14 = (bf16[2048,128]{1,0:T(8,128)(2,1)}, bf16[2048,128]{1,0:T(8,128)(2,1)}, u32[]{:S(2)}, u32[]{:S(2)}) collective-permute-start(bf16[2048,128]{1,0:T(8,128)(2,1)} %collective-permute-done.13), channel_id=1, source_target_pairs={{0,1},{1,0},{2,3},{3,2},{4,5},{5,4},{6,7},{7,6},{8,9},{9,8},{10,11... | collective-permute-start | bytes 1572872 | tf_op jit(solution)/shard_map/ppermute | solution.py:140
  104.8 11.0 %collective-permute-start.12 = (bf16[2048,128]{1,0:T(8,128)(2,1)}, bf16[2048,128]{1,0:T(8,128)(2,1)}, u32[]{:S(2)}, u32[]{:S(2)}) collective-permute-start(bf16[2048,128]{1,0:T(8,128)(2,1)} %collective-permute-done.11), channel_id=1, source_target_pairs={{0,1},{1,0},{2,3},{3,2},{4,5},{5,4},{6,7},{7,6},{8,9},{9,8},{10,11... | collective-permute-start | bytes 1572872 | tf_op jit(solution)/shard_map/ppermute | solution.py:140
  106.3 9.4 %collective-permute-start.26 = (bf16[1024,128]{1,0:T(8,128)(2,1)}, bf16[1024,128]{1,0:T(8,128)(2,1)}, u32[]{:S(2)}, u32[]{:S(2)}) collective-permute-start(bf16[1024,128]{1,0:T(8,128)(2,1)} %slice.38), channel_id=1, source_target_pairs={{0,32},{1,33},{2,34},{3,35},{4,36},{5,37},{6,38},{7,39},{8,40},{9,... | collective-permute-start | bytes 786440 | tf_op jit(solution)/shard_map/ppermute | solution.py:140
  107.8 7.9 %collective-permute-start.18 = (bf16[1024,128]{1,0:T(8,128)(2,1)}, bf16[1024,128]{1,0:T(8,128)(2,1)}, u32[]{:S(2)}, u32[]{:S(2)}) collective-permute-start(bf16[1024,128]{1,0:T(8,128)(2,1)} %collective-permute-done.16), channel_id=1, source_target_pairs={{0,1},{1,0},{2,3},{3,2},{4,5},{5,4},{6,7},{7,6},{8,9},{9,8},{10,11... | collective-permute-start | bytes 786440 | tf_op jit(solution)/shard_map/ppermute | solution.py:140
  109.9 5.8 %collective-permute-start.17 = (bf16[1024,128]{1,0:T(8,128)(2,1)}, bf16[1024,128]{1,0:T(8,128)(2,1)}, u32[]{:S(2)}, u32[]{:S(2)}) collective-permute-start(bf16[1024,128]{1,0:T(8,128)(2,1)} %collective-permute-done.15), channel_id=1, source_target_pairs={{0,1},{1,0},{2,3},{3,2},{4,5},{5,4},{6,7},{7,6},{8,9},{9,8},{10,11... | collective-permute-start | bytes 786440 | tf_op jit(solution)/shard_map/ppermute | solution.py:140
  (31 other events, 56.0 us)

commit v2 on v1

--- a/solution.py
+++ b/solution.py
@@ -19,39 +19,41 @@
 KC = 8
 
 
-def tables():
-    n = np.arange(WLEN)
-    inside = np.abs(n[:, None] - n[None, :]) <= HALF
-    harmonic = np.arange(1, F + 1)[None, :]
-    phase = 2.0 * math.pi / WLEN * (n[:, None] * harmonic % WLEN)
-    dft = np.concatenate([np.cos(phase), -np.sin(phase)], axis=1)
-    k = np.arange(F)
-    near = np.abs(k[:, None] - k[None, :]) <= BAND
-    zero = np.zeros((F, F))
-    smooth = np.block([[near, zero], [zero, near]])
-    total = np.block([[np.ones((F, F)), zero], [zero, np.ones((F, F))]])
-    sums = np.concatenate([smooth, total], axis=1)
-    sums = np.concatenate([sums, sums], axis=0)
-    bf = ml_dtypes.bfloat16
-    return (
-        inside.astype(bf),
-        (1.0 / inside.sum(0, dtype=np.float64))[None, :].astype(np.float32),
-        dft.astype(bf),
-        sums.astype(bf),
-        (1.0 / np.tile(near.sum(0), 2))[None, :].astype(np.float32),
-    )
-
-
-def whiten_kernel(
-    order, slab, wid, raw, quality, inside, inv_count, dft, sums, inv_near, out, white, placed
-):
+def dft_table():
+    n = np.arange(WLEN)[:, None]
+    phase = 2.0 * math.pi / WLEN * (n * np.arange(1, F + 1)[None, :] % WLEN)
+    table = np.concatenate([np.cos(phase), -np.sin(phase)], axis=1)
+    return jnp.asarray(table.astype(ml_dtypes.bfloat16))
+
+
+def iotas(shape):
+    return lax.broadcasted_iota(jnp.int32, shape, 0), lax.broadcasted_iota(jnp.int32, shape, 1)
+
+
+def make_tables(inside, sums):
+    row, col = iotas((WLEN, WLEN))
+    inside[...] = jnp.where(jnp.abs(row - col) <= HALF, 1.0, 0.0).astype(BF16)
+    row, col = iotas((4 * F, 4 * F))
+    same = (row // F) % 2 == (col // F) % 2
+    near = (jnp.abs(row % F - col % F) <= BAND) | (col >= 2 * F)
+    sums[...] = jnp.where(same & near, 1.0, 0.0).astype(BF16)
+
+
+def inverse_count(length, half_width, period):
+    place = iotas((1, length))[1] % period
+    upper = jnp.minimum(place + half_width + 1, period)
+    return 1.0 / (upper - jnp.maximum(place - half_width, 0)).astype(F32)
+
+
+def whiten_kernel(order, slab, wid, raw, quality, dft, out, white, placed, inside, sums):
     step = pl.program_id(0)
+    pl.when(step == 0)(functools.partial(make_tables, inside, sums))
     x = raw[0].astype(F32)
     centred = x - jnp.sum(x, axis=1, keepdims=True) * (1.0 / WLEN)
     magnitude = jnp.abs(centred)
     level = jnp.sum(magnitude, axis=1, keepdims=True) * (1.0 / WLEN) + 1e-6
     window_sum = jnp.dot(magnitude.astype(BF16), inside[...], preferred_element_type=F32)
-    normed = (centred / (window_sum * inv_count[...] + 0.25 * level)).astype(BF16)
+    normed = (centred / (window_sum * inverse_count(WLEN, HALF, WLEN) + 0.25 * level)).astype(BF16)
     spectrum = jnp.dot(normed, dft[...], preferred_element_type=F32)
     squares = spectrum * spectrum
     power = squares + pltpu.roll(squares, F, 1)
@@ -75,7 +77,7 @@
         row = quality[pl.ds(step * (ROWS // 128) + part, 1), :].astype(F32)
         weights.append(jnp.sum(jnp.where(eye, row, 0.0), axis=1, keepdims=True))
     weight = jnp.concatenate(weights, axis=0) * amplitude
-    scale = weight * lax.rsqrt(both[:, : 2 * F] * inv_near[...] + 0.1 * total)
+    scale = weight * lax.rsqrt(both[:, : 2 * F] * inverse_count(2 * F, BAND, F) + 0.1 * total)
     white[pl.ds(pl.multiple_of(step * ROWS, ROWS), ROWS), :] = spectrum * scale
 
     @pl.when(step == pl.num_programs(0) - 1)
@@ -91,9 +93,7 @@
 
 
 def whiten(raw, quality, order, slab, wid):
-    inside, inv_count, dft, sums, inv_near = tables()
-    whole = lambda a: pl.BlockSpec(a.shape, lambda i, *_: (0, 0))
-    consts = [inside, inv_count, dft, sums, inv_near]
+    whole = lambda shape: pl.BlockSpec(shape, lambda i, *_: (0, 0))
     return pl.pallas_call(
         whiten_kernel,
         grid_spec=pltpu.PrefetchScalarGridSpec(
@@ -101,16 +101,21 @@
             grid=(C // ROWS,),
             in_specs=[
                 pl.BlockSpec((1, ROWS, WLEN), lambda i, *_: (0, i, 0)),
-                whole(quality),
-                *[whole(a) for a in consts],
+                whole(quality.shape),
+                whole((WLEN, 2 * F)),
             ],
-            out_specs=pl.BlockSpec((C, 2 * F), lambda i, *_: (0, 0)),
-            scratch_shapes=[pltpu.VMEM((C, 2 * F), F32), pltpu.VMEM((C, 2 * F), F32)],
+            out_specs=whole((C, 2 * F)),
+            scratch_shapes=[
+                pltpu.VMEM((C, 2 * F), F32),
+                pltpu.VMEM((C, 2 * F), F32),
+                pltpu.VMEM((WLEN, WLEN), BF16),
+                pltpu.VMEM((4 * F, 4 * F), BF16),
+            ],
         ),
         out_shape=jax.ShapeDtypeStruct((C, 2 * F), BF16),
-        compiler_params=pltpu.CompilerParams(vmem_limit_bytes=32 << 20),
+        compiler_params=pltpu.CompilerParams(vmem_limit_bytes=58 << 20),
         name="whiten",
-    )(order, slab, wid, raw, quality, *[jnp.asarray(a) for a in consts])
+    )(order, slab, wid, raw, quality, dft_table())
 
 
 def turn_kernel(received, out, wide, turned):
@@ -218,7 +223,7 @@
             scratch_shapes=[pltpu.VMEM((KC, 256, 256), BF16), pltpu.VMEM((KC, 256, 256), BF16)],
         ),
         out_shape=jax.ShapeDtypeStruct((2, F, 256, 128), F32),
-        compiler_params=pltpu.CompilerParams(vmem_limit_bytes=40 << 20),
+        compiler_params=pltpu.CompilerParams(vmem_limit_bytes=58 << 20),
         name="product",
     )(meta, *arrays)
 

time: 142 us -> 126 us (0.89)
  local copies, waits for them, and re-layouts: 29 us -> 3.52 us
  Pallas kernels: 22.7 us -> 29 us
  waiting for transfers between devices: 28.3 us -> 31.4 us
    unnamed x70 -> x38, local copies, waits for them, and re-layouts: 26.1 us -> 0.07 us
    pallas_call x1, Pallas kernels: 12.2 us -> 16 us  [product(): pl.pallas_call(functools.partial(product_kernel, row_parts=[len(g) for g...]
    ppermute x28, waiting for transfers between devices: 28.3 us -> 31.4 us  [shift(): lax.ppermute(x, AXES, [(int(a), int(b)) for a, b in zip(ids.ravel(), to.r...]
    pallas_call x1, Pallas kernels: 9.48 us -> 12 us  [whiten(): pl.pallas_call(whiten_kernel, grid_spec=pltpu.PrefetchScalarGridSpec(num_...]
  transfers between devices with their start and end apart: 28 -> 28, of which waited for: 9 -> 9; matrix products, arithmetic and copies ran while one was open for 2% -> 3% of each run, Pallas kernels for 0% -> 0%
where the time goes in v2:
time: 126 us; the launch traced here: 125 us
  starting transfers between devices  35.3 us (28%)
  waiting for transfers between devices  31.4 us (25%)
  Pallas kernels  29 us (23%)
  blocking collectives  25.1 us (20%)
  local copies, waits for them, and re-layouts  3.52 us (3%)
    ppermute x28, starting transfers between devices, shift(): lax.ppermute(x, AXES, [(int(a), int(b)) for a, b in zip(ids.ravel(), to.r...  35.3 us
    ppermute x28, waiting for transfers between devices, shift(): lax.ppermute(x, AXES, [(int(a), int(b)) for a, b in zip(ids.ravel(), to.r...  31.4 us
    all_to_all x1, blocking collectives, body(): lax.all_to_all(spectra.reshape(NW, CB, 2 * F), AXES, split_axis=0, concat...  25.1 us
    pallas_call x1, Pallas kernels, product(): pl.pallas_call(functools.partial(product_kernel, row_parts=[len(g) for g...  16 us
    pallas_call x1, Pallas kernels, whiten(): pl.pallas_call(whiten_kernel, grid_spec=pltpu.PrefetchScalarGridSpec(num_...  12 us
  transfers between devices with their start and end apart: 28, of which 9 were waited for; matrix products, arithmetic and copies ran while one was open for 3% of the time, Pallas kernels for 0%

profile of v2, /device:TPU:1, one launch (start us, length us, event | category | flops | bytes accessed | tf_op | source)
XLA Modules:
  0.0 124.6 jit_solution(8622462363217041791)
XLA Ops:
  0.0 12.0 %whiten.1 = bf16[2048,128]{1,0:T(8,128)(2,1)} custom-call(s32[2048]{0:T(1024)} %order.1, s32[4]{0:T(128)} %slab.1, s32[1]{0:T(128)} %bitcast.24.wid, bf16[1,2048,512]{2,1,0:T(8,128)(2,1)} %raw.1, s32[16,128]{1,0:T(8,128)} %bitcast.79, bf16[512,128]{1,0:T(8,128)(2,1)} %constant.164.clone.dft), custom_call_target="tpu_custom_call" | custom-call | tf_op jit(solution)/shard_map/whiten/pallas_call | solution.py:97
  12.0 25.1 %all_to_all.5 = bf16[128,16,128]{2,1,0:T(8,128)(2,1)S(1)} all-to-all(bf16[128,16,128]{2,1,0:T(8,128)(2,1)} %bitcast.60), channel_id=1, replica_groups=mesh['src'=8,'rcv'=16] {'src','rcv'}, dimensions={0} | all-to-all | bytes 1048576 | tf_op jit(solution)/shard_map/all_to_all | solution.py:235
  37.1 1.0 turn.1
  38.7 0.9 collective-permute-start.19
  40.7 2.0 %collective-permute-start.9 = (bf16[2048,128]{1,0:T(8,128)(2,1)S(1)}, bf16[2048,128]{1,0:T(8,128)(2,1)S(1)}, u32[]{:S(2)}, u32[]{:S(2)}) collective-permute-start(bf16[2048,128]{1,0:T(8,128)(2,1)S(1)} %turn.1), channel_id=1, source_target_pairs={{0,2},{1,3},{2,0},{3,1},{4,6},{5,7},{6,4},{7,5},{8,10},{9,11},{10,... | collective-permute-start | bytes 1572872 | tf_op jit(solution)/shard_map/ppermute | solution.py:145
  42.7 7.9 %collective-permute-done.20 = bf16[2048,128]{1,0:T(8,128)(2,1)S(1)} collective-permute-done((bf16[2048,128]{1,0:T(8,128)(2,1)S(1)}, bf16[2048,128]{1,0:T(8,128)(2,1)S(1)}, u32[]{:S(2)}, u32[]{:S(2)}) %collective-permute-start.20) | collective-permute-done | bytes 524320 | tf_op jit(solution)/shard_map/ppermute | solution.py:145
  50.6 1.2 collective-permute-done.19
  51.8 2.5 %collective-permute-start = (bf16[2048,128]{1,0:T(8,128)(2,1)S(1)}, bf16[2048,128]{1,0:T(8,128)(2,1)}, u32[]{:S(2)}, u32[]{:S(2)}) collective-permute-start(bf16[2048,128]{1,0:T(8,128)(2,1)S(1)} %turn.1), channel_id=1, source_target_pairs={{0,1},{1,0},{2,3},{3,2},{4,5},{5,4},{6,7},{7,6},{8,9},{9,8},{10,11... | collective-permute-start | bytes 1572872 | tf_op jit(solution)/shard_map/ppermute | solution.py:145
  55.1 0.9 collective-permute-start.21
  56.0 8.3 %collective-permute-done.9 = bf16[2048,128]{1,0:T(8,128)(2,1)S(1)} collective-permute-done((bf16[2048,128]{1,0:T(8,128)(2,1)S(1)}, bf16[2048,128]{1,0:T(8,128)(2,1)S(1)}, u32[]{:S(2)}, u32[]{:S(2)}) %collective-permute-start.9) | collective-permute-done | bytes 524320 | tf_op jit(solution)/shard_map/ppermute | solution.py:145
  64.3 2.3 %collective-permute-start.25 = (bf16[2048,128]{1,0:T(8,128)(2,1)S(1)}, bf16[2048,128]{1,0:T(8,128)(2,1)S(1)}, u32[]{:S(2)}, u32[]{:S(2)}) collective-permute-start(bf16[2048,128]{1,0:T(8,128)(2,1)S(1)} %collective-permute-done.23), channel_id=1, source_target_pairs={{0,96},{1,97},{2,98},{3,99},{4,100},{5,101},{6,102},{7,103},{8,104... | collective-permute-start | bytes 1572872 | tf_op jit(solution)/shard_map/ppermute | solution.py:145
  66.8 1.4 %collective-permute-start.5 = (bf16[1024,128]{1,0:T(8,128)(2,1)S(1)}, bf16[1024,128]{1,0:T(8,128)(2,1)S(1)}, u32[]{:S(2)}, u32[]{:S(2)}) collective-permute-start(bf16[1024,128]{1,0:T(8,128)(2,1)S(1)} %slice.32), channel_id=1, source_target_pairs={{0,4},{1,5},{2,6},{3,7},{4,8},{5,9},{6,10},{7,11},{8,12},{9,13},{1... | collective-permute-start | bytes 786440 | tf_op jit(solution)/shard_map/ppermute | solution.py:145
  68.2 1.4 %collective-permute-start.13 = (bf16[2048,128]{1,0:T(8,128)(2,1)S(1)}, bf16[2048,128]{1,0:T(8,128)(2,1)}, u32[]{:S(2)}, u32[]{:S(2)}) collective-permute-start(bf16[2048,128]{1,0:T(8,128)(2,1)S(1)} %collective-permute-done.9), channel_id=1, source_target_pairs={{0,12},{1,13},{2,14},{3,15},{4,0},{5,1},{6,2},{7,3},{8,4},{9,5},{1... | collective-permute-start | bytes 1572872 | tf_op jit(solution)/shard_map/ppermute | solution.py:145
  69.6 2.5 %collective-permute-done.6 = bf16[1024,128]{1,0:T(8,128)(2,1)S(1)} collective-permute-done((bf16[1024,128]{1,0:T(8,128)(2,1)S(1)}, bf16[1024,128]{1,0:T(8,128)(2,1)S(1)}, u32[]{:S(2)}, u32[]{:S(2)}) %collective-permute-start.6) | collective-permute-done | bytes 262176 | tf_op jit(solution)/shard_map/ppermute | solution.py:145
  72.1 1.2 collective-permute-done.5
  73.3 5.4 %collective-permute-start.10 = (bf16[2048,128]{1,0:T(8,128)(2,1)S(1)}, bf16[2048,128]{1,0:T(8,128)(2,1)S(1)}, u32[]{:S(2)}, u32[]{:S(2)}) collective-permute-start(bf16[2048,128]{1,0:T(8,128)(2,1)S(1)} %collective-permute-done.9), channel_id=1, source_target_pairs={{0,1},{1,0},{2,3},{3,2},{4,5},{5,4},{6,7},{7,6},{8,9},{9,8},{10,11... | collective-permute-start | bytes 1572872 | tf_op jit(solution)/shard_map/ppermute | solution.py:145
  78.8 3.5 %collective-permute-start.2 = (bf16[2048,128]{1,0:T(8,128)(2,1)S(1)}, bf16[2048,128]{1,0:T(8,128)(2,1)S(1)}, u32[]{:S(2)}, u32[]{:S(2)}) collective-permute-start(bf16[2048,128]{1,0:T(8,128)(2,1)S(1)} %collective-permute-done.1), channel_id=1, source_target_pairs={{0,1},{1,0},{2,3},{3,2},{4,5},{5,4},{6,7},{7,6},{8,9},{9,8},{10,11... | collective-permute-start | bytes 1572872 | tf_op jit(solution)/shard_map/ppermute | solution.py:145
  82.3 1.0 collective-permute-done.13
  83.3 3.4 %collective-permute-start.8 = (bf16[1024,128]{1,0:T(8,128)(2,1)S(1)}, bf16[1024,128]{1,0:T(8,128)(2,1)S(1)}, u32[]{:S(2)}, u32[]{:S(2)}) collective-permute-start(bf16[1024,128]{1,0:T(8,128)(2,1)S(1)} %collective-permute-done.6), channel_id=1, source_target_pairs={{0,1},{1,0},{2,3},{3,2},{4,5},{5,4},{6,7},{7,6},{8,9},{9,8},{10,11... | collective-permute-start | bytes 786440 | tf_op jit(solution)/shard_map/ppermute | solution.py:145
  86.7 2.1 %collective-permute-start.7 = (bf16[1024,128]{1,0:T(8,128)(2,1)S(1)}, bf16[1024,128]{1,0:T(8,128)(2,1)S(1)}, u32[]{:S(2)}, u32[]{:S(2)}) collective-permute-start(bf16[1024,128]{1,0:T(8,128)(2,1)S(1)} %collective-permute-done.5), channel_id=1, source_target_pairs={{0,1},{1,0},{2,3},{3,2},{4,5},{5,4},{6,7},{7,6},{8,9},{9,8},{10,11... | collective-permute-start | bytes 786440 | tf_op jit(solution)/shard_map/ppermute | solution.py:145
  88.8 1.0 slice.35
  89.8 1.0 slice.34
  90.8 2.1 %collective-permute-start.27 = (bf16[1024,128]{1,0:T(8,128)(2,1)S(1)}, bf16[1024,128]{1,0:T(8,128)(2,1)S(1)}, u32[]{:S(2)}, u32[]{:S(2)}) collective-permute-start(bf16[1024,128]{1,0:T(8,128)(2,1)S(1)} %slice.39), channel_id=1, source_target_pairs={{0,96},{1,97},{2,98},{3,99},{4,100},{5,101},{6,102},{7,103},{8,104... | collective-permute-start | bytes 786440 | tf_op jit(solution)/shard_map/ppermute | solution.py:145
  93.0 1.3 %collective-permute-start.15 = (bf16[1024,128]{1,0:T(8,128)(2,1)S(1)}, bf16[1024,128]{1,0:T(8,128)(2,1)}, u32[]{:S(2)}, u32[]{:S(2)}) collective-permute-start(bf16[1024,128]{1,0:T(8,128)(2,1)S(1)} %slice.34), channel_id=1, source_target_pairs={{0,4},{1,5},{2,6},{3,7},{4,8},{5,9},{6,10},{7,11},{8,12},{9,13},{1... | collective-permute-start | bytes 786440 | tf_op jit(solution)/shard_map/ppermute | solution.py:145
  94.4 0.8 collective-permute-start.14
  95.3 0.8 slice.38
  96.1 2.8 %collective-permute-done.27 = bf16[1024,128]{1,0:T(8,128)(2,1)S(1)} collective-permute-done((bf16[1024,128]{1,0:T(8,128)(2,1)S(1)}, bf16[1024,128]{1,0:T(8,128)(2,1)S(1)}, u32[]{:S(2)}, u32[]{:S(2)}) %collective-permute-start.27) | collective-permute-done | bytes 262176 | tf_op jit(solution)/shard_map/ppermute | solution.py:145
  98.9 1.7 %collective-permute-done.16 = bf16[1024,128]{1,0:T(8,128)(2,1)} collective-permute-done((bf16[1024,128]{1,0:T(8,128)(2,1)S(1)}, bf16[1024,128]{1,0:T(8,128)(2,1)}, u32[]{:S(2)}, u32[]{:S(2)}) %collective-permute-start.16) | collective-permute-done | bytes 262176 | tf_op jit(solution)/shard_map/ppermute | solution.py:145
  100.6 1.1 collective-permute-start.18
  101.8 1.4 %collective-permute-start.17 = (bf16[1024,128]{1,0:T(8,128)(2,1)}, bf16[1024,128]{1,0:T(8,128)(2,1)}, u32[]{:S(2)}, u32[]{:S(2)}) collective-permute-start(bf16[1024,128]{1,0:T(8,128)(2,1)} %collective-permute-done.15), channel_id=1, source_target_pairs={{0,1},{1,0},{2,3},{3,2},{4,5},{5,4},{6,7},{7,6},{8,9},{9,8},{10,11... | collective-permute-start | bytes 786440 | tf_op jit(solution)/shard_map/ppermute | solution.py:145
  103.8 4.7 %collective-permute-done.26 = bf16[1024,128]{1,0:T(8,128)(2,1)} collective-permute-done((bf16[1024,128]{1,0:T(8,128)(2,1)}, bf16[1024,128]{1,0:T(8,128)(2,1)}, u32[]{:S(2)}, u32[]{:S(2)}) %collective-permute-start.26) | collective-permute-done | bytes 262176 | tf_op jit(solution)/shard_map/ppermute | solution.py:145
  108.6 16.0 %product.1 = f32[2,64,256,128]{3,2,1,0:T(8,128)} custom-call(s32[24]{0:T(128)} %stack.99.meta, bf16[64,32,128]{2,1,0:T(8,128)(2,1)} %bitcast.57, bf16[64,32,128]{2,1,0:T(8,128)(2,1)} %bitcast.29.refs_1_, bf16[64,32,128]{2,1,0:T(8,128)(2,1)} %bitcast.64, bf16[64,32,128]{2,1,0:T(8,128)(2,1)} %bitcast.71, bf16[64,32,128]{2,1,0:T(8,128)(2,1)} %bitcast.63, ...), custom_call_target="tpu_custom_call" | custom-call | tf_op jit(solution)/shard_map/product/pallas_call | solution.py:212
  (75 shorter events, 3.8 us)
Async XLA Ops:
  38.1 70.4 %copy-start = (bf16[2048,128]{1,0:T(8,128)(2,1)}, bf16[2048,128]{1,0:T(8,128)(2,1)S(1)}, u32[]{:S(2)}) copy-start(bf16[2048,128]{1,0:T(8,128)(2,1)S(1)} %turn.1) | copy-start | bytes 1572868
  38.1 12.5 %collective-permute-start.20 = (bf16[2048,128]{1,0:T(8,128)(2,1)S(1)}, bf16[2048,128]{1,0:T(8,128)(2,1)S(1)}, u32[]{:S(2)}, u32[]{:S(2)}) collective-permute-start(bf16[2048,128]{1,0:T(8,128)(2,1)S(1)} %turn.1), channel_id=1, source_target_pairs={{0,96},{1,97},{2,98},{3,99},{4,100},{5,101},{6,102},{7,103},{8,104... | collective-permute-start | bytes 1572872 | tf_op jit(solution)/shard_map/ppermute | solution.py:145
  38.7 13.1 %collective-permute-start.19 = (bf16[2048,128]{1,0:T(8,128)(2,1)S(1)}, bf16[2048,128]{1,0:T(8,128)(2,1)S(1)}, u32[]{:S(2)}, u32[]{:S(2)}) collective-permute-start(bf16[2048,128]{1,0:T(8,128)(2,1)S(1)} %turn.1), channel_id=1, source_target_pairs={{0,32},{1,33},{2,34},{3,35},{4,36},{5,37},{6,38},{7,39},{8,40},{9,... | collective-permute-start | bytes 1572872 | tf_op jit(solution)/shard_map/ppermute | solution.py:145
  39.6 14.7 %collective-permute-start.3 = (bf16[2048,128]{1,0:T(8,128)(2,1)S(1)}, bf16[2048,128]{1,0:T(8,128)(2,1)S(1)}, u32[]{:S(2)}, u32[]{:S(2)}) collective-permute-start(bf16[2048,128]{1,0:T(8,128)(2,1)S(1)} %turn.1), channel_id=1, source_target_pairs={{0,12},{1,13},{2,14},{3,15},{4,0},{5,1},{6,2},{7,3},{8,4},{9,5},{1... | collective-permute-start | bytes 1572872 | tf_op jit(solution)/shard_map/ppermute | solution.py:145
  40.4 14.7 %collective-permute-start.23 = (bf16[2048,128]{1,0:T(8,128)(2,1)S(1)}, bf16[2048,128]{1,0:T(8,128)(2,1)S(1)}, u32[]{:S(2)}, u32[]{:S(2)}) collective-permute-start(bf16[2048,128]{1,0:T(8,128)(2,1)S(1)} %turn.1), channel_id=1, source_target_pairs={{0,16},{1,17},{2,18},{3,19},{4,20},{5,21},{6,22},{7,23},{8,24},{9,... | collective-permute-start | bytes 1572872 | tf_op jit(solution)/shard_map/ppermute | solution.py:145
  40.7 23.7 %collective-permute-start.9 = (bf16[2048,128]{1,0:T(8,128)(2,1)S(1)}, bf16[2048,128]{1,0:T(8,128)(2,1)S(1)}, u32[]{:S(2)}, u32[]{:S(2)}) collective-permute-start(bf16[2048,128]{1,0:T(8,128)(2,1)S(1)} %turn.1), channel_id=1, source_target_pairs={{0,2},{1,3},{2,0},{3,1},{4,6},{5,7},{6,4},{7,5},{8,10},{9,11},{10,... | collective-permute-start | bytes 1572872 | tf_op jit(solution)/shard_map/ppermute | solution.py:145
  50.6 58.0 %copy-start.1 = (bf16[2048,128]{1,0:T(8,128)(2,1)}, bf16[2048,128]{1,0:T(8,128)(2,1)S(1)}, u32[]{:S(2)}) copy-start(bf16[2048,128]{1,0:T(8,128)(2,1)S(1)} %collective-permute-done.20) | copy-start | bytes 1572868
  50.6 16.0 %collective-permute-start.1 = (bf16[2048,128]{1,0:T(8,128)(2,1)S(1)}, bf16[2048,128]{1,0:T(8,128)(2,1)S(1)}, u32[]{:S(2)}, u32[]{:S(2)}) collective-permute-start(bf16[2048,128]{1,0:T(8,128)(2,1)S(1)} %turn.1), channel_id=1, source_target_pairs={{0,4},{1,5},{2,6},{3,7},{4,8},{5,9},{6,10},{7,11},{8,12},{9,13},{1... | collective-permute-start | bytes 1572872 | tf_op jit(solution)/shard_map/ppermute | solution.py:145
  51.8 56.8 %copy-start.2 = (bf16[2048,128]{1,0:T(8,128)(2,1)}, bf16[2048,128]{1,0:T(8,128)(2,1)S(1)}, u32[]{:S(2)}) copy-start(bf16[2048,128]{1,0:T(8,128)(2,1)S(1)} %collective-permute-done.19) | copy-start | bytes 1572868
  51.8 15.0 %collective-permute-start = (bf16[2048,128]{1,0:T(8,128)(2,1)S(1)}, bf16[2048,128]{1,0:T(8,128)(2,1)}, u32[]{:S(2)}, u32[]{:S(2)}) collective-permute-start(bf16[2048,128]{1,0:T(8,128)(2,1)S(1)} %turn.1), channel_id=1, source_target_pairs={{0,1},{1,0},{2,3},{3,2},{4,5},{5,4},{6,7},{7,6},{8,9},{9,8},{10,11... | collective-permute-start | bytes 1572872 | tf_op jit(solution)/shard_map/ppermute | solution.py:145
  54.3 54.2 %copy-start.3 = (bf16[2048,128]{1,0:T(8,128)(2,1)}, bf16[2048,128]{1,0:T(8,128)(2,1)S(1)}, u32[]{:S(2)}) copy-start(bf16[2048,128]{1,0:T(8,128)(2,1)S(1)} %collective-permute-done.3) | copy-start | bytes 1572868
  54.3 12.5 %collective-permute-start.22 = (bf16[1024,128]{1,0:T(8,128)(2,1)S(1)}, bf16[1024,128]{1,0:T(8,128)(2,1)S(1)}, u32[]{:S(2)}, u32[]{:S(2)}) collective-permute-start(bf16[1024,128]{1,0:T(8,128)(2,1)S(1)} %slice.37), channel_id=1, source_target_pairs={{0,96},{1,97},{2,98},{3,99},{4,100},{5,101},{6,102},{7,103},{8,104... | collective-permute-start | bytes 786440 | tf_op jit(solution)/shard_map/ppermute | solution.py:145
  55.1 13.1 %collective-permute-start.21 = (bf16[1024,128]{1,0:T(8,128)(2,1)S(1)}, bf16[1024,128]{1,0:T(8,128)(2,1)S(1)}, u32[]{:S(2)}, u32[]{:S(2)}) collective-permute-start(bf16[1024,128]{1,0:T(8,128)(2,1)S(1)} %slice.36), channel_id=1, source_target_pairs={{0,32},{1,33},{2,34},{3,35},{4,36},{5,37},{6,38},{7,39},{8,40},{9,... | collective-permute-start | bytes 786440 | tf_op jit(solution)/shard_map/ppermute | solution.py:145
  64.3 14.4 %collective-permute-start.25 = (bf16[2048,128]{1,0:T(8,128)(2,1)S(1)}, bf16[2048,128]{1,0:T(8,128)(2,1)S(1)}, u32[]{:S(2)}, u32[]{:S(2)}) collective-permute-start(bf16[2048,128]{1,0:T(8,128)(2,1)S(1)} %collective-permute-done.23), channel_id=1, source_target_pairs={{0,96},{1,97},{2,98},{3,99},{4,100},{5,101},{6,102},{7,103},{8,104... | collective-permute-start | bytes 1572872 | tf_op jit(solution)/shard_map/ppermute | solution.py:145
  66.6 5.5 %collective-permute-start.6 = (bf16[1024,128]{1,0:T(8,128)(2,1)S(1)}, bf16[1024,128]{1,0:T(8,128)(2,1)S(1)}, u32[]{:S(2)}, u32[]{:S(2)}) collective-permute-start(bf16[1024,128]{1,0:T(8,128)(2,1)S(1)} %slice.33), channel_id=1, source_target_pairs={{0,12},{1,13},{2,14},{3,15},{4,0},{5,1},{6,2},{7,3},{8,4},{9,5},{1... | collective-permute-start | bytes 786440 | tf_op jit(solution)/shard_map/ppermute | solution.py:145
  66.8 12.0 %collective-permute-start.24 = (bf16[2048,128]{1,0:T(8,128)(2,1)S(1)}, bf16[2048,128]{1,0:T(8,128)(2,1)S(1)}, u32[]{:S(2)}, u32[]{:S(2)}) collective-permute-start(bf16[2048,128]{1,0:T(8,128)(2,1)S(1)} %collective-permute-done.23), channel_id=1, source_target_pairs={{0,32},{1,33},{2,34},{3,35},{4,36},{5,37},{6,38},{7,39},{8,40},{9,... | collective-permute-start | bytes 1572872 | tf_op jit(solution)/shard_map/ppermute | solution.py:145
  66.8 6.5 %collective-permute-start.5 = (bf16[1024,128]{1,0:T(8,128)(2,1)S(1)}, bf16[1024,128]{1,0:T(8,128)(2,1)S(1)}, u32[]{:S(2)}, u32[]{:S(2)}) collective-permute-start(bf16[1024,128]{1,0:T(8,128)(2,1)S(1)} %slice.32), channel_id=1, source_target_pairs={{0,4},{1,5},{2,6},{3,7},{4,8},{5,9},{6,10},{7,11},{8,12},{9,13},{1... | collective-permute-start | bytes 786440 | tf_op jit(solution)/shard_map/ppermute | solution.py:145
  68.2 15.1 %collective-permute-start.13 = (bf16[2048,128]{1,0:T(8,128)(2,1)S(1)}, bf16[2048,128]{1,0:T(8,128)(2,1)}, u32[]{:S(2)}, u32[]{:S(2)}) collective-permute-start(bf16[2048,128]{1,0:T(8,128)(2,1)S(1)} %collective-permute-done.9), channel_id=1, source_target_pairs={{0,12},{1,13},{2,14},{3,15},{4,0},{5,1},{6,2},{7,3},{8,4},{9,5},{1... | collective-permute-start | bytes 1572872 | tf_op jit(solution)/shard_map/ppermute | solution.py:145
  72.1 14.5 %collective-permute-start.11 = (bf16[2048,128]{1,0:T(8,128)(2,1)S(1)}, bf16[2048,128]{1,0:T(8,128)(2,1)}, u32[]{:S(2)}, u32[]{:S(2)}) collective-permute-start(bf16[2048,128]{1,0:T(8,128)(2,1)S(1)} %collective-permute-done.9), channel_id=1, source_target_pairs={{0,4},{1,5},{2,6},{3,7},{4,8},{5,9},{6,10},{7,11},{8,12},{9,13},{1... | collective-permute-start | bytes 1572872 | tf_op jit(solution)/shard_map/ppermute | solution.py:145
  73.3 17.4 %collective-permute-start.10 = (bf16[2048,128]{1,0:T(8,128)(2,1)S(1)}, bf16[2048,128]{1,0:T(8,128)(2,1)S(1)}, u32[]{:S(2)}, u32[]{:S(2)}) collective-permute-start(bf16[2048,128]{1,0:T(8,128)(2,1)S(1)} %collective-permute-done.9), channel_id=1, source_target_pairs={{0,1},{1,0},{2,3},{3,2},{4,5},{5,4},{6,7},{7,6},{8,9},{9,8},{10,11... | collective-permute-start | bytes 1572872 | tf_op jit(solution)/shard_map/ppermute | solution.py:145
  78.7 14.3 %collective-permute-start.4 = (bf16[2048,128]{1,0:T(8,128)(2,1)S(1)}, bf16[2048,128]{1,0:T(8,128)(2,1)S(1)}, u32[]{:S(2)}, u32[]{:S(2)}) collective-permute-start(bf16[2048,128]{1,0:T(8,128)(2,1)S(1)} %collective-permute-done.3), channel_id=1, source_target_pairs={{0,1},{1,0},{2,3},{3,2},{4,5},{5,4},{6,7},{7,6},{8,9},{9,8},{10,11... | collective-permute-start | bytes 1572872 | tf_op jit(solution)/shard_map/ppermute | solution.py:145
  78.8 16.4 %collective-permute-start.2 = (bf16[2048,128]{1,0:T(8,128)(2,1)S(1)}, bf16[2048,128]{1,0:T(8,128)(2,1)S(1)}, u32[]{:S(2)}, u32[]{:S(2)}) collective-permute-start(bf16[2048,128]{1,0:T(8,128)(2,1)S(1)} %collective-permute-done.1), channel_id=1, source_target_pairs={{0,1},{1,0},{2,3},{3,2},{4,5},{5,4},{6,7},{7,6},{8,9},{9,8},{10,11... | collective-permute-start | bytes 1572872 | tf_op jit(solution)/shard_map/ppermute | solution.py:145
  83.3 9.6 %collective-permute-start.8 = (bf16[1024,128]{1,0:T(8,128)(2,1)S(1)}, bf16[1024,128]{1,0:T(8,128)(2,1)S(1)}, u32[]{:S(2)}, u32[]{:S(2)}) collective-permute-start(bf16[1024,128]{1,0:T(8,128)(2,1)S(1)} %collective-permute-done.6), channel_id=1, source_target_pairs={{0,1},{1,0},{2,3},{3,2},{4,5},{5,4},{6,7},{7,6},{8,9},{9,8},{10,11... | collective-permute-start | bytes 786440 | tf_op jit(solution)/shard_map/ppermute | solution.py:145
  86.7 7.7 %collective-permute-start.7 = (bf16[1024,128]{1,0:T(8,128)(2,1)S(1)}, bf16[1024,128]{1,0:T(8,128)(2,1)S(1)}, u32[]{:S(2)}, u32[]{:S(2)}) collective-permute-start(bf16[1024,128]{1,0:T(8,128)(2,1)S(1)} %collective-permute-done.5), channel_id=1, source_target_pairs={{0,1},{1,0},{2,3},{3,2},{4,5},{5,4},{6,7},{7,6},{8,9},{9,8},{10,11... | collective-permute-start | bytes 786440 | tf_op jit(solution)/shard_map/ppermute | solution.py:145
  90.8 8.1 %collective-permute-start.27 = (bf16[1024,128]{1,0:T(8,128)(2,1)S(1)}, bf16[1024,128]{1,0:T(8,128)(2,1)S(1)}, u32[]{:S(2)}, u32[]{:S(2)}) collective-permute-start(bf16[1024,128]{1,0:T(8,128)(2,1)S(1)} %slice.39), channel_id=1, source_target_pairs={{0,96},{1,97},{2,98},{3,99},{4,100},{5,101},{6,102},{7,103},{8,104... | collective-permute-start | bytes 786440 | tf_op jit(solution)/shard_map/ppermute | solution.py:145
  92.9 7.7 %collective-permute-start.16 = (bf16[1024,128]{1,0:T(8,128)(2,1)S(1)}, bf16[1024,128]{1,0:T(8,128)(2,1)}, u32[]{:S(2)}, u32[]{:S(2)}) collective-permute-start(bf16[1024,128]{1,0:T(8,128)(2,1)S(1)} %slice.35), channel_id=1, source_target_pairs={{0,12},{1,13},{2,14},{3,15},{4,0},{5,1},{6,2},{7,3},{8,4},{9,5},{1... | collective-permute-start | bytes 786440 | tf_op jit(solution)/shard_map/ppermute | solution.py:145
  93.0 8.7 %collective-permute-start.15 = (bf16[1024,128]{1,0:T(8,128)(2,1)S(1)}, bf16[1024,128]{1,0:T(8,128)(2,1)}, u32[]{:S(2)}, u32[]{:S(2)}) collective-permute-start(bf16[1024,128]{1,0:T(8,128)(2,1)S(1)} %slice.34), channel_id=1, source_target_pairs={{0,4},{1,5},{2,6},{3,7},{4,8},{5,9},{6,10},{7,11},{8,12},{9,13},{1... | collective-permute-start | bytes 786440 | tf_op jit(solution)/shard_map/ppermute | solution.py:145
  94.4 14.1 %collective-permute-start.14 = (bf16[2048,128]{1,0:T(8,128)(2,1)}, bf16[2048,128]{1,0:T(8,128)(2,1)}, u32[]{:S(2)}, u32[]{:S(2)}) collective-permute-start(bf16[2048,128]{1,0:T(8,128)(2,1)} %collective-permute-done.13), channel_id=1, source_target_pairs={{0,1},{1,0},{2,3},{3,2},{4,5},{5,4},{6,7},{7,6},{8,9},{9,8},{10,11... | collective-permute-start | bytes 1572872 | tf_op jit(solution)/shard_map/ppermute | solution.py:145
  95.2 13.3 %collective-permute-start.12 = (bf16[2048,128]{1,0:T(8,128)(2,1)}, bf16[2048,128]{1,0:T(8,128)(2,1)}, u32[]{:S(2)}, u32[]{:S(2)}) collective-permute-start(bf16[2048,128]{1,0:T(8,128)(2,1)} %collective-permute-done.11), channel_id=1, source_target_pairs={{0,1},{1,0},{2,3},{3,2},{4,5},{5,4},{6,7},{7,6},{8,9},{9,8},{10,11... | collective-permute-start | bytes 1572872 | tf_op jit(solution)/shard_map/ppermute | solution.py:145
  98.9 9.6 %collective-permute-start.26 = (bf16[1024,128]{1,0:T(8,128)(2,1)}, bf16[1024,128]{1,0:T(8,128)(2,1)}, u32[]{:S(2)}, u32[]{:S(2)}) collective-permute-start(bf16[1024,128]{1,0:T(8,128)(2,1)} %slice.38), channel_id=1, source_target_pairs={{0,32},{1,33},{2,34},{3,35},{4,36},{5,37},{6,38},{7,39},{8,40},{9,... | collective-permute-start | bytes 786440 | tf_op jit(solution)/shard_map/ppermute | solution.py:145
  100.6 7.9 %collective-permute-start.18 = (bf16[1024,128]{1,0:T(8,128)(2,1)}, bf16[1024,128]{1,0:T(8,128)(2,1)}, u32[]{:S(2)}, u32[]{:S(2)}) collective-permute-start(bf16[1024,128]{1,0:T(8,128)(2,1)} %collective-permute-done.16), channel_id=1, source_target_pairs={{0,1},{1,0},{2,3},{3,2},{4,5},{5,4},{6,7},{7,6},{8,9},{9,8},{10,11... | collective-permute-start | bytes 786440 | tf_op jit(solution)/shard_map/ppermute | solution.py:145
  101.8 6.7 %collective-permute-start.17 = (bf16[1024,128]{1,0:T(8,128)(2,1)}, bf16[1024,128]{1,0:T(8,128)(2,1)}, u32[]{:S(2)}, u32[]{:S(2)}) collective-permute-start(bf16[1024,128]{1,0:T(8,128)(2,1)} %collective-permute-done.15), channel_id=1, source_target_pairs={{0,1},{1,0},{2,3},{3,2},{4,5},{5,4},{6,7},{7,6},{8,9},{9,8},{10,11... | collective-permute-start | bytes 786440 | tf_op jit(solution)/shard_map/ppermute | solution.py:145
  (15 other events, 309.0 us)

commit v3 on v2

--- a/solution.py
+++ b/solution.py
@@ -17,6 +17,9 @@
 BF16, F32 = jnp.bfloat16, jnp.float32
 ROWS = 256
 KC = 8
+XL_BIT, XH_BIT = 16, 2
+SENT = 3 * CB
+HALF_ROWS = F * 2 * CB
 
 
 def dft_table():
@@ -34,13 +37,13 @@
     row, col = iotas((WLEN, WLEN))
     inside[...] = jnp.where(jnp.abs(row - col) <= HALF, 1.0, 0.0).astype(BF16)
     row, col = iotas((4 * F, 4 * F))
-    same = (row // F) % 2 == (col // F) % 2
-    near = (jnp.abs(row % F - col % F) <= BAND) | (col >= 2 * F)
+    same = ((row ^ col) & F) == 0
+    near = (jnp.abs((row & (F - 1)) - (col & (F - 1))) <= BAND) | (col >= 2 * F)
     sums[...] = jnp.where(same & near, 1.0, 0.0).astype(BF16)
 
 
 def inverse_count(length, half_width, period):
-    place = iotas((1, length))[1] % period
+    place = iotas((1, length))[1] & (period - 1)
     upper = jnp.minimum(place + half_width + 1, period)
     return 1.0 / (upper - jnp.maximum(place - half_width, 0)).astype(F32)
 
@@ -82,14 +85,17 @@
 
     @pl.when(step == pl.num_programs(0) - 1)
     def _():
-        def place(group, carry):
-            base = pl.multiple_of(group * 16, 16)
-            for j in range(16):
-                placed[pl.ds(base + j, 1), :] = white[pl.ds(order[base + j], 1), :]
+        def place(owner, carry):
+            base = owner * CB
+            for j in range(CB):
+                placed[pl.ds(j, 1), :] = white[pl.ds(order[base + j], 1), :]
+            block = placed[...].astype(BF16)
+            for slot, partner in enumerate((0, XH_BIT, XL_BIT)):
+                at = (owner ^ partner) * SENT + slot * CB
+                out[pl.ds(pl.multiple_of(at, CB), CB), :] = block
             return carry
 
-        lax.fori_loop(0, C // 16, place, 0)
-        out[...] = placed[...].astype(BF16)
+        lax.fori_loop(0, C // CB, place, 0)
 
 
 def whiten(raw, quality, order, slab, wid):
@@ -104,37 +110,44 @@
                 whole(quality.shape),
                 whole((WLEN, 2 * F)),
             ],
-            out_specs=whole((C, 2 * F)),
+            out_specs=whole((NW * SENT, 2 * F)),
             scratch_shapes=[
                 pltpu.VMEM((C, 2 * F), F32),
-                pltpu.VMEM((C, 2 * F), F32),
+                pltpu.VMEM((CB, 2 * F), F32),
                 pltpu.VMEM((WLEN, WLEN), BF16),
                 pltpu.VMEM((4 * F, 4 * F), BF16),
             ],
         ),
-        out_shape=jax.ShapeDtypeStruct((C, 2 * F), BF16),
+        out_shape=jax.ShapeDtypeStruct((NW * SENT, 2 * F), BF16),
         compiler_params=pltpu.CompilerParams(vmem_limit_bytes=58 << 20),
         name="whiten",
     )(order, slab, wid, raw, quality, dft_table())
 
 
-def turn_kernel(received, out, wide, turned):
+def turn_kernel(received, row_out, col_out, wide, turned):
     wide[...] = received[...].astype(F32)
-    for p in range(CB):
-        t = wide[pl.ds(p, NW, stride=CB), :].T
-        turned[pl.ds(p, F, stride=2 * CB), :] = t[:F]
-        turned[pl.ds(CB + p, F, stride=2 * CB), :] = t[F:]
-    out[...] = turned[...].astype(BF16)
+    for slot in range(3):
+        for p in range(CB):
+            t = wide[pl.ds(slot * CB + p, NW, stride=SENT), :].T
+            turned[pl.ds(p, F, stride=2 * CB), :] = t[:F]
+            turned[pl.ds(CB + p, F, stride=2 * CB), :] = t[F:]
+        block = turned[...].astype(BF16)
+        if slot == 0:
+            row_out[0:HALF_ROWS, :] = block
+            col_out[0:HALF_ROWS, :] = block
+        else:
+            (row_out if slot == 1 else col_out)[HALF_ROWS:, :] = block
 
 
 def turn(received):
+    shape = jax.ShapeDtypeStruct((2 * HALF_ROWS, NW), BF16)
     return pl.pallas_call(
         turn_kernel,
         in_specs=[pl.BlockSpec(memory_space=pltpu.VMEM)],
-        out_specs=pl.BlockSpec(memory_space=pltpu.VMEM),
-        out_shape=jax.ShapeDtypeStruct((F * 2 * CB, NW), BF16),
-        scratch_shapes=[pltpu.VMEM((NW * CB, 2 * F), F32), pltpu.VMEM((F * 2 * CB, NW), F32)],
-        compiler_params=pltpu.CompilerParams(vmem_limit_bytes=16 << 20),
+        out_specs=[pl.BlockSpec(memory_space=pltpu.VMEM)] * 2,
+        out_shape=[shape, shape],
+        scratch_shapes=[pltpu.VMEM((NW * SENT, 2 * F), F32), pltpu.VMEM((HALF_ROWS, NW), F32)],
+        compiler_params=pltpu.CompilerParams(vmem_limit_bytes=24 << 20),
         name="turn",
     )(received)
 
@@ -145,24 +158,21 @@
     return lax.ppermute(x, AXES, [(int(a), int(b)) for a, b in zip(ids.ravel(), to.ravel())])
 
 
-def gather_ring(x, ring, pair):
-    half = x.shape[0] // 2
-    other = shift(x, pair, 1)
-    found = []
-    for flip, block in ((0, x), (1, other)):
-        after = shift(block, ring, 1)
-        before = shift(block, ring, -1)
-        low = shift(after[:half], ring, 1)
-        high = shift(before[half:], ring, -1)
-        found += [(0, flip, block), (1, flip, after), (3, flip, before), (2, flip, low, high)]
-    return found
-
-
-def product_kernel(meta, *refs, row_parts, col_parts):
-    step = pl.program_id(0)
-    n_in = sum(row_parts) + sum(col_parts)
-    inputs, (out, a, b) = list(refs[:n_in]), refs[n_in:]
-    half_steps = pl.num_programs(0) // 2
+def gather_ring(pair, ring):
+    after, before = shift(pair, ring, 1), shift(pair, ring, -1)
+    low = shift(after[:HALF_ROWS], ring, 1)
+    high = shift(before[HALF_ROWS:], ring, -1)
+    return [(pair, 0, (0, 1)), (after, 1, (0, 1)), (before, -1, (0, 1)), (low, 2, (0,)), (high, 2, (1,))]
+
+
+def exchange_cores(rows, cols):
+    arrived = lax.optimization_barrier((*rows[1:3], *cols[1:3]))[:2]
+    last = lax.optimization_barrier((*rows[3:], *cols[3:]))[:2]
+    return [shift(block, CORE, 1) for block in (rows[0], *arrived, *last)]
+
+
+def product_kernel(meta, *refs):
+    rows, cols, (out, a, b) = refs[:16], refs[16:24], refs[24:]
 
     def put_row(block, offset):
         a[:, pl.ds(offset, CB), 0:NW] = block[:, 0:CB, :]
@@ -175,17 +185,9 @@
         b[:, pl.ds(128 + offset, CB), 0:NW] = -im
         b[:, pl.ds(128 + offset, CB), NW : 2 * NW] = re
 
-    position = 0
-    for put, parts in ((put_row, row_parts), (put_col, col_parts)):
-        for count in parts:
-            offset = pl.multiple_of(meta[position] * CB, CB)
-            position += 1
-            if count == 1:
-                put(inputs.pop(0), offset)
-            else:
-                low, high = inputs.pop(0), inputs.pop(0)
-                pl.when(step < half_steps)(functools.partial(put, low, offset))
-                pl.when(step >= half_steps)(functools.partial(put, high, offset))
+    for index, block in enumerate(rows + cols):
+        put = put_row if index < len(rows) else put_col
+        put(block, pl.multiple_of(meta[index] * CB, CB))
     factor = 1.0 / math.sqrt(NW)
     for k in range(KC):
         o = lax.dot_general(
@@ -195,26 +197,16 @@
         out[1, k] = o[:, 128:] * factor
 
 
-def product(meta, rows, cols):
+def product(meta, blocks):
     steps = F // KC
     arrays, specs = [], []
-    for group in rows + cols:
-        for index, array in enumerate(group):
-            array = array.reshape(-1, 2 * CB, NW)
-            if len(group) == 1:
-                index_map = lambda i, m: (i, 0, 0)
-            elif index == 0:
-                index_map = lambda i, m: (jnp.minimum(i, steps // 2 - 1), 0, 0)
-            else:
-                index_map = lambda i, m: (jnp.maximum(i - steps // 2, 0), 0, 0)
-            arrays.append(array)
+    for block in blocks:
+        for half in range(block.shape[0] // HALF_ROWS):
+            arrays.append(block.reshape(-1, 2 * CB, NW))
+            index_map = lambda i, m, half=half: (i + half * steps, 0, 0)
             specs.append(pl.BlockSpec((KC, 2 * CB, NW), index_map))
     return pl.pallas_call(
-        functools.partial(
-            product_kernel,
-            row_parts=[len(g) for g in rows],
-            col_parts=[len(g) for g in cols],
-        ),
+        product_kernel,
         grid_spec=pltpu.PrefetchScalarGridSpec(
             num_scalar_prefetch=1,
             grid=(steps,),
@@ -233,23 +225,22 @@
     wid = (src * 16 + rcv).astype(jnp.int32).reshape(1)
     spectra = whiten(raw, quality.reshape(16, 128), channel_order, slab_order, wid)
     received = lax.all_to_all(
-        spectra.reshape(NW, CB, 2 * F), AXES, split_axis=0, concat_axis=0, tiled=True
+        spectra.reshape(NW, SENT, 2 * F), AXES, split_axis=0, concat_axis=0, tiled=True
     )
-    mine = turn(received.reshape(NW * CB, 2 * F))
+    row_pair, col_pair = turn(received.reshape(NW * SENT, 2 * F))
 
     y, xl = src // 2, src % 2
     z, xh, core = rcv // 4, rcv // 2 % 2, rcv % 2
-    rows, cols, meta = [], [], []
-    for ring, flip, *blocks in gather_ring(mine, Z, XH):
-        at = (z - ring) % 4 * 4 + (xh + flip) % 2 * 2
-        rows.append(blocks)
-        meta.append(at + core)
-        rows.append([shift(block, CORE, 1) for block in blocks])
-        meta.append(at + 1 - core)
-    for ring, flip, *blocks in gather_ring(mine, Y, XL):
-        cols.append(blocks)
-        meta.append((y - ring) % 4 * 2 + (xl + flip) % 2)
-    return product(jnp.stack(meta).astype(jnp.int32), rows, cols)
+    rows, cols = gather_ring(row_pair, Z), gather_ring(col_pair, Y)
+    others = exchange_cores([r[0] for r in rows], [c[0] for c in cols])
+    meta = []
+    for which in (core, 1 - core):
+        for _, ring, flips in rows:
+            meta += [(z - ring) % 4 * 4 + (xh + flip) % 2 * 2 + which for flip in flips]
+    for _, ring, flips in cols:
+        meta += [(y - ring) % 4 * 2 + (xl + flip) % 2 for flip in flips]
+    blocks = [block for block, _, _ in rows] + others + [block for block, _, _ in cols]
+    return product(jnp.stack(meta).astype(jnp.int32), blocks)
 
 
 def solution(mesh):

time: 126 us -> 120 us (0.952)
  starting transfers between devices: 35.3 us -> 14 us
  blocking collectives: 25.1 us -> 36.3 us
  Pallas kernels: 29 us -> 31.6 us
  local copies, waits for them, and re-layouts: 3.52 us -> 5.05 us
    ppermute x28 -> x13, starting transfers between devices: 35.3 us -> 14 us  [shift(): lax.ppermute(x, AXES, [(int(a), int(b)) for a, b in zip(ids.ravel(), to.r...]
    all_to_all x1, blocking collectives: 25.1 us -> 36.3 us  [body(): lax.all_to_all(spectra.reshape(NW, SENT, 2 * F), AXES, split_axis=0, conc...]
    unnamed x38 -> x16, local copies, waits for them, and re-layouts: 0.07 us -> 2.2 us
    pallas_call x1, Pallas kernels: 0.99 us -> 2.97 us  [turn(): pl.pallas_call(turn_kernel, in_specs=[pl.BlockSpec(memory_space=pltpu.VME...]
    slice x8 -> x4, local copies, waits for them, and re-layouts: 2.8 us -> 2.22 us  [the longest x2 1.11 us: gather_ring(): high = shift(before[HALF_ROWS:], ring, -1)]
    ppermute x28 -> x13, waiting for transfers between devices: 31.4 us -> 31.8 us  [shift(): lax.ppermute(x, AXES, [(int(a), int(b)) for a, b in zip(ids.ravel(), to.r...]
  transfers between devices with their start and end apart: 28 -> 13, of which waited for: 9 -> 6; matrix products, arithmetic and copies ran while one was open for 3% -> 2% of each run, Pallas kernels for 0% -> 0%
where the time goes in v3:
time: 120 us; the launch traced here: 119 us
  blocking collectives  36.3 us (30%)
  waiting for transfers between devices  31.8 us (26%)
  Pallas kernels  31.6 us (26%)
  starting transfers between devices  14 us (12%)
  local copies, waits for them, and re-layouts  5.05 us (4%)
    all_to_all x1, blocking collectives, body(): lax.all_to_all(spectra.reshape(NW, SENT, 2 * F), AXES, split_axis=0, conc...  36.3 us
    ppermute x13, waiting for transfers between devices, shift(): lax.ppermute(x, AXES, [(int(a), int(b)) for a, b in zip(ids.ravel(), to.r...  31.8 us
    pallas_call x1, Pallas kernels, product(): pl.pallas_call(product_kernel, grid_spec=pltpu.PrefetchScalarGridSpec(num...  15.7 us
    ppermute x13, starting transfers between devices, shift(): lax.ppermute(x, AXES, [(int(a), int(b)) for a, b in zip(ids.ravel(), to.r...  14 us
    pallas_call x1, Pallas kernels, whiten(): pl.pallas_call(whiten_kernel, grid_spec=pltpu.PrefetchScalarGridSpec(num_...  12.9 us
    pallas_call x1, Pallas kernels, turn(): pl.pallas_call(turn_kernel, in_specs=[pl.BlockSpec(memory_space=pltpu.VME...  2.97 us
  transfers between devices with their start and end apart: 13, of which 6 were waited for; matrix products, arithmetic and copies ran while one was open for 2% of the time, Pallas kernels for 0%

profile of v3, /device:TPU:1, one launch (start us, length us, event | category | flops | bytes accessed | tf_op | source)
XLA Modules:
  0.0 118.9 jit_solution(16018605694464816295)
XLA Ops:
  0.0 12.9 %whiten.1 = bf16[6144,128]{1,0:T(8,128)(2,1)} custom-call(s32[2048]{0:T(1024)} %order.1, s32[4]{0:T(128)} %slab.1, s32[1]{0:T(128)} %bitcast.24.wid, bf16[1,2048,512]{2,1,0:T(8,128)(2,1)} %raw.1, s32[16,128]{1,0:T(8,128)} %bitcast.59, bf16[512,128]{1,0:T(8,128)(2,1)} %constant.195.clone.dft), custom_call_target="tpu_custom_call" | custom-call | tf_op jit(solution)/shard_map/whiten/pallas_call | solution.py:103
  12.9 36.3 %all_to_all.5 = bf16[128,48,128]{2,1,0:T(8,128)(2,1)S(1)} all-to-all(bf16[128,48,128]{2,1,0:T(8,128)(2,1)} %bitcast.52), channel_id=1, replica_groups=mesh['src'=8,'rcv'=16] {'src','rcv'}, dimensions={0} | all-to-all | bytes 3145728 | tf_op jit(solution)/shard_map/all_to_all | solution.py:227
  49.2 3.0 %turn.1 = (bf16[4096,128]{1,0:T(8,128)(2,1)S(1)}, bf16[4096,128]{1,0:T(8,128)(2,1)S(1)}) custom-call(bf16[6144,128]{1,0:T(8,128)(2,1)S(1)} %bitcast.43), custom_call_target="tpu_custom_call" | custom-call | tf_op jit(solution)/shard_map/turn/pallas_call | solution.py:144
  52.2 0.6 collective-permute-start.6
  52.8 1.0 collective-permute-start.5
  53.8 0.6 collective-permute-start.1
  54.4 0.8 collective-permute-start
  55.2 21.4 %collective-permute-done.6 = bf16[4096,128]{1,0:T(8,128)(2,1)S(1)} collective-permute-done((bf16[4096,128]{1,0:T(8,128)(2,1)S(1)}, bf16[4096,128]{1,0:T(8,128)(2,1)S(1)}, u32[]{:S(2)}, u32[]{:S(2)}) %collective-permute-start.6) | collective-permute-done | bytes 1048608 | tf_op jit(solution)/shard_map/ppermute | solution.py:158
  76.7 1.4 %collective-permute-start.10 = (bf16[2048,128]{1,0:T(8,128)(2,1)S(1)}, bf16[2048,128]{1,0:T(8,128)(2,1)S(1)}, u32[]{:S(2)}, u32[]{:S(2)}) collective-permute-start(bf16[2048,128]{1,0:T(8,128)(2,1)S(1)} %slice.19), channel_id=1, source_target_pairs={{0,96},{1,97},{2,98},{3,99},{4,100},{5,101},{6,102},{7,103},{8,104... | collective-permute-start | bytes 1572872 | tf_op jit(solution)/shard_map/ppermute | solution.py:158
  78.1 0.0 collective-permute-done.5
  78.1 0.2 collective-permute-start.9
  78.3 1.8 %collective-permute-start.4 = (bf16[4096,128]{1,0:T(8,128)(2,1)S(1)}, bf16[4096,128]{1,0:T(8,128)(2,1)}, u32[]{:S(2)}, u32[]{:S(2)}) collective-permute-start(bf16[4096,128]{1,0:T(8,128)(2,1)S(1)} %get-tuple-element.11), channel_id=1, source_target_pairs={{0,1},{1,0},{2,3},{3,2},{4,5},{5,4},{6,7},{7,6},{8,9},{9,8},{10,11... | collective-permute-start | bytes 3145736 | tf_op jit(solution)/shard_map/ppermute | solution.py:158
  80.2 1.1 slice.17
  81.3 1.0 collective-permute-start.3
  82.3 1.1 slice.16
  83.4 0.6 collective-permute-start.2
  84.0 5.1 %collective-permute-done.10 = bf16[2048,128]{1,0:T(8,128)(2,1)S(1)} collective-permute-done((bf16[2048,128]{1,0:T(8,128)(2,1)S(1)}, bf16[2048,128]{1,0:T(8,128)(2,1)S(1)}, u32[]{:S(2)}, u32[]{:S(2)}) %collective-permute-start.10) | collective-permute-done | bytes 524320 | tf_op jit(solution)/shard_map/ppermute | solution.py:158
  89.1 2.0 %collective-permute-start.7 = (bf16[4096,128]{1,0:T(8,128)(2,1)}, bf16[4096,128]{1,0:T(8,128)(2,1)S(1)}, u32[]{:S(2)}, u32[]{:S(2)}) collective-permute-start(bf16[4096,128]{1,0:T(8,128)(2,1)} %collective-permute-done), channel_id=1, source_target_pairs={{0,1},{1,0},{2,3},{3,2},{4,5},{5,4},{6,7},{7,6},{8,9},{9,8},{10,11... | collective-permute-start | bytes 3145736 | tf_op jit(solution)/shard_map/ppermute | solution.py:158
  91.1 0.8 copy-done.7
  91.9 2.6 %collective-permute-start.8 = (bf16[4096,128]{1,0:T(8,128)(2,1)}, bf16[4096,128]{1,0:T(8,128)(2,1)S(1)}, u32[]{:S(2)}, u32[]{:S(2)}) collective-permute-start(bf16[4096,128]{1,0:T(8,128)(2,1)} %collective-permute-done.1), channel_id=1, source_target_pairs={{0,1},{1,0},{2,3},{3,2},{4,5},{5,4},{6,7},{7,6},{8,9},{9,8},{10,11... | collective-permute-start | bytes 3145736 | tf_op jit(solution)/shard_map/ppermute | solution.py:158
  94.5 0.3 collective-permute-done.3
  94.8 3.0 %collective-permute-done.2 = bf16[2048,128]{1,0:T(8,128)(2,1)} collective-permute-done((bf16[2048,128]{1,0:T(8,128)(2,1)S(1)}, bf16[2048,128]{1,0:T(8,128)(2,1)}, u32[]{:S(2)}, u32[]{:S(2)}) %collective-permute-start.2) | collective-permute-done | bytes 524320 | tf_op jit(solution)/shard_map/ppermute | solution.py:158
  97.8 1.3 %collective-permute-start.11 = (bf16[2048,128]{1,0:T(8,128)(2,1)}, bf16[2048,128]{1,0:T(8,128)(2,1)}, u32[]{:S(2)}, u32[]{:S(2)}) collective-permute-start(bf16[2048,128]{1,0:T(8,128)(2,1)} %collective-permute-done.2), channel_id=1, source_target_pairs={{0,1},{1,0},{2,3},{3,2},{4,5},{5,4},{6,7},{7,6},{8,9},{9,8},{10,11... | collective-permute-start | bytes 1572872 | tf_op jit(solution)/shard_map/ppermute | solution.py:158
  99.1 0.0 collective-permute-start.12
  99.1 0.6 stack.99.meta
  99.8 0.0 collective-permute-done.4
  99.8 1.2 %collective-permute-done.11 = bf16[2048,128]{1,0:T(8,128)(2,1)} collective-permute-done((bf16[2048,128]{1,0:T(8,128)(2,1)}, bf16[2048,128]{1,0:T(8,128)(2,1)}, u32[]{:S(2)}, u32[]{:S(2)}) %collective-permute-start.11) | collective-permute-done | bytes 524320 | tf_op jit(solution)/shard_map/ppermute | solution.py:158
  101.0 0.7 collective-permute-done.12
  101.8 0.0 collective-permute-done.7
  101.8 1.0 copy-done.4
  102.8 0.4 copy-done.5
  103.2 15.7 %product.1 = f32[2,64,256,128]{3,2,1,0:T(8,128)} custom-call(s32[24]{0:T(128)} %stack.99.meta, bf16[128,32,128]{2,1,0:T(8,128)(2,1)} %bitcast.44, bf16[128,32,128]{2,1,0:T(8,128)(2,1)} %bitcast.45, bf16[128,32,128]{2,1,0:T(8,128)(2,1)} %bitcast.29.refs_2_.refs_3_, bf16[128,32,128]{2,1,0:T(8,128)(2,1)} %bitcast.29.refs_2_.refs_3_, ...), custom_call_target="tpu_custom_call" | custom-call | tf_op jit(solution)/shard_map/product/pallas_call | solution.py:208
  (19 shorter events, 0.1 us)
Async XLA Ops:
  52.2 31.2 %copy-start = (bf16[4096,128]{1,0:T(8,128)(2,1)}, bf16[4096,128]{1,0:T(8,128)(2,1)S(1)}, u32[]{:S(2)}) copy-start(bf16[4096,128]{1,0:T(8,128)(2,1)S(1)} %get-tuple-element.11) | copy-start | bytes 3145732
  52.2 31.2 %copy-start.1 = (bf16[4096,128]{1,0:T(8,128)(2,1)}, bf16[4096,128]{1,0:T(8,128)(2,1)S(1)}, u32[]{:S(2)}) copy-start(bf16[4096,128]{1,0:T(8,128)(2,1)S(1)} %get-tuple-element.12) | copy-start | bytes 3145732
  52.2 24.4 %collective-permute-start.6 = (bf16[4096,128]{1,0:T(8,128)(2,1)S(1)}, bf16[4096,128]{1,0:T(8,128)(2,1)S(1)}, u32[]{:S(2)}, u32[]{:S(2)}) collective-permute-start(bf16[4096,128]{1,0:T(8,128)(2,1)S(1)} %get-tuple-element.12), channel_id=1, source_target_pairs={{0,96},{1,97},{2,98},{3,99},{4,100},{5,101},{6,102},{7,103},{8,104... | collective-permute-start | bytes 3145736 | tf_op jit(solution)/shard_map/ppermute | solution.py:158
  52.8 25.3 %collective-permute-start.5 = (bf16[4096,128]{1,0:T(8,128)(2,1)S(1)}, bf16[4096,128]{1,0:T(8,128)(2,1)S(1)}, u32[]{:S(2)}, u32[]{:S(2)}) collective-permute-start(bf16[4096,128]{1,0:T(8,128)(2,1)S(1)} %get-tuple-element.12), channel_id=1, source_target_pairs={{0,32},{1,33},{2,34},{3,35},{4,36},{5,37},{6,38},{7,39},{8,40},{9,... | collective-permute-start | bytes 3145736 | tf_op jit(solution)/shard_map/ppermute | solution.py:158
  53.8 26.4 %collective-permute-start.1 = (bf16[4096,128]{1,0:T(8,128)(2,1)S(1)}, bf16[4096,128]{1,0:T(8,128)(2,1)}, u32[]{:S(2)}, u32[]{:S(2)}) collective-permute-start(bf16[4096,128]{1,0:T(8,128)(2,1)S(1)} %get-tuple-element.11), channel_id=1, source_target_pairs={{0,12},{1,13},{2,14},{3,15},{4,0},{5,1},{6,2},{7,3},{8,4},{9,5},{1... | collective-permute-start | bytes 3145736 | tf_op jit(solution)/shard_map/ppermute | solution.py:158
  54.4 27.9 %collective-permute-start = (bf16[4096,128]{1,0:T(8,128)(2,1)S(1)}, bf16[4096,128]{1,0:T(8,128)(2,1)}, u32[]{:S(2)}, u32[]{:S(2)}) collective-permute-start(bf16[4096,128]{1,0:T(8,128)(2,1)S(1)} %get-tuple-element.11), channel_id=1, source_target_pairs={{0,4},{1,5},{2,6},{3,7},{4,8},{5,9},{6,10},{7,11},{8,12},{9,13},{1... | collective-permute-start | bytes 3145736 | tf_op jit(solution)/shard_map/ppermute | solution.py:158
  76.7 6.7 %copy-start.2 = (bf16[4096,128]{1,0:T(8,128)(2,1)}, bf16[4096,128]{1,0:T(8,128)(2,1)S(1)}, u32[]{:S(2)}) copy-start(bf16[4096,128]{1,0:T(8,128)(2,1)S(1)} %collective-permute-done.6) | copy-start | bytes 3145732
  76.7 12.4 %collective-permute-start.10 = (bf16[2048,128]{1,0:T(8,128)(2,1)S(1)}, bf16[2048,128]{1,0:T(8,128)(2,1)S(1)}, u32[]{:S(2)}, u32[]{:S(2)}) collective-permute-start(bf16[2048,128]{1,0:T(8,128)(2,1)S(1)} %slice.19), channel_id=1, source_target_pairs={{0,96},{1,97},{2,98},{3,99},{4,100},{5,101},{6,102},{7,103},{8,104... | collective-permute-start | bytes 1572872 | tf_op jit(solution)/shard_map/ppermute | solution.py:158
  78.1 5.9 %copy-start.3 = (bf16[4096,128]{1,0:T(8,128)(2,1)}, bf16[4096,128]{1,0:T(8,128)(2,1)S(1)}, u32[]{:S(2)}) copy-start(bf16[4096,128]{1,0:T(8,128)(2,1)S(1)} %collective-permute-done.5) | copy-start | bytes 3145732
  78.1 13.0 %collective-permute-start.9 = (bf16[2048,128]{1,0:T(8,128)(2,1)S(1)}, bf16[2048,128]{1,0:T(8,128)(2,1)S(1)}, u32[]{:S(2)}, u32[]{:S(2)}) collective-permute-start(bf16[2048,128]{1,0:T(8,128)(2,1)S(1)} %slice.18), channel_id=1, source_target_pairs={{0,32},{1,33},{2,34},{3,35},{4,36},{5,37},{6,38},{7,39},{8,40},{9,... | collective-permute-start | bytes 1572872 | tf_op jit(solution)/shard_map/ppermute | solution.py:158
  78.3 21.4 %collective-permute-start.4 = (bf16[4096,128]{1,0:T(8,128)(2,1)S(1)}, bf16[4096,128]{1,0:T(8,128)(2,1)}, u32[]{:S(2)}, u32[]{:S(2)}) collective-permute-start(bf16[4096,128]{1,0:T(8,128)(2,1)S(1)} %get-tuple-element.11), channel_id=1, source_target_pairs={{0,1},{1,0},{2,3},{3,2},{4,5},{5,4},{6,7},{7,6},{8,9},{9,8},{10,11... | collective-permute-start | bytes 3145736 | tf_op jit(solution)/shard_map/ppermute | solution.py:158
  81.3 13.5 %collective-permute-start.3 = (bf16[2048,128]{1,0:T(8,128)(2,1)S(1)}, bf16[2048,128]{1,0:T(8,128)(2,1)}, u32[]{:S(2)}, u32[]{:S(2)}) collective-permute-start(bf16[2048,128]{1,0:T(8,128)(2,1)S(1)} %slice.17), channel_id=1, source_target_pairs={{0,12},{1,13},{2,14},{3,15},{4,0},{5,1},{6,2},{7,3},{8,4},{9,5},{1... | collective-permute-start | bytes 1572872 | tf_op jit(solution)/shard_map/ppermute | solution.py:158
  83.4 14.4 %collective-permute-start.2 = (bf16[2048,128]{1,0:T(8,128)(2,1)S(1)}, bf16[2048,128]{1,0:T(8,128)(2,1)}, u32[]{:S(2)}, u32[]{:S(2)}) collective-permute-start(bf16[2048,128]{1,0:T(8,128)(2,1)S(1)} %slice.16), channel_id=1, source_target_pairs={{0,4},{1,5},{2,6},{3,7},{4,8},{5,9},{6,10},{7,11},{8,12},{9,13},{1... | collective-permute-start | bytes 1572872 | tf_op jit(solution)/shard_map/ppermute | solution.py:158
  89.1 2.0 %copy-start.6 = (bf16[2048,128]{1,0:T(8,128)(2,1)}, bf16[2048,128]{1,0:T(8,128)(2,1)S(1)}, u32[]{:S(2)}) copy-start(bf16[2048,128]{1,0:T(8,128)(2,1)S(1)} %collective-permute-done.10) | copy-start | bytes 1572868
  89.1 12.7 %collective-permute-start.7 = (bf16[4096,128]{1,0:T(8,128)(2,1)}, bf16[4096,128]{1,0:T(8,128)(2,1)S(1)}, u32[]{:S(2)}, u32[]{:S(2)}) collective-permute-start(bf16[4096,128]{1,0:T(8,128)(2,1)} %collective-permute-done), channel_id=1, source_target_pairs={{0,1},{1,0},{2,3},{3,2},{4,5},{5,4},{6,7},{7,6},{8,9},{9,8},{10,11... | collective-permute-start | bytes 3145736 | tf_op jit(solution)/shard_map/ppermute | solution.py:158
  91.1 0.8 copy-start.7
  91.9 9.9 %collective-permute-start.8 = (bf16[4096,128]{1,0:T(8,128)(2,1)}, bf16[4096,128]{1,0:T(8,128)(2,1)S(1)}, u32[]{:S(2)}, u32[]{:S(2)}) collective-permute-start(bf16[4096,128]{1,0:T(8,128)(2,1)} %collective-permute-done.1), channel_id=1, source_target_pairs={{0,1},{1,0},{2,3},{3,2},{4,5},{5,4},{6,7},{7,6},{8,9},{9,8},{10,11... | collective-permute-start | bytes 3145736 | tf_op jit(solution)/shard_map/ppermute | solution.py:158
  97.8 3.2 %collective-permute-start.11 = (bf16[2048,128]{1,0:T(8,128)(2,1)}, bf16[2048,128]{1,0:T(8,128)(2,1)}, u32[]{:S(2)}, u32[]{:S(2)}) collective-permute-start(bf16[2048,128]{1,0:T(8,128)(2,1)} %collective-permute-done.2), channel_id=1, source_target_pairs={{0,1},{1,0},{2,3},{3,2},{4,5},{5,4},{6,7},{7,6},{8,9},{9,8},{10,11... | collective-permute-start | bytes 1572872 | tf_op jit(solution)/shard_map/ppermute | solution.py:158
  99.1 2.6 %collective-permute-start.12 = (bf16[2048,128]{1,0:T(8,128)(2,1)}, bf16[2048,128]{1,0:T(8,128)(2,1)}, u32[]{:S(2)}, u32[]{:S(2)}) collective-permute-start(bf16[2048,128]{1,0:T(8,128)(2,1)} %collective-permute-done.3), channel_id=1, source_target_pairs={{0,1},{1,0},{2,3},{3,2},{4,5},{5,4},{6,7},{7,6},{8,9},{9,8},{10,11... | collective-permute-start | bytes 1572872 | tf_op jit(solution)/shard_map/ppermute | solution.py:158
  101.8 1.1 copy-start.4
  101.8 1.4 %copy-start.5 = (bf16[4096,128]{1,0:T(8,128)(2,1)}, bf16[4096,128]{1,0:T(8,128)(2,1)S(1)}, u32[]{:S(2)}) copy-start(bf16[4096,128]{1,0:T(8,128)(2,1)S(1)} %collective-permute-done.8) | copy-start | bytes 3145732

commit v4 on v3

--- a/solution.py
+++ b/solution.py
@@ -15,8 +15,8 @@
 GRID = (4, 2, 4, 2, 2)
 Y, XL, Z, XH, CORE = range(5)
 BF16, F32 = jnp.bfloat16, jnp.float32
-ROWS = 256
-KC = 8
+ROWS = 1024
+KC = 32
 XL_BIT, XH_BIT = 16, 2
 SENT = 3 * CB
 HALF_ROWS = F * 2 * CB
@@ -124,32 +124,44 @@
     )(order, slab, wid, raw, quality, dft_table())
 
 
-def turn_kernel(received, row_out, col_out, wide, turned):
-    wide[...] = received[...].astype(F32)
-    for slot in range(3):
-        for p in range(CB):
-            t = wide[pl.ds(slot * CB + p, NW, stride=SENT), :].T
-            turned[pl.ds(p, F, stride=2 * CB), :] = t[:F]
-            turned[pl.ds(CB + p, F, stride=2 * CB), :] = t[F:]
-        block = turned[...].astype(BF16)
-        if slot == 0:
-            row_out[0:HALF_ROWS, :] = block
-            col_out[0:HALF_ROWS, :] = block
-        else:
-            (row_out if slot == 1 else col_out)[HALF_ROWS:, :] = block
-
-
-def turn(received):
-    shape = jax.ShapeDtypeStruct((2 * HALF_ROWS, NW), BF16)
+def turn_block(wide, first, step, turned):
+    for p in range(CB):
+        t = wide[pl.ds(first + p, NW, stride=step), :].T
+        turned[pl.ds(p, F, stride=2 * CB), :] = t[:F]
+        turned[pl.ds(CB + p, F, stride=2 * CB), :] = t[F:]
+    return turned[...].astype(BF16)
+
+
+def turn_two_kernel(received, out, wide, turned):
+    wide[...] = received[...].astype(F32).reshape(wide.shape)
+    for slot in range(2):
+        block = turn_block(wide, slot * CB, 2 * CB, turned)
+        out[pl.ds(slot * HALF_ROWS, HALF_ROWS), :] = block
+
+
+def turn_one_kernel(received, own, out, wide, turned):
+    wide[...] = received[...].astype(F32).reshape(wide.shape)
+    out[0:HALF_ROWS, :] = own[...]
+    out[HALF_ROWS:, :] = turn_block(wide, 0, CB, turned)
+
+
+def turn_call(kernel, received, slots, first, *own):
     return pl.pallas_call(
-        turn_kernel,
-        in_specs=[pl.BlockSpec(memory_space=pltpu.VMEM)],
-        out_specs=[pl.BlockSpec(memory_space=pltpu.VMEM)] * 2,
-        out_shape=[shape, shape],
-        scratch_shapes=[pltpu.VMEM((NW * SENT, 2 * F), F32), pltpu.VMEM((HALF_ROWS, NW), F32)],
+        kernel,
+        grid=(1,),
+        in_specs=[
+            pl.BlockSpec((NW, slots * CB, 2 * F), lambda i: (0, first, 0)),
+            *[pl.BlockSpec((HALF_ROWS, NW), lambda i: (0, 0)) for _ in own],
+        ],
+        out_specs=pl.BlockSpec((2 * HALF_ROWS, NW), lambda i: (0, 0)),
+        out_shape=jax.ShapeDtypeStruct((2 * HALF_ROWS, NW), BF16),
+        scratch_shapes=[
+            pltpu.VMEM((NW * slots * CB, 2 * F), F32),
+            pltpu.VMEM((HALF_ROWS, NW), F32),
+        ],
         compiler_params=pltpu.CompilerParams(vmem_limit_bytes=24 << 20),
         name="turn",
-    )(received)
+    )(received, *own)
 
 
 def shift(x, axis, amount):
@@ -158,46 +170,61 @@
     return lax.ppermute(x, AXES, [(int(a), int(b)) for a, b in zip(ids.ravel(), to.ravel())])
 
 
-def gather_ring(pair, ring):
-    after, before = shift(pair, ring, 1), shift(pair, ring, -1)
-    low = shift(after[:HALF_ROWS], ring, 1)
-    high = shift(before[HALF_ROWS:], ring, -1)
-    return [(pair, 0, (0, 1)), (after, 1, (0, 1)), (before, -1, (0, 1)), (low, 2, (0,)), (high, 2, (1,))]
-
-
-def exchange_cores(rows, cols):
-    arrived = lax.optimization_barrier((*rows[1:3], *cols[1:3]))[:2]
-    last = lax.optimization_barrier((*rows[3:], *cols[3:]))[:2]
-    return [shift(block, CORE, 1) for block in (rows[0], *arrived, *last)]
-
-
-def product_kernel(meta, *refs):
-    rows, cols, (out, a, b) = refs[:16], refs[16:24], refs[24:]
-
-    def put_row(block, offset):
-        a[:, pl.ds(offset, CB), 0:NW] = block[:, 0:CB, :]
-        a[:, pl.ds(offset, CB), NW : 2 * NW] = block[:, CB : 2 * CB, :]
-
-    def put_col(block, offset):
+def gather_rings(row_pair, col_pair):
+    rows = [row_pair, shift(row_pair, Z, 1), shift(row_pair, Z, -1)]
+    cols = [col_pair, shift(col_pair, Y, 1), shift(col_pair, Y, -1)]
+    others = [shift(row_pair, CORE, 1)]
+    halves = (rows[1][:HALF_ROWS], rows[2][HALF_ROWS:])
+    halves = lax.optimization_barrier((*halves, *others))[:2]
+    for ring, halves in ((Z, halves), (Y, (cols[1][:HALF_ROWS], cols[2][HALF_ROWS:]))):
+        far = [shift(half, ring, way) for half, way in zip(halves, (1, -1))]
+        (rows if ring == Z else cols).extend(far)
+    after = lax.optimization_barrier((*rows[1:3], *cols[1:3]))[0]
+    others.append(shift(after, CORE, 1))
+    before, _ = lax.optimization_barrier((rows[2], others[1]))
+    others.append(shift(before, CORE, 1))
+    far = lax.optimization_barrier((*rows[3:], *cols[3:]))[:2]
+    others += [shift(block, CORE, 1) for block in far]
+    return rows, others, cols
+
+
+def block_offsets(wid):
+    bits = lambda low, size: (wid >> low) & (size - 1)
+    y, xl, z, xh, core = bits(5, 4), bits(4, 2), bits(2, 4), bits(1, 2), bits(0, 2)
+    held = [(0, 0), (0, 1), (1, 0), (1, 1), (3, 0), (3, 1), (2, 0), (2, 1)]
+    rows = [((z - ring) & 3) * 4 + (xh ^ flip) * 2 for ring, flip in held]
+    cols = [((y - ring) & 3) * 2 + (xl ^ flip) for ring, flip in held]
+    return [at * CB for at in [r + core for r in rows] + [r + 1 - core for r in rows] + cols]
+
+
+def product_kernel(wid, *refs):
+    rows, cols, (out, b) = refs[:16], refs[16:24], refs[24:]
+    offsets = [pl.multiple_of(at, CB) for at in block_offsets(wid[0])]
+    for block, offset in zip(cols, offsets[16:]):
         re, im = block[:, 0:CB, :], block[:, CB : 2 * CB, :]
         b[:, pl.ds(offset, CB), 0:NW] = re
         b[:, pl.ds(offset, CB), NW : 2 * NW] = im
         b[:, pl.ds(128 + offset, CB), 0:NW] = -im
         b[:, pl.ds(128 + offset, CB), NW : 2 * NW] = re
-
-    for index, block in enumerate(rows + cols):
-        put = put_row if index < len(rows) else put_col
-        put(block, pl.multiple_of(meta[index] * CB, CB))
     factor = 1.0 / math.sqrt(NW)
     for k in range(KC):
+        halves = [
+            jnp.concatenate([row[k, 0:CB, :], row[k, CB : 2 * CB, :]], axis=1) for row in rows
+        ]
         o = lax.dot_general(
-            a[k], b[k], (((1,), (1,)), ((), ())), preferred_element_type=F32
+            jnp.concatenate(halves, axis=0),
+            b[k],
+            (((1,), (1,)), ((), ())),
+            preferred_element_type=F32,
         )
-        out[0, k] = o[:, :128] * factor
-        out[1, k] = o[:, 128:] * factor
-
-
-def product(meta, blocks):
+        o = o * factor
+        for index, offset in enumerate(offsets[:16]):
+            part = o[index * CB : (index + 1) * CB]
+            out[0, k, pl.ds(offset, CB), :] = part[:, :128]
+            out[1, k, pl.ds(offset, CB), :] = part[:, 128:]
+
+
+def product(wid, blocks):
     steps = F // KC
     arrays, specs = [], []
     for block in blocks:
@@ -212,12 +239,12 @@
             grid=(steps,),
             in_specs=specs,
             out_specs=pl.BlockSpec((2, KC, 256, 128), lambda i, m: (0, i, 0, 0)),
-            scratch_shapes=[pltpu.VMEM((KC, 256, 256), BF16), pltpu.VMEM((KC, 256, 256), BF16)],
+            scratch_shapes=[pltpu.VMEM((KC, 256, 256), BF16)],
         ),
         out_shape=jax.ShapeDtypeStruct((2, F, 256, 128), F32),
         compiler_params=pltpu.CompilerParams(vmem_limit_bytes=58 << 20),
         name="product",
-    )(meta, *arrays)
+    )(wid, *arrays)
 
 
 def body(raw, quality, channel_order, slab_order):
@@ -227,20 +254,10 @@
     received = lax.all_to_all(
         spectra.reshape(NW, SENT, 2 * F), AXES, split_axis=0, concat_axis=0, tiled=True
     )
-    row_pair, col_pair = turn(received.reshape(NW * SENT, 2 * F))
-
-    y, xl = src // 2, src % 2
-    z, xh, core = rcv // 4, rcv // 2 % 2, rcv % 2
-    rows, cols = gather_ring(row_pair, Z), gather_ring(col_pair, Y)
-    others = exchange_cores([r[0] for r in rows], [c[0] for c in cols])
-    meta = []
-    for which in (core, 1 - core):
-        for _, ring, flips in rows:
-            meta += [(z - ring) % 4 * 4 + (xh + flip) % 2 * 2 + which for flip in flips]
-    for _, ring, flips in cols:
-        meta += [(y - ring) % 4 * 2 + (xl + flip) % 2 for flip in flips]
-    blocks = [block for block, _, _ in rows] + others + [block for block, _, _ in cols]
-    return product(jnp.stack(meta).astype(jnp.int32), blocks)
+    row_pair = turn_call(turn_two_kernel, received, 2, 0)
+    col_pair = turn_call(turn_one_kernel, received, 1, 2, row_pair)
+    rows, others, cols = gather_rings(row_pair, col_pair)
+    return product(wid, rows + others + cols)
 
 
 def solution(mesh):

time: 120 us -> 112 us (0.933)
  Pallas kernels: 31.6 us -> 24.4 us
  local copies, waits for them, and re-layouts: 5.05 us -> 1.24 us
  waiting for transfers between devices: 31.8 us -> 35.1 us
    pallas_call x1, Pallas kernels: 15.7 us -> 11.2 us  [product(): pl.pallas_call(product_kernel, grid_spec=pltpu.PrefetchScalarGridSpec(num...]
    pallas_call x1, Pallas kernels: 12.9 us -> 9.51 us  [whiten(): pl.pallas_call(whiten_kernel, grid_spec=pltpu.PrefetchScalarGridSpec(num_...]
    ppermute x13, waiting for transfers between devices: 31.8 us -> 35.1 us  [shift(): lax.ppermute(x, AXES, [(int(a), int(b)) for a, b in zip(ids.ravel(), to.r...]
    slice x4, local copies, waits for them, and re-layouts: 2.22 us -> 0.14 us  [the longest x2 0.07 us: gather_rings(): halves = (rows[1][:HALF_ROWS], rows[2][HALF_ROWS:])]
    pallas_call x1 -> x2, Pallas kernels: 2.97 us -> 3.66 us  [turn_call(): pl.pallas_call(kernel, grid=(1,), in_specs=[pl.BlockSpec((NW, slots * CB,...]
  transfers between devices with their start and end apart: 13 -> 13, of which waited for: 6 -> 8; matrix products, arithmetic and copies ran while one was open for 2% -> 0% of each run, Pallas kernels for 0% -> 0%
where the time goes in v4:
time: 112 us; the launch traced here: 111 us
  blocking collectives  36.3 us (32%)
  waiting for transfers between devices  35.1 us (31%)
  Pallas kernels  24.4 us (22%)
  starting transfers between devices  14 us (12%)
  local copies, waits for them, and re-layouts  1.24 us (1%)
    all_to_all x1, blocking collectives, body(): lax.all_to_all(spectra.reshape(NW, SENT, 2 * F), AXES, split_axis=0, conc...  36.3 us
    ppermute x13, waiting for transfers between devices, shift(): lax.ppermute(x, AXES, [(int(a), int(b)) for a, b in zip(ids.ravel(), to.r...  35.1 us
    ppermute x13, starting transfers between devices, shift(): lax.ppermute(x, AXES, [(int(a), int(b)) for a, b in zip(ids.ravel(), to.r...  14 us
    pallas_call x1, Pallas kernels, product(): pl.pallas_call(product_kernel, grid_spec=pltpu.PrefetchScalarGridSpec(num...  11.2 us
    pallas_call x1, Pallas kernels, whiten(): pl.pallas_call(whiten_kernel, grid_spec=pltpu.PrefetchScalarGridSpec(num_...  9.51 us
    pallas_call x2, Pallas kernels, turn_call(): pl.pallas_call(kernel, grid=(1,), in_specs=[pl.BlockSpec((NW, slots * CB,...  3.66 us
  transfers between devices with their start and end apart: 13, of which 8 were waited for; matrix products, arithmetic and copies ran while one was open for 0% of the time, Pallas kernels for 0%

profile of v4, /device:TPU:1, one launch (start us, length us, event | category | flops | bytes accessed | tf_op | source)
XLA Modules:
  0.0 111.3 jit_solution(9116199154502519384)
XLA Ops:
  0.0 9.5 %whiten.1 = bf16[6144,128]{1,0:T(8,128)(2,1)} custom-call(s32[2048]{0:T(1024)} %order.1, s32[4]{0:T(128)} %slab.1, s32[1]{0:T(128)} %bitcast.wid, bf16[1,2048,512]{2,1,0:T(8,128)(2,1)} %raw.1, s32[16,128]{1,0:T(8,128)} %bitcast.43, bf16[512,128]{1,0:T(8,128)(2,1)} %constant.13.clone.dft), custom_call_target="tpu_custom_call" | custom-call | tf_op jit(solution)/shard_map/whiten/pallas_call | solution.py:103
  9.5 36.3 %all_to_all.5.received = bf16[128,48,128]{2,1,0:T(8,128)(2,1)S(1)} all-to-all(bf16[128,48,128]{2,1,0:T(8,128)(2,1)} %bitcast.30), channel_id=1, replica_groups=mesh['src'=8,'rcv'=16] {'src','rcv'}, dimensions={0} | all-to-all | bytes 3145728 | tf_op jit(solution)/shard_map/all_to_all | solution.py:254
  45.8 2.6 %turn.2.own = bf16[4096,128]{1,0:T(8,128)(2,1)S(1)} custom-call(bf16[128,48,128]{2,1,0:T(8,128)(2,1)S(1)} %all_to_all.5.received), custom_call_target="tpu_custom_call" | custom-call | tf_op jit(solution)/shard_map/turn/pallas_call | solution.py:149
  48.4 1.1 turn.3
  49.5 0.6 collective-permute-start.6
  50.1 1.0 collective-permute-start.5
  51.0 0.6 collective-permute-start.1
  51.7 0.8 collective-permute-start
  52.5 1.6 %collective-permute-start.2 = (bf16[4096,128]{1,0:T(8,128)(2,1)S(1)}, bf16[4096,128]{1,0:T(8,128)(2,1)S(1)}, u32[]{:S(2)}, u32[]{:S(2)}) collective-permute-start(bf16[4096,128]{1,0:T(8,128)(2,1)S(1)} %turn.2.own), channel_id=1, source_target_pairs={{0,1},{1,0},{2,3},{3,2},{4,5},{5,4},{6,7},{7,6},{8,9},{9,8},{10,11... | collective-permute-start | bytes 3145736 | tf_op jit(solution)/shard_map/ppermute | solution.py:170
  54.1 19.7 %collective-permute-done.6 = bf16[4096,128]{1,0:T(8,128)(2,1)S(1)} collective-permute-done((bf16[4096,128]{1,0:T(8,128)(2,1)S(1)}, bf16[4096,128]{1,0:T(8,128)(2,1)S(1)}, u32[]{:S(2)}, u32[]{:S(2)}) %collective-permute-start.6) | collective-permute-done | bytes 1048608 | tf_op jit(solution)/shard_map/ppermute | solution.py:170
  73.8 1.0 collective-permute-done.5
  74.8 0.0 collective-permute-done.1
  74.8 1.5 %collective-permute-done = bf16[4096,128]{1,0:T(8,128)(2,1)S(1)} collective-permute-done((bf16[4096,128]{1,0:T(8,128)(2,1)S(1)}, bf16[4096,128]{1,0:T(8,128)(2,1)S(1)}, u32[]{:S(2)}, u32[]{:S(2)}) %collective-permute-start) | collective-permute-done | bytes 1048608 | tf_op jit(solution)/shard_map/ppermute | solution.py:170
  76.3 2.1 %collective-permute-start.7 = (bf16[4096,128]{1,0:T(8,128)(2,1)S(1)}, bf16[4096,128]{1,0:T(8,128)(2,1)S(1)}, u32[]{:S(2)}, u32[]{:S(2)}) collective-permute-start(bf16[4096,128]{1,0:T(8,128)(2,1)S(1)} %collective-permute-done), channel_id=1, source_target_pairs={{0,1},{1,0},{2,3},{3,2},{4,5},{5,4},{6,7},{7,6},{8,9},{9,8},{10,11... | collective-permute-start | bytes 3145736 | tf_op jit(solution)/shard_map/ppermute | solution.py:170
  78.5 2.1 %collective-permute-start.10 = (bf16[2048,128]{1,0:T(8,128)(2,1)S(1)}, bf16[2048,128]{1,0:T(8,128)(2,1)S(1)}, u32[]{:S(2)}, u32[]{:S(2)}) collective-permute-start(bf16[2048,128]{1,0:T(8,128)(2,1)S(1)} %slice.19), channel_id=1, source_target_pairs={{0,96},{1,97},{2,98},{3,99},{4,100},{5,101},{6,102},{7,103},{8,104... | collective-permute-start | bytes 1572872 | tf_op jit(solution)/shard_map/ppermute | solution.py:170
  80.6 0.1 collective-permute-start.9
  80.8 0.0 collective-permute-done.2
  80.9 0.1 collective-permute-start.3
  80.9 2.7 %collective-permute-start.4 = (bf16[2048,128]{1,0:T(8,128)(2,1)S(1)}, bf16[2048,128]{1,0:T(8,128)(2,1)S(1)}, u32[]{:S(2)}, u32[]{:S(2)}) collective-permute-start(bf16[2048,128]{1,0:T(8,128)(2,1)S(1)} %slice.17), channel_id=1, source_target_pairs={{0,12},{1,13},{2,14},{3,15},{4,0},{5,1},{6,2},{7,3},{8,4},{9,5},{1... | collective-permute-start | bytes 1572872 | tf_op jit(solution)/shard_map/ppermute | solution.py:170
  83.6 0.0 collective-permute-done.7
  83.6 0.9 collective-permute-start.8
  84.5 7.6 %collective-permute-done.10 = bf16[2048,128]{1,0:T(8,128)(2,1)S(1)} collective-permute-done((bf16[2048,128]{1,0:T(8,128)(2,1)S(1)}, bf16[2048,128]{1,0:T(8,128)(2,1)S(1)}, u32[]{:S(2)}, u32[]{:S(2)}) %collective-permute-start.10) | collective-permute-done | bytes 524320 | tf_op jit(solution)/shard_map/ppermute | solution.py:170
  92.1 3.0 %collective-permute-done.9 = bf16[2048,128]{1,0:T(8,128)(2,1)S(1)} collective-permute-done((bf16[2048,128]{1,0:T(8,128)(2,1)S(1)}, bf16[2048,128]{1,0:T(8,128)(2,1)S(1)}, u32[]{:S(2)}, u32[]{:S(2)}) %collective-permute-start.9) | collective-permute-done | bytes 524320 | tf_op jit(solution)/shard_map/ppermute | solution.py:170
  95.2 0.2 collective-permute-done.3
  95.4 1.2 %collective-permute-start.11 = (bf16[2048,128]{1,0:T(8,128)(2,1)S(1)}, bf16[2048,128]{1,0:T(8,128)(2,1)S(1)}, u32[]{:S(2)}, u32[]{:S(2)}) collective-permute-start(bf16[2048,128]{1,0:T(8,128)(2,1)S(1)} %collective-permute-done.3), channel_id=1, source_target_pairs={{0,1},{1,0},{2,3},{3,2},{4,5},{5,4},{6,7},{7,6},{8,9},{9,8},{10,11... | collective-permute-start | bytes 1572872 | tf_op jit(solution)/shard_map/ppermute | solution.py:170
  96.6 0.3 collective-permute-start.12
  96.8 1.3 %collective-permute-done.11 = bf16[2048,128]{1,0:T(8,128)(2,1)S(1)} collective-permute-done((bf16[2048,128]{1,0:T(8,128)(2,1)S(1)}, bf16[2048,128]{1,0:T(8,128)(2,1)S(1)}, u32[]{:S(2)}, u32[]{:S(2)}) %collective-permute-start.11) | collective-permute-done | bytes 524320 | tf_op jit(solution)/shard_map/ppermute | solution.py:170
  98.1 0.7 collective-permute-done.12
  98.9 0.0 collective-permute-done.8
  98.9 0.7 copy-done.14
  99.6 0.3 copy-done.8
  100.0 11.2 %product.1 = f32[2,64,256,128]{3,2,1,0:T(8,128)} custom-call(s32[1]{0:T(128)} %bitcast.wid, bf16[128,32,128]{2,1,0:T(8,128)(2,1)} %bitcast.18, bf16[128,32,128]{2,1,0:T(8,128)(2,1)} %bitcast.19, bf16[128,32,128]{2,1,0:T(8,128)(2,1)} %bitcast.28, bf16[128,32,128]{2,1,0:T(8,128)(2,1)} %bitcast.29, bf16[128,32,128]{2,1,0:T(8,128)(2,1)} %bitcast.26, ...), custom_call_target="tpu_custom_call" | custom-call | tf_op jit(solution)/shard_map/product/pallas_call | solution.py:235
  (33 shorter events, 0.2 us)
Async XLA Ops:
  48.4 30.1 %copy-start = (bf16[4096,128]{1,0:T(8,128)(2,1)}, bf16[4096,128]{1,0:T(8,128)(2,1)S(1)}, u32[]{:S(2)}) copy-start(bf16[4096,128]{1,0:T(8,128)(2,1)S(1)} %turn.2.own) | copy-start | bytes 3145732
  49.5 31.3 %copy-start.1 = (bf16[4096,128]{1,0:T(8,128)(2,1)}, bf16[4096,128]{1,0:T(8,128)(2,1)S(1)}, u32[]{:S(2)}) copy-start(bf16[4096,128]{1,0:T(8,128)(2,1)S(1)} %turn.3) | copy-start | bytes 3145732
  49.5 24.3 %collective-permute-start.6 = (bf16[4096,128]{1,0:T(8,128)(2,1)S(1)}, bf16[4096,128]{1,0:T(8,128)(2,1)S(1)}, u32[]{:S(2)}, u32[]{:S(2)}) collective-permute-start(bf16[4096,128]{1,0:T(8,128)(2,1)S(1)} %turn.3), channel_id=1, source_target_pairs={{0,96},{1,97},{2,98},{3,99},{4,100},{5,101},{6,102},{7,103},{8,104... | collective-permute-start | bytes 3145736 | tf_op jit(solution)/shard_map/ppermute | solution.py:170
  50.1 24.8 %collective-permute-start.5 = (bf16[4096,128]{1,0:T(8,128)(2,1)S(1)}, bf16[4096,128]{1,0:T(8,128)(2,1)S(1)}, u32[]{:S(2)}, u32[]{:S(2)}) collective-permute-start(bf16[4096,128]{1,0:T(8,128)(2,1)S(1)} %turn.3), channel_id=1, source_target_pairs={{0,32},{1,33},{2,34},{3,35},{4,36},{5,37},{6,38},{7,39},{8,40},{9,... | collective-permute-start | bytes 3145736 | tf_op jit(solution)/shard_map/ppermute | solution.py:170
  51.0 23.8 %collective-permute-start.1 = (bf16[4096,128]{1,0:T(8,128)(2,1)S(1)}, bf16[4096,128]{1,0:T(8,128)(2,1)S(1)}, u32[]{:S(2)}, u32[]{:S(2)}) collective-permute-start(bf16[4096,128]{1,0:T(8,128)(2,1)S(1)} %turn.2.own), channel_id=1, source_target_pairs={{0,12},{1,13},{2,14},{3,15},{4,0},{5,1},{6,2},{7,3},{8,4},{9,5},{1... | collective-permute-start | bytes 3145736 | tf_op jit(solution)/shard_map/ppermute | solution.py:170
  51.7 24.7 %collective-permute-start = (bf16[4096,128]{1,0:T(8,128)(2,1)S(1)}, bf16[4096,128]{1,0:T(8,128)(2,1)S(1)}, u32[]{:S(2)}, u32[]{:S(2)}) collective-permute-start(bf16[4096,128]{1,0:T(8,128)(2,1)S(1)} %turn.2.own), channel_id=1, source_target_pairs={{0,4},{1,5},{2,6},{3,7},{4,8},{5,9},{6,10},{7,11},{8,12},{9,13},{1... | collective-permute-start | bytes 3145736 | tf_op jit(solution)/shard_map/ppermute | solution.py:170
  52.5 28.4 %collective-permute-start.2 = (bf16[4096,128]{1,0:T(8,128)(2,1)S(1)}, bf16[4096,128]{1,0:T(8,128)(2,1)S(1)}, u32[]{:S(2)}, u32[]{:S(2)}) collective-permute-start(bf16[4096,128]{1,0:T(8,128)(2,1)S(1)} %turn.2.own), channel_id=1, source_target_pairs={{0,1},{1,0},{2,3},{3,2},{4,5},{5,4},{6,7},{7,6},{8,9},{9,8},{10,11... | collective-permute-start | bytes 3145736 | tf_op jit(solution)/shard_map/ppermute | solution.py:170
  73.8 7.0 %copy-start.2 = (bf16[4096,128]{1,0:T(8,128)(2,1)}, bf16[4096,128]{1,0:T(8,128)(2,1)S(1)}, u32[]{:S(2)}) copy-start(bf16[4096,128]{1,0:T(8,128)(2,1)S(1)} %collective-permute-done.6) | copy-start | bytes 3145732
  74.8 6.0 %copy-start.3 = (bf16[4096,128]{1,0:T(8,128)(2,1)}, bf16[4096,128]{1,0:T(8,128)(2,1)S(1)}, u32[]{:S(2)}) copy-start(bf16[4096,128]{1,0:T(8,128)(2,1)S(1)} %collective-permute-done.5) | copy-start | bytes 3145732
  74.8 8.8 %copy-start.4 = (bf16[4096,128]{1,0:T(8,128)(2,1)}, bf16[4096,128]{1,0:T(8,128)(2,1)S(1)}, u32[]{:S(2)}) copy-start(bf16[4096,128]{1,0:T(8,128)(2,1)S(1)} %collective-permute-done.1) | copy-start | bytes 3145732
  76.3 22.5 %copy-start.5 = (bf16[4096,128]{1,0:T(8,128)(2,1)}, bf16[4096,128]{1,0:T(8,128)(2,1)S(1)}, u32[]{:S(2)}) copy-start(bf16[4096,128]{1,0:T(8,128)(2,1)S(1)} %collective-permute-done) | copy-start | bytes 3145732
  76.3 7.3 %collective-permute-start.7 = (bf16[4096,128]{1,0:T(8,128)(2,1)S(1)}, bf16[4096,128]{1,0:T(8,128)(2,1)S(1)}, u32[]{:S(2)}, u32[]{:S(2)}) collective-permute-start(bf16[4096,128]{1,0:T(8,128)(2,1)S(1)} %collective-permute-done), channel_id=1, source_target_pairs={{0,1},{1,0},{2,3},{3,2},{4,5},{5,4},{6,7},{7,6},{8,9},{9,8},{10,11... | collective-permute-start | bytes 3145736 | tf_op jit(solution)/shard_map/ppermute | solution.py:170
  78.5 13.6 %collective-permute-start.10 = (bf16[2048,128]{1,0:T(8,128)(2,1)S(1)}, bf16[2048,128]{1,0:T(8,128)(2,1)S(1)}, u32[]{:S(2)}, u32[]{:S(2)}) collective-permute-start(bf16[2048,128]{1,0:T(8,128)(2,1)S(1)} %slice.19), channel_id=1, source_target_pairs={{0,96},{1,97},{2,98},{3,99},{4,100},{5,101},{6,102},{7,103},{8,104... | collective-permute-start | bytes 1572872 | tf_op jit(solution)/shard_map/ppermute | solution.py:170
  80.6 14.5 %collective-permute-start.9 = (bf16[2048,128]{1,0:T(8,128)(2,1)S(1)}, bf16[2048,128]{1,0:T(8,128)(2,1)S(1)}, u32[]{:S(2)}, u32[]{:S(2)}) collective-permute-start(bf16[2048,128]{1,0:T(8,128)(2,1)S(1)} %slice.18), channel_id=1, source_target_pairs={{0,32},{1,33},{2,34},{3,35},{4,36},{5,37},{6,38},{7,39},{8,40},{9,... | collective-permute-start | bytes 1572872 | tf_op jit(solution)/shard_map/ppermute | solution.py:170
  80.8 18.0 %copy-start.6 = (bf16[4096,128]{1,0:T(8,128)(2,1)}, bf16[4096,128]{1,0:T(8,128)(2,1)S(1)}, u32[]{:S(2)}) copy-start(bf16[4096,128]{1,0:T(8,128)(2,1)S(1)} %collective-permute-done.2) | copy-start | bytes 3145732
  80.9 14.5 %collective-permute-start.3 = (bf16[2048,128]{1,0:T(8,128)(2,1)S(1)}, bf16[2048,128]{1,0:T(8,128)(2,1)S(1)}, u32[]{:S(2)}, u32[]{:S(2)}) collective-permute-start(bf16[2048,128]{1,0:T(8,128)(2,1)S(1)} %slice.16), channel_id=1, source_target_pairs={{0,4},{1,5},{2,6},{3,7},{4,8},{5,9},{6,10},{7,11},{8,12},{9,13},{1... | collective-permute-start | bytes 1572872 | tf_op jit(solution)/shard_map/ppermute | solution.py:170
  80.9 14.4 %collective-permute-start.4 = (bf16[2048,128]{1,0:T(8,128)(2,1)S(1)}, bf16[2048,128]{1,0:T(8,128)(2,1)S(1)}, u32[]{:S(2)}, u32[]{:S(2)}) collective-permute-start(bf16[2048,128]{1,0:T(8,128)(2,1)S(1)} %slice.17), channel_id=1, source_target_pairs={{0,12},{1,13},{2,14},{3,15},{4,0},{5,1},{6,2},{7,3},{8,4},{9,5},{1... | collective-permute-start | bytes 1572872 | tf_op jit(solution)/shard_map/ppermute | solution.py:170
  83.6 15.3 %copy-start.7 = (bf16[4096,128]{1,0:T(8,128)(2,1)}, bf16[4096,128]{1,0:T(8,128)(2,1)S(1)}, u32[]{:S(2)}) copy-start(bf16[4096,128]{1,0:T(8,128)(2,1)S(1)} %collective-permute-done.7) | copy-start | bytes 3145732
  83.6 15.2 %collective-permute-start.8 = (bf16[4096,128]{1,0:T(8,128)(2,1)S(1)}, bf16[4096,128]{1,0:T(8,128)(2,1)S(1)}, u32[]{:S(2)}, u32[]{:S(2)}) collective-permute-start(bf16[4096,128]{1,0:T(8,128)(2,1)S(1)} %collective-permute-done.1), channel_id=1, source_target_pairs={{0,1},{1,0},{2,3},{3,2},{4,5},{5,4},{6,7},{7,6},{8,9},{9,8},{10,11... | collective-permute-start | bytes 3145736 | tf_op jit(solution)/shard_map/ppermute | solution.py:170
  92.1 6.8 %copy-start.9 = (bf16[2048,128]{1,0:T(8,128)(2,1)}, bf16[2048,128]{1,0:T(8,128)(2,1)S(1)}, u32[]{:S(2)}) copy-start(bf16[2048,128]{1,0:T(8,128)(2,1)S(1)} %collective-permute-done.10) | copy-start | bytes 1572868
  95.2 3.7 %copy-start.10 = (bf16[2048,128]{1,0:T(8,128)(2,1)}, bf16[2048,128]{1,0:T(8,128)(2,1)S(1)}, u32[]{:S(2)}) copy-start(bf16[2048,128]{1,0:T(8,128)(2,1)S(1)} %collective-permute-done.9) | copy-start | bytes 1572868
  95.4 3.5 %copy-start.11 = (bf16[2048,128]{1,0:T(8,128)(2,1)}, bf16[2048,128]{1,0:T(8,128)(2,1)S(1)}, u32[]{:S(2)}) copy-start(bf16[2048,128]{1,0:T(8,128)(2,1)S(1)} %collective-permute-done.3) | copy-start | bytes 1572868
  95.4 3.5 %copy-start.12 = (bf16[2048,128]{1,0:T(8,128)(2,1)}, bf16[2048,128]{1,0:T(8,128)(2,1)S(1)}, u32[]{:S(2)}) copy-start(bf16[2048,128]{1,0:T(8,128)(2,1)S(1)} %collective-permute-done.4) | copy-start | bytes 1572868
  95.4 2.7 %collective-permute-start.11 = (bf16[2048,128]{1,0:T(8,128)(2,1)S(1)}, bf16[2048,128]{1,0:T(8,128)(2,1)S(1)}, u32[]{:S(2)}, u32[]{:S(2)}) collective-permute-start(bf16[2048,128]{1,0:T(8,128)(2,1)S(1)} %collective-permute-done.3), channel_id=1, source_target_pairs={{0,1},{1,0},{2,3},{3,2},{4,5},{5,4},{6,7},{7,6},{8,9},{9,8},{10,11... | collective-permute-start | bytes 1572872 | tf_op jit(solution)/shard_map/ppermute | solution.py:170
  96.6 2.3 %collective-permute-start.12 = (bf16[2048,128]{1,0:T(8,128)(2,1)S(1)}, bf16[2048,128]{1,0:T(8,128)(2,1)S(1)}, u32[]{:S(2)}, u32[]{:S(2)}) collective-permute-start(bf16[2048,128]{1,0:T(8,128)(2,1)S(1)} %collective-permute-done.4), channel_id=1, source_target_pairs={{0,1},{1,0},{2,3},{3,2},{4,5},{5,4},{6,7},{7,6},{8,9},{9,8},{10,11... | collective-permute-start | bytes 1572872 | tf_op jit(solution)/shard_map/ppermute | solution.py:170
  98.1 0.8 copy-start.13
  98.8 0.8 copy-start.14
  98.9 1.1 %copy-start.8 = (bf16[4096,128]{1,0:T(8,128)(2,1)}, bf16[4096,128]{1,0:T(8,128)(2,1)S(1)}, u32[]{:S(2)}) copy-start(bf16[4096,128]{1,0:T(8,128)(2,1)S(1)} %collective-permute-done.8) | copy-start | bytes 3145732

commit v5 on v4

--- a/solution.py
+++ b/solution.py
@@ -16,9 +16,10 @@
 Y, XL, Z, XH, CORE = range(5)
 BF16, F32 = jnp.bfloat16, jnp.float32
 ROWS = 1024
+GROUP = 8
 KC = 32
-XL_BIT, XH_BIT = 16, 2
-SENT = 3 * CB
+XH_BIT = 2
+SENT = 2 * CB
 HALF_ROWS = F * 2 * CB
 
 
@@ -85,17 +86,20 @@
 
     @pl.when(step == pl.num_programs(0) - 1)
     def _():
-        def place(owner, carry):
-            base = owner * CB
-            for j in range(CB):
-                placed[pl.ds(j, 1), :] = white[pl.ds(order[base + j], 1), :]
-            block = placed[...].astype(BF16)
-            for slot, partner in enumerate((0, XH_BIT, XL_BIT)):
-                at = (owner ^ partner) * SENT + slot * CB
-                out[pl.ds(pl.multiple_of(at, CB), CB), :] = block
+        def place(group, carry):
+            for u in range(GROUP):
+                base = (group * GROUP + u) * CB
+                for j in range(CB):
+                    placed[pl.ds(u * CB + j, 1), :] = white[pl.ds(order[base + j], 1), :]
+            for u in range(GROUP):
+                owner = group * GROUP + u
+                block = placed[pl.ds(u * CB, CB), :].astype(BF16)
+                for slot, partner in enumerate((0, XH_BIT)):
+                    at = (owner ^ partner) * SENT + slot * CB
+                    out[pl.ds(pl.multiple_of(at, CB), CB), :] = block
             return carry
 
-        lax.fori_loop(0, C // CB, place, 0)
+        lax.fori_loop(0, C // CB // GROUP, place, 0)
 
 
 def whiten(raw, quality, order, slab, wid):
@@ -113,7 +117,7 @@
             out_specs=whole((NW * SENT, 2 * F)),
             scratch_shapes=[
                 pltpu.VMEM((C, 2 * F), F32),
-                pltpu.VMEM((CB, 2 * F), F32),
+                pltpu.VMEM((GROUP * CB, 2 * F), F32),
                 pltpu.VMEM((WLEN, WLEN), BF16),
                 pltpu.VMEM((4 * F, 4 * F), BF16),
             ],
@@ -132,36 +136,28 @@
     return turned[...].astype(BF16)
 
 
-def turn_two_kernel(received, out, wide, turned):
-    wide[...] = received[...].astype(F32).reshape(wide.shape)
+def turn_kernel(received, pair, own, wide, turned):
+    wide[...] = received[...].astype(F32)
     for slot in range(2):
-        block = turn_block(wide, slot * CB, 2 * CB, turned)
-        out[pl.ds(slot * HALF_ROWS, HALF_ROWS), :] = block
-
-
-def turn_one_kernel(received, own, out, wide, turned):
-    wide[...] = received[...].astype(F32).reshape(wide.shape)
-    out[0:HALF_ROWS, :] = own[...]
-    out[HALF_ROWS:, :] = turn_block(wide, 0, CB, turned)
-
-
-def turn_call(kernel, received, slots, first, *own):
+        block = turn_block(wide, slot * CB, SENT, turned)
+        pair[pl.ds(slot * HALF_ROWS, HALF_ROWS), :] = block
+        if slot == 0:
+            own[...] = block
+
+
+def turn(received):
     return pl.pallas_call(
-        kernel,
-        grid=(1,),
-        in_specs=[
-            pl.BlockSpec((NW, slots * CB, 2 * F), lambda i: (0, first, 0)),
-            *[pl.BlockSpec((HALF_ROWS, NW), lambda i: (0, 0)) for _ in own],
+        turn_kernel,
+        in_specs=[pl.BlockSpec(memory_space=pltpu.VMEM)],
+        out_specs=[pl.BlockSpec(memory_space=pltpu.VMEM)] * 2,
+        out_shape=[
+            jax.ShapeDtypeStruct((2 * HALF_ROWS, NW), BF16),
+            jax.ShapeDtypeStruct((HALF_ROWS, NW), BF16),
         ],
-        out_specs=pl.BlockSpec((2 * HALF_ROWS, NW), lambda i: (0, 0)),
-        out_shape=jax.ShapeDtypeStruct((2 * HALF_ROWS, NW), BF16),
-        scratch_shapes=[
-            pltpu.VMEM((NW * slots * CB, 2 * F), F32),
-            pltpu.VMEM((HALF_ROWS, NW), F32),
-        ],
+        scratch_shapes=[pltpu.VMEM((NW * SENT, 2 * F), F32), pltpu.VMEM((HALF_ROWS, NW), F32)],
         compiler_params=pltpu.CompilerParams(vmem_limit_bytes=24 << 20),
         name="turn",
-    )(received, *own)
+    )(received)
 
 
 def shift(x, axis, amount):
@@ -170,20 +166,19 @@
     return lax.ppermute(x, AXES, [(int(a), int(b)) for a, b in zip(ids.ravel(), to.ravel())])
 
 
-def gather_rings(row_pair, col_pair):
-    rows = [row_pair, shift(row_pair, Z, 1), shift(row_pair, Z, -1)]
-    cols = [col_pair, shift(col_pair, Y, 1), shift(col_pair, Y, -1)]
-    others = [shift(row_pair, CORE, 1)]
-    halves = (rows[1][:HALF_ROWS], rows[2][HALF_ROWS:])
-    halves = lax.optimization_barrier((*halves, *others))[:2]
-    for ring, halves in ((Z, halves), (Y, (cols[1][:HALF_ROWS], cols[2][HALF_ROWS:]))):
-        far = [shift(half, ring, way) for half, way in zip(halves, (1, -1))]
-        (rows if ring == Z else cols).extend(far)
-    after = lax.optimization_barrier((*rows[1:3], *cols[1:3]))[0]
-    others.append(shift(after, CORE, 1))
-    before, _ = lax.optimization_barrier((rows[2], others[1]))
-    others.append(shift(before, CORE, 1))
-    far = lax.optimization_barrier((*rows[3:], *cols[3:]))[:2]
+def gather_rings(pair, own):
+    rows = [pair, shift(pair, Z, 1), shift(pair, Z, -1)]
+    partner = shift(own, XL, 1)
+    cols = []
+    for block, far in ((own, 1), (partner, -1)):
+        near = {way: shift(block, Y, way) for way in (1, -1)}
+        cols += [block, near[1], near[-1], shift(near[far], Y, far)]
+    rows.append(shift(rows[1][:HALF_ROWS], Z, 1))
+    rows.append(shift(rows[2][HALF_ROWS:], Z, -1))
+    others = [shift(pair, CORE, 1)]
+    near = lax.optimization_barrier((*rows[1:3], *cols[1:3], *cols[5:7]))[:2]
+    others += [shift(block, CORE, 1) for block in near]
+    far = lax.optimization_barrier((*rows[3:], cols[3], cols[7]))[:2]
     others += [shift(block, CORE, 1) for block in far]
     return rows, others, cols
 
@@ -193,7 +188,7 @@
     y, xl, z, xh, core = bits(5, 4), bits(4, 2), bits(2, 4), bits(1, 2), bits(0, 2)
     held = [(0, 0), (0, 1), (1, 0), (1, 1), (3, 0), (3, 1), (2, 0), (2, 1)]
     rows = [((z - ring) & 3) * 4 + (xh ^ flip) * 2 for ring, flip in held]
-    cols = [((y - ring) & 3) * 2 + (xl ^ flip) for ring, flip in held]
+    cols = [((y - ring) & 3) * 2 + (xl ^ flip) for flip in (0, 1) for ring in (0, 1, 3, 2)]
     return [at * CB for at in [r + core for r in rows] + [r + 1 - core for r in rows] + cols]
 
 
@@ -254,9 +249,8 @@
     received = lax.all_to_all(
         spectra.reshape(NW, SENT, 2 * F), AXES, split_axis=0, concat_axis=0, tiled=True
     )
-    row_pair = turn_call(turn_two_kernel, received, 2, 0)
-    col_pair = turn_call(turn_one_kernel, received, 1, 2, row_pair)
-    rows, others, cols = gather_rings(row_pair, col_pair)
+    pair, own = turn(received.reshape(NW * SENT, 2 * F))
+    rows, others, cols = gather_rings(pair, own)
     return product(wid, rows + others + cols)
 
 

time: 112 us -> 101 us (0.902)
  blocking collectives: 36.3 us -> 30.7 us
  waiting for transfers between devices: 35.1 us -> 31.9 us
  Pallas kernels: 24.4 us -> 22.4 us
    all_to_all x1, blocking collectives: 36.3 us -> 30.7 us  [body(): lax.all_to_all(spectra.reshape(NW, SENT, 2 * F), AXES, split_axis=0, conc...]
    ppermute x13 -> x16, waiting for transfers between devices: 35.1 us -> 31.9 us  [shift(): lax.ppermute(x, AXES, [(int(a), int(b)) for a, b in zip(ids.ravel(), to.r...]
    pallas_call x2 -> x1, Pallas kernels: 3.66 us -> 2.54 us  [turn(): pl.pallas_call(turn_kernel, in_specs=[pl.BlockSpec(memory_space=pltpu.VME...]
    ppermute x13 -> x16, starting transfers between devices: 14 us -> 13.5 us  [shift(): lax.ppermute(x, AXES, [(int(a), int(b)) for a, b in zip(ids.ravel(), to.r...]
  transfers between devices with their start and end apart: 13 -> 16, of which waited for: 8 -> 8; matrix products, arithmetic and copies ran while one was open for 0% -> 0% of each run, Pallas kernels for 0% -> 0%
where the time goes in v5:
time: 101 us
  waiting for transfers between devices  31.9 us (32%)
  blocking collectives  30.7 us (30%)
  Pallas kernels  22.4 us (22%)
  starting transfers between devices  13.5 us (13%)
  local copies, waits for them, and re-layouts  2.03 us (2%)
    ppermute x16, waiting for transfers between devices, shift(): lax.ppermute(x, AXES, [(int(a), int(b)) for a, b in zip(ids.ravel(), to.r...  31.9 us
    all_to_all x1, blocking collectives, body(): lax.all_to_all(spectra.reshape(NW, SENT, 2 * F), AXES, split_axis=0, conc...  30.7 us
    ppermute x16, starting transfers between devices, shift(): lax.ppermute(x, AXES, [(int(a), int(b)) for a, b in zip(ids.ravel(), to.r...  13.5 us
    pallas_call x1, Pallas kernels, product(): pl.pallas_call(product_kernel, grid_spec=pltpu.PrefetchScalarGridSpec(num...  11.2 us
    pallas_call x1, Pallas kernels, whiten(): pl.pallas_call(whiten_kernel, grid_spec=pltpu.PrefetchScalarGridSpec(num_...  8.64 us
    pallas_call x1, Pallas kernels, turn(): pl.pallas_call(turn_kernel, in_specs=[pl.BlockSpec(memory_space=pltpu.VME...  2.54 us
  transfers between devices with their start and end apart: 16, of which 8 were waited for; matrix products, arithmetic and copies ran while one was open for 0% of the time, Pallas kernels for 0%

profile of v5, /device:TPU:1, one launch (start us, length us, event | category | flops | bytes accessed | tf_op | source)
XLA Modules:
  0.0 100.8 jit_solution(9220048537946261521)
XLA Ops:
  0.0 8.6 %whiten.1 = bf16[4096,128]{1,0:T(8,128)(2,1)} custom-call(s32[2048]{0:T(1024)} %order.1, s32[4]{0:T(128)} %slab.1, s32[1]{0:T(128)} %bitcast.wid, bf16[1,2048,512]{2,1,0:T(8,128)(2,1)} %raw.1, s32[16,128]{1,0:T(8,128)} %bitcast.48, bf16[512,128]{1,0:T(8,128)(2,1)} %constant.13.clone.dft), custom_call_target="tpu_custom_call" | custom-call | tf_op jit(solution)/shard_map/whiten/pallas_call | solution.py:107
  8.6 30.7 %all_to_all.5 = bf16[128,32,128]{2,1,0:T(8,128)(2,1)S(1)} all-to-all(bf16[128,32,128]{2,1,0:T(8,128)(2,1)} %bitcast.36), channel_id=1, replica_groups=mesh['src'=8,'rcv'=16] {'src','rcv'}, dimensions={0} | all-to-all | bytes 2097152 | tf_op jit(solution)/shard_map/all_to_all | solution.py:249
  39.3 2.5 %turn.1 = (bf16[4096,128]{1,0:T(8,128)(2,1)S(1)}, bf16[2048,128]{1,0:T(8,128)(2,1)S(1)}) custom-call(bf16[4096,128]{1,0:T(8,128)(2,1)S(1)} %bitcast.24), custom_call_target="tpu_custom_call" | custom-call | tf_op jit(solution)/shard_map/turn/pallas_call | solution.py:149
  41.9 0.8 collective-permute-start.1
  42.7 0.8 collective-permute-start
  43.4 0.0 collective-permute-start.7
  43.5 0.4 collective-permute-start.5
  43.8 2.3 %collective-permute-start.6 = (bf16[2048,128]{1,0:T(8,128)(2,1)S(1)}, bf16[2048,128]{1,0:T(8,128)(2,1)S(1)}, u32[]{:S(2)}, u32[]{:S(2)}) collective-permute-start(bf16[2048,128]{1,0:T(8,128)(2,1)S(1)} %get-tuple-element.12), channel_id=1, source_target_pairs={{0,96},{1,97},{2,98},{3,99},{4,100},{5,101},{6,102},{7,103},{8,104... | collective-permute-start | bytes 1572872 | tf_op jit(solution)/shard_map/ppermute | solution.py:166
  46.1 9.3 %collective-permute-done.7 = bf16[2048,128]{1,0:T(8,128)(2,1)S(1)} collective-permute-done((bf16[2048,128]{1,0:T(8,128)(2,1)S(1)}, bf16[2048,128]{1,0:T(8,128)(2,1)S(1)}, u32[]{:S(2)}, u32[]{:S(2)}) %collective-permute-start.7) | collective-permute-done | bytes 524320 | tf_op jit(solution)/shard_map/ppermute | solution.py:166
  55.5 0.2 collective-permute-start.9
  55.7 0.5 collective-permute-done.5
  56.1 0.8 collective-permute-start.8
  56.9 8.9 %collective-permute-done.1 = bf16[4096,128]{1,0:T(8,128)(2,1)S(1)} collective-permute-done((bf16[4096,128]{1,0:T(8,128)(2,1)S(1)}, bf16[4096,128]{1,0:T(8,128)(2,1)S(1)}, u32[]{:S(2)}, u32[]{:S(2)}) %collective-permute-start.1) | collective-permute-done | bytes 1048608 | tf_op jit(solution)/shard_map/ppermute | solution.py:166
  65.9 2.1 %collective-permute-done = bf16[4096,128]{1,0:T(8,128)(2,1)S(1)} collective-permute-done((bf16[4096,128]{1,0:T(8,128)(2,1)S(1)}, bf16[4096,128]{1,0:T(8,128)(2,1)S(1)}, u32[]{:S(2)}, u32[]{:S(2)}) %collective-permute-start) | collective-permute-done | bytes 1048608 | tf_op jit(solution)/shard_map/ppermute | solution.py:166
  68.0 0.8 collective-permute-start.3
  68.8 1.8 %collective-permute-start.4 = (bf16[4096,128]{1,0:T(8,128)(2,1)S(1)}, bf16[4096,128]{1,0:T(8,128)(2,1)S(1)}, u32[]{:S(2)}, u32[]{:S(2)}) collective-permute-start(bf16[4096,128]{1,0:T(8,128)(2,1)S(1)} %get-tuple-element.11), channel_id=1, source_target_pairs={{0,1},{1,0},{2,3},{3,2},{4,5},{5,4},{6,7},{7,6},{8,9},{9,8},{10,11... | collective-permute-start | bytes 3145736 | tf_op jit(solution)/shard_map/ppermute | solution.py:166
  70.6 0.0 collective-permute-done.9
  70.6 0.7 collective-permute-start.2
  71.4 0.0 collective-permute-done.8
  71.4 1.7 %collective-permute-start.13 = (bf16[2048,128]{1,0:T(8,128)(2,1)S(1)}, bf16[2048,128]{1,0:T(8,128)(2,1)S(1)}, u32[]{:S(2)}, u32[]{:S(2)}) collective-permute-start(bf16[2048,128]{1,0:T(8,128)(2,1)S(1)} %collective-permute-done.9), channel_id=1, source_target_pairs={{0,96},{1,97},{2,98},{3,99},{4,100},{5,101},{6,102},{7,103},{8,104... | collective-permute-start | bytes 1572872 | tf_op jit(solution)/shard_map/ppermute | solution.py:166
  73.1 8.0 %collective-permute-done.12 = bf16[2048,128]{1,0:T(8,128)(2,1)S(1)} collective-permute-done((bf16[2048,128]{1,0:T(8,128)(2,1)S(1)}, bf16[2048,128]{1,0:T(8,128)(2,1)S(1)}, u32[]{:S(2)}, u32[]{:S(2)}) %collective-permute-start.12) | collective-permute-done | bytes 524320 | tf_op jit(solution)/shard_map/ppermute | solution.py:166
  81.0 1.9 %collective-permute-start.10 = (bf16[4096,128]{1,0:T(8,128)(2,1)S(1)}, bf16[4096,128]{1,0:T(8,128)(2,1)S(1)}, u32[]{:S(2)}, u32[]{:S(2)}) collective-permute-start(bf16[4096,128]{1,0:T(8,128)(2,1)S(1)} %collective-permute-done), channel_id=1, source_target_pairs={{0,1},{1,0},{2,3},{3,2},{4,5},{5,4},{6,7},{7,6},{8,9},{9,8},{10,11... | collective-permute-start | bytes 3145736 | tf_op jit(solution)/shard_map/ppermute | solution.py:166
  82.9 0.1 collective-permute-start.11
  83.0 2.3 %collective-permute-done.2 = bf16[2048,128]{1,0:T(8,128)(2,1)S(1)} collective-permute-done((bf16[2048,128]{1,0:T(8,128)(2,1)S(1)}, bf16[2048,128]{1,0:T(8,128)(2,1)S(1)}, u32[]{:S(2)}, u32[]{:S(2)}) %collective-permute-start.2) | collective-permute-done | bytes 524320 | tf_op jit(solution)/shard_map/ppermute | solution.py:166
  85.3 0.9 collective-permute-start.14
  86.3 0.3 collective-permute-start.15
  86.6 0.1 collective-permute-done.11
  86.7 1.1 %copy-done.6 = bf16[4096,128]{1,0:T(8,128)(2,1)} copy-done((bf16[4096,128]{1,0:T(8,128)(2,1)}, bf16[4096,128]{1,0:T(8,128)(2,1)S(1)}, u32[]{:S(2)}) %copy-start.6) | copy-done | bytes 1048600
  87.8 0.7 collective-permute-done.15
  88.6 0.1 copy-done.16
  88.7 0.7 copy-done.17
  89.5 11.2 %product.1 = f32[2,64,256,128]{3,2,1,0:T(8,128)} custom-call(s32[1]{0:T(128)} %bitcast.wid, bf16[128,32,128]{2,1,0:T(8,128)(2,1)} %bitcast.22, bf16[128,32,128]{2,1,0:T(8,128)(2,1)} %bitcast.23, bf16[128,32,128]{2,1,0:T(8,128)(2,1)} %bitcast.28, bf16[128,32,128]{2,1,0:T(8,128)(2,1)} %bitcast.29, bf16[128,32,128]{2,1,0:T(8,128)(2,1)} %bitcast.26, ...), custom_call_target="tpu_custom_call" | custom-call | tf_op jit(solution)/shard_map/product/pallas_call | solution.py:230
  (42 shorter events, 0.1 us)
Async XLA Ops:
  41.9 47.5 %copy-start = (bf16[4096,128]{1,0:T(8,128)(2,1)}, bf16[4096,128]{1,0:T(8,128)(2,1)S(1)}, u32[]{:S(2)}) copy-start(bf16[4096,128]{1,0:T(8,128)(2,1)S(1)} %get-tuple-element.11) | copy-start | bytes 3145732
  41.9 47.5 %copy-start.1 = (bf16[2048,128]{1,0:T(8,128)(2,1)}, bf16[2048,128]{1,0:T(8,128)(2,1)S(1)}, u32[]{:S(2)}) copy-start(bf16[2048,128]{1,0:T(8,128)(2,1)S(1)} %get-tuple-element.12) | copy-start | bytes 1572868
  41.9 23.9 %collective-permute-start.1 = (bf16[4096,128]{1,0:T(8,128)(2,1)S(1)}, bf16[4096,128]{1,0:T(8,128)(2,1)S(1)}, u32[]{:S(2)}, u32[]{:S(2)}) collective-permute-start(bf16[4096,128]{1,0:T(8,128)(2,1)S(1)} %get-tuple-element.11), channel_id=1, source_target_pairs={{0,12},{1,13},{2,14},{3,15},{4,0},{5,1},{6,2},{7,3},{8,4},{9,5},{1... | collective-permute-start | bytes 3145736 | tf_op jit(solution)/shard_map/ppermute | solution.py:166
  42.7 25.3 %collective-permute-start = (bf16[4096,128]{1,0:T(8,128)(2,1)S(1)}, bf16[4096,128]{1,0:T(8,128)(2,1)S(1)}, u32[]{:S(2)}, u32[]{:S(2)}) collective-permute-start(bf16[4096,128]{1,0:T(8,128)(2,1)S(1)} %get-tuple-element.11), channel_id=1, source_target_pairs={{0,4},{1,5},{2,6},{3,7},{4,8},{5,9},{6,10},{7,11},{8,12},{9,13},{1... | collective-permute-start | bytes 3145736 | tf_op jit(solution)/shard_map/ppermute | solution.py:166
  43.4 12.0 %collective-permute-start.7 = (bf16[2048,128]{1,0:T(8,128)(2,1)S(1)}, bf16[2048,128]{1,0:T(8,128)(2,1)S(1)}, u32[]{:S(2)}, u32[]{:S(2)}) collective-permute-start(bf16[2048,128]{1,0:T(8,128)(2,1)S(1)} %get-tuple-element.12), channel_id=1, source_target_pairs={{0,16},{1,17},{2,18},{3,19},{4,20},{5,21},{6,22},{7,23},{8,24},{9,... | collective-permute-start | bytes 1572872 | tf_op jit(solution)/shard_map/ppermute | solution.py:166
  43.5 12.7 %collective-permute-start.5 = (bf16[2048,128]{1,0:T(8,128)(2,1)S(1)}, bf16[2048,128]{1,0:T(8,128)(2,1)S(1)}, u32[]{:S(2)}, u32[]{:S(2)}) collective-permute-start(bf16[2048,128]{1,0:T(8,128)(2,1)S(1)} %get-tuple-element.12), channel_id=1, source_target_pairs={{0,32},{1,33},{2,34},{3,35},{4,36},{5,37},{6,38},{7,39},{8,40},{9,... | collective-permute-start | bytes 1572872 | tf_op jit(solution)/shard_map/ppermute | solution.py:166
  43.8 25.0 %collective-permute-start.6 = (bf16[2048,128]{1,0:T(8,128)(2,1)S(1)}, bf16[2048,128]{1,0:T(8,128)(2,1)S(1)}, u32[]{:S(2)}, u32[]{:S(2)}) collective-permute-start(bf16[2048,128]{1,0:T(8,128)(2,1)S(1)} %get-tuple-element.12), channel_id=1, source_target_pairs={{0,96},{1,97},{2,98},{3,99},{4,100},{5,101},{6,102},{7,103},{8,104... | collective-permute-start | bytes 1572872 | tf_op jit(solution)/shard_map/ppermute | solution.py:166
  55.5 32.4 %copy-start.7 = (bf16[2048,128]{1,0:T(8,128)(2,1)}, bf16[2048,128]{1,0:T(8,128)(2,1)S(1)}, u32[]{:S(2)}) copy-start(bf16[2048,128]{1,0:T(8,128)(2,1)S(1)} %collective-permute-done.7) | copy-start | bytes 1572868
  55.5 15.2 %collective-permute-start.9 = (bf16[2048,128]{1,0:T(8,128)(2,1)S(1)}, bf16[2048,128]{1,0:T(8,128)(2,1)S(1)}, u32[]{:S(2)}, u32[]{:S(2)}) collective-permute-start(bf16[2048,128]{1,0:T(8,128)(2,1)S(1)} %collective-permute-done.7), channel_id=1, source_target_pairs={{0,96},{1,97},{2,98},{3,99},{4,100},{5,101},{6,102},{7,103},{8,104... | collective-permute-start | bytes 1572872 | tf_op jit(solution)/shard_map/ppermute | solution.py:166
  56.1 32.4 %copy-start.8 = (bf16[2048,128]{1,0:T(8,128)(2,1)}, bf16[2048,128]{1,0:T(8,128)(2,1)S(1)}, u32[]{:S(2)}) copy-start(bf16[2048,128]{1,0:T(8,128)(2,1)S(1)} %collective-permute-done.5) | copy-start | bytes 1572868
  56.1 15.2 %collective-permute-start.8 = (bf16[2048,128]{1,0:T(8,128)(2,1)S(1)}, bf16[2048,128]{1,0:T(8,128)(2,1)S(1)}, u32[]{:S(2)}, u32[]{:S(2)}) collective-permute-start(bf16[2048,128]{1,0:T(8,128)(2,1)S(1)} %collective-permute-done.7), channel_id=1, source_target_pairs={{0,32},{1,33},{2,34},{3,35},{4,36},{5,37},{6,38},{7,39},{8,40},{9,... | collective-permute-start | bytes 1572872 | tf_op jit(solution)/shard_map/ppermute | solution.py:166
  65.8 23.6 %copy-start.2 = (bf16[4096,128]{1,0:T(8,128)(2,1)}, bf16[4096,128]{1,0:T(8,128)(2,1)S(1)}, u32[]{:S(2)}) copy-start(bf16[4096,128]{1,0:T(8,128)(2,1)S(1)} %collective-permute-done.1) | copy-start | bytes 3145732
  65.8 15.2 %collective-permute-start.12 = (bf16[2048,128]{1,0:T(8,128)(2,1)S(1)}, bf16[2048,128]{1,0:T(8,128)(2,1)S(1)}, u32[]{:S(2)}, u32[]{:S(2)}) collective-permute-start(bf16[2048,128]{1,0:T(8,128)(2,1)S(1)} %collective-permute-done.5), channel_id=1, source_target_pairs={{0,32},{1,33},{2,34},{3,35},{4,36},{5,37},{6,38},{7,39},{8,40},{9,... | collective-permute-start | bytes 1572872 | tf_op jit(solution)/shard_map/ppermute | solution.py:166
  68.0 21.5 %copy-start.3 = (bf16[4096,128]{1,0:T(8,128)(2,1)}, bf16[4096,128]{1,0:T(8,128)(2,1)S(1)}, u32[]{:S(2)}) copy-start(bf16[4096,128]{1,0:T(8,128)(2,1)S(1)} %collective-permute-done) | copy-start | bytes 3145732
  68.0 15.0 %collective-permute-start.3 = (bf16[2048,128]{1,0:T(8,128)(2,1)S(1)}, bf16[2048,128]{1,0:T(8,128)(2,1)S(1)}, u32[]{:S(2)}, u32[]{:S(2)}) collective-permute-start(bf16[2048,128]{1,0:T(8,128)(2,1)S(1)} %slice.9), channel_id=1, source_target_pairs={{0,12},{1,13},{2,14},{3,15},{4,0},{5,1},{6,2},{7,3},{8,4},{9,5},{1... | collective-permute-start | bytes 1572872 | tf_op jit(solution)/shard_map/ppermute | solution.py:166
  68.8 19.8 %copy-start.9 = (bf16[2048,128]{1,0:T(8,128)(2,1)}, bf16[2048,128]{1,0:T(8,128)(2,1)S(1)}, u32[]{:S(2)}) copy-start(bf16[2048,128]{1,0:T(8,128)(2,1)S(1)} %collective-permute-done.6) | copy-start | bytes 1572868
  68.8 17.7 %collective-permute-start.4 = (bf16[4096,128]{1,0:T(8,128)(2,1)S(1)}, bf16[4096,128]{1,0:T(8,128)(2,1)S(1)}, u32[]{:S(2)}, u32[]{:S(2)}) collective-permute-start(bf16[4096,128]{1,0:T(8,128)(2,1)S(1)} %get-tuple-element.11), channel_id=1, source_target_pairs={{0,1},{1,0},{2,3},{3,2},{4,5},{5,4},{6,7},{7,6},{8,9},{9,8},{10,11... | collective-permute-start | bytes 3145736 | tf_op jit(solution)/shard_map/ppermute | solution.py:166
  70.6 17.9 %copy-start.10 = (bf16[2048,128]{1,0:T(8,128)(2,1)}, bf16[2048,128]{1,0:T(8,128)(2,1)S(1)}, u32[]{:S(2)}) copy-start(bf16[2048,128]{1,0:T(8,128)(2,1)S(1)} %collective-permute-done.9) | copy-start | bytes 1572868
  70.6 14.7 %collective-permute-start.2 = (bf16[2048,128]{1,0:T(8,128)(2,1)S(1)}, bf16[2048,128]{1,0:T(8,128)(2,1)S(1)}, u32[]{:S(2)}, u32[]{:S(2)}) collective-permute-start(bf16[2048,128]{1,0:T(8,128)(2,1)S(1)} %slice.8), channel_id=1, source_target_pairs={{0,4},{1,5},{2,6},{3,7},{4,8},{5,9},{6,10},{7,11},{8,12},{9,13},{1... | collective-permute-start | bytes 1572872 | tf_op jit(solution)/shard_map/ppermute | solution.py:166
  71.4 17.2 %copy-start.11 = (bf16[2048,128]{1,0:T(8,128)(2,1)}, bf16[2048,128]{1,0:T(8,128)(2,1)S(1)}, u32[]{:S(2)}) copy-start(bf16[2048,128]{1,0:T(8,128)(2,1)S(1)} %collective-permute-done.8) | copy-start | bytes 1572868
  71.4 14.0 %collective-permute-start.13 = (bf16[2048,128]{1,0:T(8,128)(2,1)S(1)}, bf16[2048,128]{1,0:T(8,128)(2,1)S(1)}, u32[]{:S(2)}, u32[]{:S(2)}) collective-permute-start(bf16[2048,128]{1,0:T(8,128)(2,1)S(1)} %collective-permute-done.9), channel_id=1, source_target_pairs={{0,96},{1,97},{2,98},{3,99},{4,100},{5,101},{6,102},{7,103},{8,104... | collective-permute-start | bytes 1572872 | tf_op jit(solution)/shard_map/ppermute | solution.py:166
  81.0 7.6 %copy-start.12 = (bf16[2048,128]{1,0:T(8,128)(2,1)}, bf16[2048,128]{1,0:T(8,128)(2,1)S(1)}, u32[]{:S(2)}) copy-start(bf16[2048,128]{1,0:T(8,128)(2,1)S(1)} %collective-permute-done.12) | copy-start | bytes 1572868
  81.0 5.5 %collective-permute-start.10 = (bf16[4096,128]{1,0:T(8,128)(2,1)S(1)}, bf16[4096,128]{1,0:T(8,128)(2,1)S(1)}, u32[]{:S(2)}, u32[]{:S(2)}) collective-permute-start(bf16[4096,128]{1,0:T(8,128)(2,1)S(1)} %collective-permute-done), channel_id=1, source_target_pairs={{0,1},{1,0},{2,3},{3,2},{4,5},{5,4},{6,7},{7,6},{8,9},{9,8},{10,11... | collective-permute-start | bytes 3145736 | tf_op jit(solution)/shard_map/ppermute | solution.py:166
  82.9 5.7 %copy-start.13 = (bf16[2048,128]{1,0:T(8,128)(2,1)}, bf16[2048,128]{1,0:T(8,128)(2,1)S(1)}, u32[]{:S(2)}) copy-start(bf16[2048,128]{1,0:T(8,128)(2,1)S(1)} %collective-permute-done.3) | copy-start | bytes 1572868
  82.9 3.8 %collective-permute-start.11 = (bf16[4096,128]{1,0:T(8,128)(2,1)S(1)}, bf16[4096,128]{1,0:T(8,128)(2,1)S(1)}, u32[]{:S(2)}, u32[]{:S(2)}) collective-permute-start(bf16[4096,128]{1,0:T(8,128)(2,1)S(1)} %collective-permute-done.1), channel_id=1, source_target_pairs={{0,1},{1,0},{2,3},{3,2},{4,5},{5,4},{6,7},{7,6},{8,9},{9,8},{10,11... | collective-permute-start | bytes 3145736 | tf_op jit(solution)/shard_map/ppermute | solution.py:166
  85.3 3.3 %copy-start.14 = (bf16[2048,128]{1,0:T(8,128)(2,1)}, bf16[2048,128]{1,0:T(8,128)(2,1)S(1)}, u32[]{:S(2)}) copy-start(bf16[2048,128]{1,0:T(8,128)(2,1)S(1)} %collective-permute-done.2) | copy-start | bytes 1572868
  85.3 3.3 %copy-start.15 = (bf16[2048,128]{1,0:T(8,128)(2,1)}, bf16[2048,128]{1,0:T(8,128)(2,1)S(1)}, u32[]{:S(2)}) copy-start(bf16[2048,128]{1,0:T(8,128)(2,1)S(1)} %collective-permute-done.13) | copy-start | bytes 1572868
  85.3 2.5 %collective-permute-start.14 = (bf16[2048,128]{1,0:T(8,128)(2,1)S(1)}, bf16[2048,128]{1,0:T(8,128)(2,1)S(1)}, u32[]{:S(2)}, u32[]{:S(2)}) collective-permute-start(bf16[2048,128]{1,0:T(8,128)(2,1)S(1)} %collective-permute-done.2), channel_id=1, source_target_pairs={{0,1},{1,0},{2,3},{3,2},{4,5},{5,4},{6,7},{7,6},{8,9},{9,8},{10,11... | collective-permute-start | bytes 1572872 | tf_op jit(solution)/shard_map/ppermute | solution.py:166
  86.3 2.3 %collective-permute-start.15 = (bf16[2048,128]{1,0:T(8,128)(2,1)S(1)}, bf16[2048,128]{1,0:T(8,128)(2,1)S(1)}, u32[]{:S(2)}, u32[]{:S(2)}) collective-permute-start(bf16[2048,128]{1,0:T(8,128)(2,1)S(1)} %collective-permute-done.3), channel_id=1, source_target_pairs={{0,1},{1,0},{2,3},{3,2},{4,5},{5,4},{6,7},{7,6},{8,9},{9,8},{10,11... | collective-permute-start | bytes 1572872 | tf_op jit(solution)/shard_map/ppermute | solution.py:166
  86.6 2.9 %copy-start.4 = (bf16[4096,128]{1,0:T(8,128)(2,1)}, bf16[4096,128]{1,0:T(8,128)(2,1)S(1)}, u32[]{:S(2)}) copy-start(bf16[4096,128]{1,0:T(8,128)(2,1)S(1)} %collective-permute-done.4) | copy-start | bytes 3145732
  86.6 2.9 %copy-start.5 = (bf16[4096,128]{1,0:T(8,128)(2,1)}, bf16[4096,128]{1,0:T(8,128)(2,1)S(1)}, u32[]{:S(2)}) copy-start(bf16[4096,128]{1,0:T(8,128)(2,1)S(1)} %collective-permute-done.10) | copy-start | bytes 3145732
  86.7 1.1 %copy-start.6 = (bf16[4096,128]{1,0:T(8,128)(2,1)}, bf16[4096,128]{1,0:T(8,128)(2,1)S(1)}, u32[]{:S(2)}) copy-start(bf16[4096,128]{1,0:T(8,128)(2,1)S(1)} %collective-permute-done.11) | copy-start | bytes 3145732
  (2 other events, 1.7 us)

commit v6 on v5

--- a/solution.py
+++ b/solution.py
@@ -18,6 +18,7 @@
 ROWS = 1024
 GROUP = 8
 KC = 32
+OUT_BINS = 8
 XH_BIT = 2
 SENT = 2 * CB
 HALF_ROWS = F * 2 * CB
@@ -193,7 +194,16 @@
 
 
 def product_kernel(wid, *refs):
-    rows, cols, (out, b) = refs[:16], refs[16:24], refs[24:]
+    rows, cols, (out, b, made, sent) = refs[:16], refs[16:24], refs[24:]
+    step = pl.program_id(0)
+    chunks = KC // OUT_BINS
+
+    def send(slot, at):
+        first = pl.multiple_of(at * KC + slot * OUT_BINS, OUT_BINS)
+        return pltpu.make_async_copy(
+            made.at[slot], out.at[:, pl.ds(first, OUT_BINS)], sent.at[slot]
+        )
+
     offsets = [pl.multiple_of(at, CB) for at in block_offsets(wid[0])]
     for block, offset in zip(cols, offsets[16:]):
         re, im = block[:, 0:CB, :], block[:, CB : 2 * CB, :]
@@ -202,21 +212,30 @@
         b[:, pl.ds(128 + offset, CB), 0:NW] = -im
         b[:, pl.ds(128 + offset, CB), NW : 2 * NW] = re
     factor = 1.0 / math.sqrt(NW)
-    for k in range(KC):
-        halves = [
-            jnp.concatenate([row[k, 0:CB, :], row[k, CB : 2 * CB, :]], axis=1) for row in rows
-        ]
-        o = lax.dot_general(
-            jnp.concatenate(halves, axis=0),
-            b[k],
-            (((1,), (1,)), ((), ())),
-            preferred_element_type=F32,
-        )
-        o = o * factor
-        for index, offset in enumerate(offsets[:16]):
-            part = o[index * CB : (index + 1) * CB]
-            out[0, k, pl.ds(offset, CB), :] = part[:, :128]
-            out[1, k, pl.ds(offset, CB), :] = part[:, 128:]
+    for slot in range(chunks):
+        pl.when(step > 0)(lambda slot=slot: send(slot, step - 1).wait())
+        for bin_index in range(OUT_BINS):
+            k = slot * OUT_BINS + bin_index
+            parts = [
+                jnp.concatenate([row[k, 0:CB, :], row[k, CB : 2 * CB, :]], axis=1) for row in rows
+            ]
+            o = lax.dot_general(
+                jnp.concatenate(parts, axis=0),
+                b[k],
+                (((1,), (1,)), ((), ())),
+                preferred_element_type=F32,
+            )
+            o = o * factor
+            for index, offset in enumerate(offsets[:16]):
+                part = o[index * CB : (index + 1) * CB]
+                made[slot, 0, bin_index, pl.ds(offset, CB), :] = part[:, :128]
+                made[slot, 1, bin_index, pl.ds(offset, CB), :] = part[:, 128:]
+        send(slot, step).start()
+
+    @pl.when(step == pl.num_programs(0) - 1)
+    def _():
+        for slot in range(chunks):
+            send(slot, step).wait()
 
 
 def product(wid, blocks):
@@ -233,8 +252,12 @@
             num_scalar_prefetch=1,
             grid=(steps,),
             in_specs=specs,
-            out_specs=pl.BlockSpec((2, KC, 256, 128), lambda i, m: (0, i, 0, 0)),
-            scratch_shapes=[pltpu.VMEM((KC, 256, 256), BF16)],
+            out_specs=pl.BlockSpec(memory_space=pl.ANY),
+            scratch_shapes=[
+                pltpu.VMEM((KC, 256, 256), BF16),
+                pltpu.VMEM((KC // OUT_BINS, 2, OUT_BINS, 256, 128), F32),
+                pltpu.SemaphoreType.DMA((KC // OUT_BINS,)),
+            ],
         ),
         out_shape=jax.ShapeDtypeStruct((2, F, 256, 128), F32),
         compiler_params=pltpu.CompilerParams(vmem_limit_bytes=58 << 20),

time: 101 us -> 99.9 us (0.989)
  Pallas kernels: 22.4 us -> 21.2 us
    pallas_call x1, Pallas kernels: 11.2 us -> 10 us  [product(): pl.pallas_call(product_kernel, grid_spec=pltpu.PrefetchScalarGridSpec(num...]
where the time goes in v6:
time: 99.9 us; the launch traced here: 99.6 us
  waiting for transfers between devices  31.9 us (32%)
  blocking collectives  30.7 us (31%)
  Pallas kernels  21.2 us (21%)
  starting transfers between devices  13.5 us (14%)
  local copies, waits for them, and re-layouts  2.03 us (2%)
    ppermute x16, waiting for transfers between devices, shift(): lax.ppermute(x, AXES, [(int(a), int(b)) for a, b in zip(ids.ravel(), to.r...  31.9 us
    all_to_all x1, blocking collectives, body(): lax.all_to_all(spectra.reshape(NW, SENT, 2 * F), AXES, split_axis=0, conc...  30.7 us
    ppermute x16, starting transfers between devices, shift(): lax.ppermute(x, AXES, [(int(a), int(b)) for a, b in zip(ids.ravel(), to.r...  13.5 us
    pallas_call x1, Pallas kernels, product(): pl.pallas_call(product_kernel, grid_spec=pltpu.PrefetchScalarGridSpec(num...  10 us
    pallas_call x1, Pallas kernels, whiten(): pl.pallas_call(whiten_kernel, grid_spec=pltpu.PrefetchScalarGridSpec(num_...  8.64 us
    pallas_call x1, Pallas kernels, turn(): pl.pallas_call(turn_kernel, in_specs=[pl.BlockSpec(memory_space=pltpu.VME...  2.54 us
  transfers between devices with their start and end apart: 16, of which 8 were waited for; matrix products, arithmetic and copies ran while one was open for 0% of the time, Pallas kernels for 0%

profile of v6, /device:TPU:1, one launch (start us, length us, event | category | flops | bytes accessed | tf_op | source)
XLA Modules:
  0.0 99.6 jit_solution(10134292877534416080)
XLA Ops:
  0.0 8.6 %whiten.1 = bf16[4096,128]{1,0:T(8,128)(2,1)} custom-call(s32[2048]{0:T(1024)} %order.1, s32[4]{0:T(128)} %slab.1, s32[1]{0:T(128)} %bitcast.wid, bf16[1,2048,512]{2,1,0:T(8,128)(2,1)} %raw.1, s32[16,128]{1,0:T(8,128)} %bitcast.48, bf16[512,128]{1,0:T(8,128)(2,1)} %constant.13.clone.dft), custom_call_target="tpu_custom_call" | custom-call | tf_op jit(solution)/shard_map/whiten/pallas_call | solution.py:108
  8.6 30.7 %all_to_all.5 = bf16[128,32,128]{2,1,0:T(8,128)(2,1)S(1)} all-to-all(bf16[128,32,128]{2,1,0:T(8,128)(2,1)} %bitcast.36), channel_id=1, replica_groups=mesh['src'=8,'rcv'=16] {'src','rcv'}, dimensions={0} | all-to-all | bytes 2097152 | tf_op jit(solution)/shard_map/all_to_all | solution.py:272
  39.3 2.5 %turn.1 = (bf16[4096,128]{1,0:T(8,128)(2,1)S(1)}, bf16[2048,128]{1,0:T(8,128)(2,1)S(1)}) custom-call(bf16[4096,128]{1,0:T(8,128)(2,1)S(1)} %bitcast.24), custom_call_target="tpu_custom_call" | custom-call | tf_op jit(solution)/shard_map/turn/pallas_call | solution.py:150
  41.9 0.8 collective-permute-start.1
  42.7 0.8 collective-permute-start
  43.4 0.0 collective-permute-start.7
  43.5 0.4 collective-permute-start.5
  43.8 2.3 %collective-permute-start.6 = (bf16[2048,128]{1,0:T(8,128)(2,1)S(1)}, bf16[2048,128]{1,0:T(8,128)(2,1)S(1)}, u32[]{:S(2)}, u32[]{:S(2)}) collective-permute-start(bf16[2048,128]{1,0:T(8,128)(2,1)S(1)} %get-tuple-element.12), channel_id=1, source_target_pairs={{0,96},{1,97},{2,98},{3,99},{4,100},{5,101},{6,102},{7,103},{8,104... | collective-permute-start | bytes 1572872 | tf_op jit(solution)/shard_map/ppermute | solution.py:167
  46.1 9.3 %collective-permute-done.7 = bf16[2048,128]{1,0:T(8,128)(2,1)S(1)} collective-permute-done((bf16[2048,128]{1,0:T(8,128)(2,1)S(1)}, bf16[2048,128]{1,0:T(8,128)(2,1)S(1)}, u32[]{:S(2)}, u32[]{:S(2)}) %collective-permute-start.7) | collective-permute-done | bytes 524320 | tf_op jit(solution)/shard_map/ppermute | solution.py:167
  55.5 0.2 collective-permute-start.9
  55.7 0.5 collective-permute-done.5
  56.2 0.8 collective-permute-start.8
  56.9 8.9 %collective-permute-done.1 = bf16[4096,128]{1,0:T(8,128)(2,1)S(1)} collective-permute-done((bf16[4096,128]{1,0:T(8,128)(2,1)S(1)}, bf16[4096,128]{1,0:T(8,128)(2,1)S(1)}, u32[]{:S(2)}, u32[]{:S(2)}) %collective-permute-start.1) | collective-permute-done | bytes 1048608 | tf_op jit(solution)/shard_map/ppermute | solution.py:167
  65.9 2.1 %collective-permute-done = bf16[4096,128]{1,0:T(8,128)(2,1)S(1)} collective-permute-done((bf16[4096,128]{1,0:T(8,128)(2,1)S(1)}, bf16[4096,128]{1,0:T(8,128)(2,1)S(1)}, u32[]{:S(2)}, u32[]{:S(2)}) %collective-permute-start) | collective-permute-done | bytes 1048608 | tf_op jit(solution)/shard_map/ppermute | solution.py:167
  68.0 0.8 collective-permute-start.3
  68.8 1.8 %collective-permute-start.4 = (bf16[4096,128]{1,0:T(8,128)(2,1)S(1)}, bf16[4096,128]{1,0:T(8,128)(2,1)S(1)}, u32[]{:S(2)}, u32[]{:S(2)}) collective-permute-start(bf16[4096,128]{1,0:T(8,128)(2,1)S(1)} %get-tuple-element.11), channel_id=1, source_target_pairs={{0,1},{1,0},{2,3},{3,2},{4,5},{5,4},{6,7},{7,6},{8,9},{9,8},{10,11... | collective-permute-start | bytes 3145736 | tf_op jit(solution)/shard_map/ppermute | solution.py:167
  70.6 0.0 collective-permute-done.9
  70.6 0.7 collective-permute-start.2
  71.4 0.0 collective-permute-done.8
  71.4 1.7 %collective-permute-start.13 = (bf16[2048,128]{1,0:T(8,128)(2,1)S(1)}, bf16[2048,128]{1,0:T(8,128)(2,1)S(1)}, u32[]{:S(2)}, u32[]{:S(2)}) collective-permute-start(bf16[2048,128]{1,0:T(8,128)(2,1)S(1)} %collective-permute-done.9), channel_id=1, source_target_pairs={{0,96},{1,97},{2,98},{3,99},{4,100},{5,101},{6,102},{7,103},{8,104... | collective-permute-start | bytes 1572872 | tf_op jit(solution)/shard_map/ppermute | solution.py:167
  73.1 8.0 %collective-permute-done.12 = bf16[2048,128]{1,0:T(8,128)(2,1)S(1)} collective-permute-done((bf16[2048,128]{1,0:T(8,128)(2,1)S(1)}, bf16[2048,128]{1,0:T(8,128)(2,1)S(1)}, u32[]{:S(2)}, u32[]{:S(2)}) %collective-permute-start.12) | collective-permute-done | bytes 524320 | tf_op jit(solution)/shard_map/ppermute | solution.py:167
  81.0 1.9 %collective-permute-start.10 = (bf16[4096,128]{1,0:T(8,128)(2,1)S(1)}, bf16[4096,128]{1,0:T(8,128)(2,1)S(1)}, u32[]{:S(2)}, u32[]{:S(2)}) collective-permute-start(bf16[4096,128]{1,0:T(8,128)(2,1)S(1)} %collective-permute-done), channel_id=1, source_target_pairs={{0,1},{1,0},{2,3},{3,2},{4,5},{5,4},{6,7},{7,6},{8,9},{9,8},{10,11... | collective-permute-start | bytes 3145736 | tf_op jit(solution)/shard_map/ppermute | solution.py:167
  82.9 0.1 collective-permute-start.11
  83.0 2.3 %collective-permute-done.2 = bf16[2048,128]{1,0:T(8,128)(2,1)S(1)} collective-permute-done((bf16[2048,128]{1,0:T(8,128)(2,1)S(1)}, bf16[2048,128]{1,0:T(8,128)(2,1)S(1)}, u32[]{:S(2)}, u32[]{:S(2)}) %collective-permute-start.2) | collective-permute-done | bytes 524320 | tf_op jit(solution)/shard_map/ppermute | solution.py:167
  85.3 0.9 collective-permute-start.14
  86.3 0.3 collective-permute-start.15
  86.6 0.1 collective-permute-done.11
  86.7 1.1 %copy-done.6 = bf16[4096,128]{1,0:T(8,128)(2,1)} copy-done((bf16[4096,128]{1,0:T(8,128)(2,1)}, bf16[4096,128]{1,0:T(8,128)(2,1)S(1)}, u32[]{:S(2)}) %copy-start.6) | copy-done | bytes 1048600
  87.9 0.7 collective-permute-done.15
  88.6 0.1 copy-done.16
  88.7 0.7 copy-done.17
  89.5 10.0 %product.1 = f32[2,64,256,128]{3,2,1,0:T(8,128)} custom-call(s32[1]{0:T(128)} %bitcast.wid, bf16[128,32,128]{2,1,0:T(8,128)(2,1)} %bitcast.22, bf16[128,32,128]{2,1,0:T(8,128)(2,1)} %bitcast.23, bf16[128,32,128]{2,1,0:T(8,128)(2,1)} %bitcast.28, bf16[128,32,128]{2,1,0:T(8,128)(2,1)} %bitcast.29, bf16[128,32,128]{2,1,0:T(8,128)(2,1)} %bitcast.26, ...), custom_call_target="tpu_custom_call" | custom-call | tf_op jit(solution)/shard_map/product/pallas_call | solution.py:249
  (42 shorter events, 0.1 us)
Async XLA Ops:
  41.9 47.5 %copy-start = (bf16[4096,128]{1,0:T(8,128)(2,1)}, bf16[4096,128]{1,0:T(8,128)(2,1)S(1)}, u32[]{:S(2)}) copy-start(bf16[4096,128]{1,0:T(8,128)(2,1)S(1)} %get-tuple-element.11) | copy-start | bytes 3145732
  41.9 47.5 %copy-start.1 = (bf16[2048,128]{1,0:T(8,128)(2,1)}, bf16[2048,128]{1,0:T(8,128)(2,1)S(1)}, u32[]{:S(2)}) copy-start(bf16[2048,128]{1,0:T(8,128)(2,1)S(1)} %get-tuple-element.12) | copy-start | bytes 1572868
  41.9 23.9 %collective-permute-start.1 = (bf16[4096,128]{1,0:T(8,128)(2,1)S(1)}, bf16[4096,128]{1,0:T(8,128)(2,1)S(1)}, u32[]{:S(2)}, u32[]{:S(2)}) collective-permute-start(bf16[4096,128]{1,0:T(8,128)(2,1)S(1)} %get-tuple-element.11), channel_id=1, source_target_pairs={{0,12},{1,13},{2,14},{3,15},{4,0},{5,1},{6,2},{7,3},{8,4},{9,5},{1... | collective-permute-start | bytes 3145736 | tf_op jit(solution)/shard_map/ppermute | solution.py:167
  42.7 25.3 %collective-permute-start = (bf16[4096,128]{1,0:T(8,128)(2,1)S(1)}, bf16[4096,128]{1,0:T(8,128)(2,1)S(1)}, u32[]{:S(2)}, u32[]{:S(2)}) collective-permute-start(bf16[4096,128]{1,0:T(8,128)(2,1)S(1)} %get-tuple-element.11), channel_id=1, source_target_pairs={{0,4},{1,5},{2,6},{3,7},{4,8},{5,9},{6,10},{7,11},{8,12},{9,13},{1... | collective-permute-start | bytes 3145736 | tf_op jit(solution)/shard_map/ppermute | solution.py:167
  43.4 12.0 %collective-permute-start.7 = (bf16[2048,128]{1,0:T(8,128)(2,1)S(1)}, bf16[2048,128]{1,0:T(8,128)(2,1)S(1)}, u32[]{:S(2)}, u32[]{:S(2)}) collective-permute-start(bf16[2048,128]{1,0:T(8,128)(2,1)S(1)} %get-tuple-element.12), channel_id=1, source_target_pairs={{0,16},{1,17},{2,18},{3,19},{4,20},{5,21},{6,22},{7,23},{8,24},{9,... | collective-permute-start | bytes 1572872 | tf_op jit(solution)/shard_map/ppermute | solution.py:167
  43.5 12.7 %collective-permute-start.5 = (bf16[2048,128]{1,0:T(8,128)(2,1)S(1)}, bf16[2048,128]{1,0:T(8,128)(2,1)S(1)}, u32[]{:S(2)}, u32[]{:S(2)}) collective-permute-start(bf16[2048,128]{1,0:T(8,128)(2,1)S(1)} %get-tuple-element.12), channel_id=1, source_target_pairs={{0,32},{1,33},{2,34},{3,35},{4,36},{5,37},{6,38},{7,39},{8,40},{9,... | collective-permute-start | bytes 1572872 | tf_op jit(solution)/shard_map/ppermute | solution.py:167
  43.8 25.0 %collective-permute-start.6 = (bf16[2048,128]{1,0:T(8,128)(2,1)S(1)}, bf16[2048,128]{1,0:T(8,128)(2,1)S(1)}, u32[]{:S(2)}, u32[]{:S(2)}) collective-permute-start(bf16[2048,128]{1,0:T(8,128)(2,1)S(1)} %get-tuple-element.12), channel_id=1, source_target_pairs={{0,96},{1,97},{2,98},{3,99},{4,100},{5,101},{6,102},{7,103},{8,104... | collective-permute-start | bytes 1572872 | tf_op jit(solution)/shard_map/ppermute | solution.py:167
  55.5 32.4 %copy-start.7 = (bf16[2048,128]{1,0:T(8,128)(2,1)}, bf16[2048,128]{1,0:T(8,128)(2,1)S(1)}, u32[]{:S(2)}) copy-start(bf16[2048,128]{1,0:T(8,128)(2,1)S(1)} %collective-permute-done.7) | copy-start | bytes 1572868
  55.5 15.2 %collective-permute-start.9 = (bf16[2048,128]{1,0:T(8,128)(2,1)S(1)}, bf16[2048,128]{1,0:T(8,128)(2,1)S(1)}, u32[]{:S(2)}, u32[]{:S(2)}) collective-permute-start(bf16[2048,128]{1,0:T(8,128)(2,1)S(1)} %collective-permute-done.7), channel_id=1, source_target_pairs={{0,96},{1,97},{2,98},{3,99},{4,100},{5,101},{6,102},{7,103},{8,104... | collective-permute-start | bytes 1572872 | tf_op jit(solution)/shard_map/ppermute | solution.py:167
  56.2 32.4 %copy-start.8 = (bf16[2048,128]{1,0:T(8,128)(2,1)}, bf16[2048,128]{1,0:T(8,128)(2,1)S(1)}, u32[]{:S(2)}) copy-start(bf16[2048,128]{1,0:T(8,128)(2,1)S(1)} %collective-permute-done.5) | copy-start | bytes 1572868
  56.2 15.2 %collective-permute-start.8 = (bf16[2048,128]{1,0:T(8,128)(2,1)S(1)}, bf16[2048,128]{1,0:T(8,128)(2,1)S(1)}, u32[]{:S(2)}, u32[]{:S(2)}) collective-permute-start(bf16[2048,128]{1,0:T(8,128)(2,1)S(1)} %collective-permute-done.7), channel_id=1, source_target_pairs={{0,32},{1,33},{2,34},{3,35},{4,36},{5,37},{6,38},{7,39},{8,40},{9,... | collective-permute-start | bytes 1572872 | tf_op jit(solution)/shard_map/ppermute | solution.py:167
  65.8 23.6 %copy-start.2 = (bf16[4096,128]{1,0:T(8,128)(2,1)}, bf16[4096,128]{1,0:T(8,128)(2,1)S(1)}, u32[]{:S(2)}) copy-start(bf16[4096,128]{1,0:T(8,128)(2,1)S(1)} %collective-permute-done.1) | copy-start | bytes 3145732
  65.8 15.2 %collective-permute-start.12 = (bf16[2048,128]{1,0:T(8,128)(2,1)S(1)}, bf16[2048,128]{1,0:T(8,128)(2,1)S(1)}, u32[]{:S(2)}, u32[]{:S(2)}) collective-permute-start(bf16[2048,128]{1,0:T(8,128)(2,1)S(1)} %collective-permute-done.5), channel_id=1, source_target_pairs={{0,32},{1,33},{2,34},{3,35},{4,36},{5,37},{6,38},{7,39},{8,40},{9,... | collective-permute-start | bytes 1572872 | tf_op jit(solution)/shard_map/ppermute | solution.py:167
  68.0 21.5 %copy-start.3 = (bf16[4096,128]{1,0:T(8,128)(2,1)}, bf16[4096,128]{1,0:T(8,128)(2,1)S(1)}, u32[]{:S(2)}) copy-start(bf16[4096,128]{1,0:T(8,128)(2,1)S(1)} %collective-permute-done) | copy-start | bytes 3145732
  68.0 15.0 %collective-permute-start.3 = (bf16[2048,128]{1,0:T(8,128)(2,1)S(1)}, bf16[2048,128]{1,0:T(8,128)(2,1)S(1)}, u32[]{:S(2)}, u32[]{:S(2)}) collective-permute-start(bf16[2048,128]{1,0:T(8,128)(2,1)S(1)} %slice.9), channel_id=1, source_target_pairs={{0,12},{1,13},{2,14},{3,15},{4,0},{5,1},{6,2},{7,3},{8,4},{9,5},{1... | collective-permute-start | bytes 1572872 | tf_op jit(solution)/shard_map/ppermute | solution.py:167
  68.8 19.8 %copy-start.9 = (bf16[2048,128]{1,0:T(8,128)(2,1)}, bf16[2048,128]{1,0:T(8,128)(2,1)S(1)}, u32[]{:S(2)}) copy-start(bf16[2048,128]{1,0:T(8,128)(2,1)S(1)} %collective-permute-done.6) | copy-start | bytes 1572868
  68.8 17.7 %collective-permute-start.4 = (bf16[4096,128]{1,0:T(8,128)(2,1)S(1)}, bf16[4096,128]{1,0:T(8,128)(2,1)S(1)}, u32[]{:S(2)}, u32[]{:S(2)}) collective-permute-start(bf16[4096,128]{1,0:T(8,128)(2,1)S(1)} %get-tuple-element.11), channel_id=1, source_target_pairs={{0,1},{1,0},{2,3},{3,2},{4,5},{5,4},{6,7},{7,6},{8,9},{9,8},{10,11... | collective-permute-start | bytes 3145736 | tf_op jit(solution)/shard_map/ppermute | solution.py:167
  70.6 17.9 %copy-start.10 = (bf16[2048,128]{1,0:T(8,128)(2,1)}, bf16[2048,128]{1,0:T(8,128)(2,1)S(1)}, u32[]{:S(2)}) copy-start(bf16[2048,128]{1,0:T(8,128)(2,1)S(1)} %collective-permute-done.9) | copy-start | bytes 1572868
  70.6 14.7 %collective-permute-start.2 = (bf16[2048,128]{1,0:T(8,128)(2,1)S(1)}, bf16[2048,128]{1,0:T(8,128)(2,1)S(1)}, u32[]{:S(2)}, u32[]{:S(2)}) collective-permute-start(bf16[2048,128]{1,0:T(8,128)(2,1)S(1)} %slice.8), channel_id=1, source_target_pairs={{0,4},{1,5},{2,6},{3,7},{4,8},{5,9},{6,10},{7,11},{8,12},{9,13},{1... | collective-permute-start | bytes 1572872 | tf_op jit(solution)/shard_map/ppermute | solution.py:167
  71.4 17.2 %copy-start.11 = (bf16[2048,128]{1,0:T(8,128)(2,1)}, bf16[2048,128]{1,0:T(8,128)(2,1)S(1)}, u32[]{:S(2)}) copy-start(bf16[2048,128]{1,0:T(8,128)(2,1)S(1)} %collective-permute-done.8) | copy-start | bytes 1572868
  71.4 14.0 %collective-permute-start.13 = (bf16[2048,128]{1,0:T(8,128)(2,1)S(1)}, bf16[2048,128]{1,0:T(8,128)(2,1)S(1)}, u32[]{:S(2)}, u32[]{:S(2)}) collective-permute-start(bf16[2048,128]{1,0:T(8,128)(2,1)S(1)} %collective-permute-done.9), channel_id=1, source_target_pairs={{0,96},{1,97},{2,98},{3,99},{4,100},{5,101},{6,102},{7,103},{8,104... | collective-permute-start | bytes 1572872 | tf_op jit(solution)/shard_map/ppermute | solution.py:167
  81.0 7.6 %copy-start.12 = (bf16[2048,128]{1,0:T(8,128)(2,1)}, bf16[2048,128]{1,0:T(8,128)(2,1)S(1)}, u32[]{:S(2)}) copy-start(bf16[2048,128]{1,0:T(8,128)(2,1)S(1)} %collective-permute-done.12) | copy-start | bytes 1572868
  81.0 5.5 %collective-permute-start.10 = (bf16[4096,128]{1,0:T(8,128)(2,1)S(1)}, bf16[4096,128]{1,0:T(8,128)(2,1)S(1)}, u32[]{:S(2)}, u32[]{:S(2)}) collective-permute-start(bf16[4096,128]{1,0:T(8,128)(2,1)S(1)} %collective-permute-done), channel_id=1, source_target_pairs={{0,1},{1,0},{2,3},{3,2},{4,5},{5,4},{6,7},{7,6},{8,9},{9,8},{10,11... | collective-permute-start | bytes 3145736 | tf_op jit(solution)/shard_map/ppermute | solution.py:167
  82.9 5.7 %copy-start.13 = (bf16[2048,128]{1,0:T(8,128)(2,1)}, bf16[2048,128]{1,0:T(8,128)(2,1)S(1)}, u32[]{:S(2)}) copy-start(bf16[2048,128]{1,0:T(8,128)(2,1)S(1)} %collective-permute-done.3) | copy-start | bytes 1572868
  82.9 3.8 %collective-permute-start.11 = (bf16[4096,128]{1,0:T(8,128)(2,1)S(1)}, bf16[4096,128]{1,0:T(8,128)(2,1)S(1)}, u32[]{:S(2)}, u32[]{:S(2)}) collective-permute-start(bf16[4096,128]{1,0:T(8,128)(2,1)S(1)} %collective-permute-done.1), channel_id=1, source_target_pairs={{0,1},{1,0},{2,3},{3,2},{4,5},{5,4},{6,7},{7,6},{8,9},{9,8},{10,11... | collective-permute-start | bytes 3145736 | tf_op jit(solution)/shard_map/ppermute | solution.py:167
  85.3 3.3 %copy-start.14 = (bf16[2048,128]{1,0:T(8,128)(2,1)}, bf16[2048,128]{1,0:T(8,128)(2,1)S(1)}, u32[]{:S(2)}) copy-start(bf16[2048,128]{1,0:T(8,128)(2,1)S(1)} %collective-permute-done.2) | copy-start | bytes 1572868
  85.3 3.3 %copy-start.15 = (bf16[2048,128]{1,0:T(8,128)(2,1)}, bf16[2048,128]{1,0:T(8,128)(2,1)S(1)}, u32[]{:S(2)}) copy-start(bf16[2048,128]{1,0:T(8,128)(2,1)S(1)} %collective-permute-done.13) | copy-start | bytes 1572868
  85.3 2.5 %collective-permute-start.14 = (bf16[2048,128]{1,0:T(8,128)(2,1)S(1)}, bf16[2048,128]{1,0:T(8,128)(2,1)S(1)}, u32[]{:S(2)}, u32[]{:S(2)}) collective-permute-start(bf16[2048,128]{1,0:T(8,128)(2,1)S(1)} %collective-permute-done.2), channel_id=1, source_target_pairs={{0,1},{1,0},{2,3},{3,2},{4,5},{5,4},{6,7},{7,6},{8,9},{9,8},{10,11... | collective-permute-start | bytes 1572872 | tf_op jit(solution)/shard_map/ppermute | solution.py:167
  86.3 2.3 %collective-permute-start.15 = (bf16[2048,128]{1,0:T(8,128)(2,1)S(1)}, bf16[2048,128]{1,0:T(8,128)(2,1)S(1)}, u32[]{:S(2)}, u32[]{:S(2)}) collective-permute-start(bf16[2048,128]{1,0:T(8,128)(2,1)S(1)} %collective-permute-done.3), channel_id=1, source_target_pairs={{0,1},{1,0},{2,3},{3,2},{4,5},{5,4},{6,7},{7,6},{8,9},{9,8},{10,11... | collective-permute-start | bytes 1572872 | tf_op jit(solution)/shard_map/ppermute | solution.py:167
  86.6 2.9 %copy-start.4 = (bf16[4096,128]{1,0:T(8,128)(2,1)}, bf16[4096,128]{1,0:T(8,128)(2,1)S(1)}, u32[]{:S(2)}) copy-start(bf16[4096,128]{1,0:T(8,128)(2,1)S(1)} %collective-permute-done.4) | copy-start | bytes 3145732
  86.6 2.9 %copy-start.5 = (bf16[4096,128]{1,0:T(8,128)(2,1)}, bf16[4096,128]{1,0:T(8,128)(2,1)S(1)}, u32[]{:S(2)}) copy-start(bf16[4096,128]{1,0:T(8,128)(2,1)S(1)} %collective-permute-done.10) | copy-start | bytes 3145732
  86.7 1.1 %copy-start.6 = (bf16[4096,128]{1,0:T(8,128)(2,1)}, bf16[4096,128]{1,0:T(8,128)(2,1)S(1)}, u32[]{:S(2)}) copy-start(bf16[4096,128]{1,0:T(8,128)(2,1)S(1)} %collective-permute-done.11) | copy-start | bytes 3145732
  (2 other events, 1.7 us)

commit v7 on v6

--- a/solution.py
+++ b/solution.py
@@ -16,7 +16,7 @@
 Y, XL, Z, XH, CORE = range(5)
 BF16, F32 = jnp.bfloat16, jnp.float32
 ROWS = 1024
-GROUP = 8
+GROUP = 16
 KC = 32
 OUT_BINS = 8
 XH_BIT = 2
@@ -260,7 +260,7 @@
             ],
         ),
         out_shape=jax.ShapeDtypeStruct((2, F, 256, 128), F32),
-        compiler_params=pltpu.CompilerParams(vmem_limit_bytes=58 << 20),
+        compiler_params=pltpu.CompilerParams(vmem_limit_bytes=36 << 20),
         name="product",
     )(wid, *arrays)
 

time: 99.9 us -> 96 us (0.961)
  Pallas kernels: 21.2 us -> 18.3 us
  local copies, waits for them, and re-layouts: 2.03 us -> 0.07 us
  waiting for transfers between devices: 31.9 us -> 33.5 us
    pallas_call x1, Pallas kernels: 10 us -> 7.23 us  [product(): pl.pallas_call(product_kernel, grid_spec=pltpu.PrefetchScalarGridSpec(num...]
    unnamed x36 -> x0, local copies, waits for them, and re-layouts: 1.96 us -> none
    ppermute x16, waiting for transfers between devices: 31.9 us -> 33.5 us  [shift(): lax.ppermute(x, AXES, [(int(a), int(b)) for a, b in zip(ids.ravel(), to.r...]
  transfers between devices with their start and end apart: 16 -> 16, of which waited for: 8 -> 9; matrix products, arithmetic and copies ran while one was open for 0% -> 0% of each run, Pallas kernels for 0% -> 0%
where the time goes in v7:
time: 96 us; the launch traced here: 95.7 us
  waiting for transfers between devices  33.5 us (35%)
  blocking collectives  30.7 us (32%)
  Pallas kernels  18.3 us (19%)
  starting transfers between devices  13 us (14%)
    ppermute x16, waiting for transfers between devices, shift(): lax.ppermute(x, AXES, [(int(a), int(b)) for a, b in zip(ids.ravel(), to.r...  33.5 us
    all_to_all x1, blocking collectives, body(): lax.all_to_all(spectra.reshape(NW, SENT, 2 * F), AXES, split_axis=0, conc...  30.7 us
    ppermute x16, starting transfers between devices, shift(): lax.ppermute(x, AXES, [(int(a), int(b)) for a, b in zip(ids.ravel(), to.r...  13 us
    pallas_call x1, Pallas kernels, whiten(): pl.pallas_call(whiten_kernel, grid_spec=pltpu.PrefetchScalarGridSpec(num_...  8.53 us
    pallas_call x1, Pallas kernels, product(): pl.pallas_call(product_kernel, grid_spec=pltpu.PrefetchScalarGridSpec(num...  7.23 us
    pallas_call x1, Pallas kernels, turn(): pl.pallas_call(turn_kernel, in_specs=[pl.BlockSpec(memory_space=pltpu.VME...  2.54 us
  transfers between devices with their start and end apart: 16, of which 9 were waited for; matrix products, arithmetic and copies ran while one was open for 0% of the time, Pallas kernels for 0%

profile of v7, /device:TPU:1, one launch (start us, length us, event | category | flops | bytes accessed | tf_op | source)
XLA Modules:
  0.0 95.7 jit_solution(12638125263579792286)
XLA Ops:
  0.0 8.5 %whiten.1 = bf16[4096,128]{1,0:T(8,128)(2,1)} custom-call(s32[2048]{0:T(1024)} %order.1, s32[4]{0:T(128)} %slab.1, s32[1]{0:T(128)} %bitcast.wid, bf16[1,2048,512]{2,1,0:T(8,128)(2,1)} %raw.1, s32[16,128]{1,0:T(8,128)} %bitcast.48, bf16[512,128]{1,0:T(8,128)(2,1)} %constant.13.clone.dft), custom_call_target="tpu_custom_call" | custom-call | tf_op jit(solution)/shard_map/whiten/pallas_call | solution.py:108
  8.5 30.7 %all_to_all.5 = bf16[128,32,128]{2,1,0:T(8,128)(2,1)S(1)} all-to-all(bf16[128,32,128]{2,1,0:T(8,128)(2,1)} %bitcast.47), channel_id=1, replica_groups=mesh['src'=8,'rcv'=16] {'src','rcv'}, dimensions={0} | all-to-all | bytes 2097152 | tf_op jit(solution)/shard_map/all_to_all | solution.py:272
  39.2 2.5 %turn.1 = (bf16[4096,128]{1,0:T(8,128)(2,1)S(1)}, bf16[2048,128]{1,0:T(8,128)(2,1)S(1)}) custom-call(bf16[4096,128]{1,0:T(8,128)(2,1)S(1)} %bitcast.34), custom_call_target="tpu_custom_call" | custom-call | tf_op jit(solution)/shard_map/turn/pallas_call | solution.py:150
  41.8 0.8 collective-permute-start.1
  42.5 0.8 collective-permute-start
  43.3 0.0 collective-permute-start.7
  43.3 0.4 collective-permute-start.5
  43.7 2.3 %collective-permute-start.6 = (bf16[2048,128]{1,0:T(8,128)(2,1)S(1)}, bf16[2048,128]{1,0:T(8,128)(2,1)S(1)}, u32[]{:S(2)}, u32[]{:S(2)}) collective-permute-start(bf16[2048,128]{1,0:T(8,128)(2,1)S(1)} %get-tuple-element.12), channel_id=1, source_target_pairs={{0,96},{1,97},{2,98},{3,99},{4,100},{5,101},{6,102},{7,103},{8,104... | collective-permute-start | bytes 1572872 | tf_op jit(solution)/shard_map/ppermute | solution.py:167
  46.0 9.3 %collective-permute-done.7 = bf16[2048,128]{1,0:T(8,128)(2,1)S(1)} collective-permute-done((bf16[2048,128]{1,0:T(8,128)(2,1)S(1)}, bf16[2048,128]{1,0:T(8,128)(2,1)S(1)}, u32[]{:S(2)}, u32[]{:S(2)}) %collective-permute-start.7) | collective-permute-done | bytes 524320 | tf_op jit(solution)/shard_map/ppermute | solution.py:167
  55.3 0.2 collective-permute-start.9
  55.5 0.5 collective-permute-done.5
  56.0 0.8 collective-permute-start.8
  56.8 8.9 %collective-permute-done.1 = bf16[4096,128]{1,0:T(8,128)(2,1)S(1)} collective-permute-done((bf16[4096,128]{1,0:T(8,128)(2,1)S(1)}, bf16[4096,128]{1,0:T(8,128)(2,1)S(1)}, u32[]{:S(2)}, u32[]{:S(2)}) %collective-permute-start.1) | collective-permute-done | bytes 1048608 | tf_op jit(solution)/shard_map/ppermute | solution.py:167
  65.7 0.0 collective-permute-start.12
  65.7 2.1 %collective-permute-done = bf16[4096,128]{1,0:T(8,128)(2,1)S(1)} collective-permute-done((bf16[4096,128]{1,0:T(8,128)(2,1)S(1)}, bf16[4096,128]{1,0:T(8,128)(2,1)S(1)}, u32[]{:S(2)}, u32[]{:S(2)}) %collective-permute-start) | collective-permute-done | bytes 1048608 | tf_op jit(solution)/shard_map/ppermute | solution.py:167
  67.8 0.8 collective-permute-start.3
  68.7 1.8 %collective-permute-start.4 = (bf16[4096,128]{1,0:T(8,128)(2,1)S(1)}, bf16[4096,128]{1,0:T(8,128)(2,1)S(1)}, u32[]{:S(2)}, u32[]{:S(2)}) collective-permute-start(bf16[4096,128]{1,0:T(8,128)(2,1)S(1)} %get-tuple-element.11), channel_id=1, source_target_pairs={{0,1},{1,0},{2,3},{3,2},{4,5},{5,4},{6,7},{7,6},{8,9},{9,8},{10,11... | collective-permute-start | bytes 3145736 | tf_op jit(solution)/shard_map/ppermute | solution.py:167
  70.5 0.0 collective-permute-done.9
  70.5 0.7 collective-permute-start.2
  71.2 1.7 %collective-permute-start.13 = (bf16[2048,128]{1,0:T(8,128)(2,1)S(1)}, bf16[2048,128]{1,0:T(8,128)(2,1)S(1)}, u32[]{:S(2)}, u32[]{:S(2)}) collective-permute-start(bf16[2048,128]{1,0:T(8,128)(2,1)S(1)} %collective-permute-done.9), channel_id=1, source_target_pairs={{0,96},{1,97},{2,98},{3,99},{4,100},{5,101},{6,102},{7,103},{8,104... | collective-permute-start | bytes 1572872 | tf_op jit(solution)/shard_map/ppermute | solution.py:167
  72.9 8.0 %collective-permute-done.12 = bf16[2048,128]{1,0:T(8,128)(2,1)S(1)} collective-permute-done((bf16[2048,128]{1,0:T(8,128)(2,1)S(1)}, bf16[2048,128]{1,0:T(8,128)(2,1)S(1)}, u32[]{:S(2)}, u32[]{:S(2)}) %collective-permute-start.12) | collective-permute-done | bytes 524320 | tf_op jit(solution)/shard_map/ppermute | solution.py:167
  80.9 1.9 %collective-permute-start.10 = (bf16[4096,128]{1,0:T(8,128)(2,1)S(1)}, bf16[4096,128]{1,0:T(8,128)(2,1)S(1)}, u32[]{:S(2)}, u32[]{:S(2)}) collective-permute-start(bf16[4096,128]{1,0:T(8,128)(2,1)S(1)} %collective-permute-done), channel_id=1, source_target_pairs={{0,1},{1,0},{2,3},{3,2},{4,5},{5,4},{6,7},{7,6},{8,9},{9,8},{10,11... | collective-permute-start | bytes 3145736 | tf_op jit(solution)/shard_map/ppermute | solution.py:167
  82.8 0.0 collective-permute-start.11
  82.8 2.4 %collective-permute-done.2 = bf16[2048,128]{1,0:T(8,128)(2,1)S(1)} collective-permute-done((bf16[2048,128]{1,0:T(8,128)(2,1)S(1)}, bf16[2048,128]{1,0:T(8,128)(2,1)S(1)}, u32[]{:S(2)}, u32[]{:S(2)}) %collective-permute-start.2) | collective-permute-done | bytes 524320 | tf_op jit(solution)/shard_map/ppermute | solution.py:167
  85.2 0.9 collective-permute-start.14
  86.0 0.0 collective-permute-start.15
  86.1 0.0 collective-permute-done.4
  86.1 0.0 collective-permute-done.10
  86.1 0.5 collective-permute-done.11
  86.6 1.0 %collective-permute-done.14 = bf16[2048,128]{1,0:T(8,128)(2,1)S(1)} collective-permute-done((bf16[2048,128]{1,0:T(8,128)(2,1)S(1)}, bf16[2048,128]{1,0:T(8,128)(2,1)S(1)}, u32[]{:S(2)}, u32[]{:S(2)}) %collective-permute-start.14) | collective-permute-done | bytes 524320 | tf_op jit(solution)/shard_map/ppermute | solution.py:167
  87.6 0.7 collective-permute-done.15
  88.3 7.2 %product.1 = f32[2,64,256,128]{3,2,1,0:T(8,128)} custom-call(s32[1]{0:T(128)} %bitcast.wid, bf16[128,32,128]{2,1,0:T(8,128)(2,1)S(1)} %bitcast.26, bf16[128,32,128]{2,1,0:T(8,128)(2,1)S(1)} %bitcast.27, bf16[128,32,128]{2,1,0:T(8,128)(2,1)S(1)} %bitcast.24, bf16[128,32,128]{2,1,0:T(8,128)(2,1)S(1)} %bitcast.25, bf16[128,32,128]{2,1,0:T(8,128)(2,1)S(1)} %bitcast.22, ...), custom_call_target="tpu_custom_call" | custom-call | tf_op jit(solution)/shard_map/product/pallas_call | solution.py:249
  (6 shorter events, 0.1 us)
Async XLA Ops:
  41.8 23.9 %collective-permute-start.1 = (bf16[4096,128]{1,0:T(8,128)(2,1)S(1)}, bf16[4096,128]{1,0:T(8,128)(2,1)S(1)}, u32[]{:S(2)}, u32[]{:S(2)}) collective-permute-start(bf16[4096,128]{1,0:T(8,128)(2,1)S(1)} %get-tuple-element.11), channel_id=1, source_target_pairs={{0,12},{1,13},{2,14},{3,15},{4,0},{5,1},{6,2},{7,3},{8,4},{9,5},{1... | collective-permute-start | bytes 3145736 | tf_op jit(solution)/shard_map/ppermute | solution.py:167
  42.5 25.3 %collective-permute-start = (bf16[4096,128]{1,0:T(8,128)(2,1)S(1)}, bf16[4096,128]{1,0:T(8,128)(2,1)S(1)}, u32[]{:S(2)}, u32[]{:S(2)}) collective-permute-start(bf16[4096,128]{1,0:T(8,128)(2,1)S(1)} %get-tuple-element.11), channel_id=1, source_target_pairs={{0,4},{1,5},{2,6},{3,7},{4,8},{5,9},{6,10},{7,11},{8,12},{9,13},{1... | collective-permute-start | bytes 3145736 | tf_op jit(solution)/shard_map/ppermute | solution.py:167
  43.3 12.0 %collective-permute-start.7 = (bf16[2048,128]{1,0:T(8,128)(2,1)S(1)}, bf16[2048,128]{1,0:T(8,128)(2,1)S(1)}, u32[]{:S(2)}, u32[]{:S(2)}) collective-permute-start(bf16[2048,128]{1,0:T(8,128)(2,1)S(1)} %get-tuple-element.12), channel_id=1, source_target_pairs={{0,16},{1,17},{2,18},{3,19},{4,20},{5,21},{6,22},{7,23},{8,24},{9,... | collective-permute-start | bytes 1572872 | tf_op jit(solution)/shard_map/ppermute | solution.py:167
  43.3 12.7 %collective-permute-start.5 = (bf16[2048,128]{1,0:T(8,128)(2,1)S(1)}, bf16[2048,128]{1,0:T(8,128)(2,1)S(1)}, u32[]{:S(2)}, u32[]{:S(2)}) collective-permute-start(bf16[2048,128]{1,0:T(8,128)(2,1)S(1)} %get-tuple-element.12), channel_id=1, source_target_pairs={{0,32},{1,33},{2,34},{3,35},{4,36},{5,37},{6,38},{7,39},{8,40},{9,... | collective-permute-start | bytes 1572872 | tf_op jit(solution)/shard_map/ppermute | solution.py:167
  43.7 25.0 %collective-permute-start.6 = (bf16[2048,128]{1,0:T(8,128)(2,1)S(1)}, bf16[2048,128]{1,0:T(8,128)(2,1)S(1)}, u32[]{:S(2)}, u32[]{:S(2)}) collective-permute-start(bf16[2048,128]{1,0:T(8,128)(2,1)S(1)} %get-tuple-element.12), channel_id=1, source_target_pairs={{0,96},{1,97},{2,98},{3,99},{4,100},{5,101},{6,102},{7,103},{8,104... | collective-permute-start | bytes 1572872 | tf_op jit(solution)/shard_map/ppermute | solution.py:167
  55.3 15.1 %collective-permute-start.9 = (bf16[2048,128]{1,0:T(8,128)(2,1)S(1)}, bf16[2048,128]{1,0:T(8,128)(2,1)S(1)}, u32[]{:S(2)}, u32[]{:S(2)}) collective-permute-start(bf16[2048,128]{1,0:T(8,128)(2,1)S(1)} %collective-permute-done.7), channel_id=1, source_target_pairs={{0,96},{1,97},{2,98},{3,99},{4,100},{5,101},{6,102},{7,103},{8,104... | collective-permute-start | bytes 1572872 | tf_op jit(solution)/shard_map/ppermute | solution.py:167
  56.0 15.2 %collective-permute-start.8 = (bf16[2048,128]{1,0:T(8,128)(2,1)S(1)}, bf16[2048,128]{1,0:T(8,128)(2,1)S(1)}, u32[]{:S(2)}, u32[]{:S(2)}) collective-permute-start(bf16[2048,128]{1,0:T(8,128)(2,1)S(1)} %collective-permute-done.7), channel_id=1, source_target_pairs={{0,32},{1,33},{2,34},{3,35},{4,36},{5,37},{6,38},{7,39},{8,40},{9,... | collective-permute-start | bytes 1572872 | tf_op jit(solution)/shard_map/ppermute | solution.py:167
  65.7 15.2 %collective-permute-start.12 = (bf16[2048,128]{1,0:T(8,128)(2,1)S(1)}, bf16[2048,128]{1,0:T(8,128)(2,1)S(1)}, u32[]{:S(2)}, u32[]{:S(2)}) collective-permute-start(bf16[2048,128]{1,0:T(8,128)(2,1)S(1)} %collective-permute-done.5), channel_id=1, source_target_pairs={{0,32},{1,33},{2,34},{3,35},{4,36},{5,37},{6,38},{7,39},{8,40},{9,... | collective-permute-start | bytes 1572872 | tf_op jit(solution)/shard_map/ppermute | solution.py:167
  67.8 15.0 %collective-permute-start.3 = (bf16[2048,128]{1,0:T(8,128)(2,1)S(1)}, bf16[2048,128]{1,0:T(8,128)(2,1)S(1)}, u32[]{:S(2)}, u32[]{:S(2)}) collective-permute-start(bf16[2048,128]{1,0:T(8,128)(2,1)S(1)} %slice.9), channel_id=1, source_target_pairs={{0,12},{1,13},{2,14},{3,15},{4,0},{5,1},{6,2},{7,3},{8,4},{9,5},{1... | collective-permute-start | bytes 1572872 | tf_op jit(solution)/shard_map/ppermute | solution.py:167
  68.7 17.4 %collective-permute-start.4 = (bf16[4096,128]{1,0:T(8,128)(2,1)S(1)}, bf16[4096,128]{1,0:T(8,128)(2,1)S(1)}, u32[]{:S(2)}, u32[]{:S(2)}) collective-permute-start(bf16[4096,128]{1,0:T(8,128)(2,1)S(1)} %get-tuple-element.11), channel_id=1, source_target_pairs={{0,1},{1,0},{2,3},{3,2},{4,5},{5,4},{6,7},{7,6},{8,9},{9,8},{10,11... | collective-permute-start | bytes 3145736 | tf_op jit(solution)/shard_map/ppermute | solution.py:167
  70.5 14.7 %collective-permute-start.2 = (bf16[2048,128]{1,0:T(8,128)(2,1)S(1)}, bf16[2048,128]{1,0:T(8,128)(2,1)S(1)}, u32[]{:S(2)}, u32[]{:S(2)}) collective-permute-start(bf16[2048,128]{1,0:T(8,128)(2,1)S(1)} %slice.8), channel_id=1, source_target_pairs={{0,4},{1,5},{2,6},{3,7},{4,8},{5,9},{6,10},{7,11},{8,12},{9,13},{1... | collective-permute-start | bytes 1572872 | tf_op jit(solution)/shard_map/ppermute | solution.py:167
  71.2 14.0 %collective-permute-start.13 = (bf16[2048,128]{1,0:T(8,128)(2,1)S(1)}, bf16[2048,128]{1,0:T(8,128)(2,1)S(1)}, u32[]{:S(2)}, u32[]{:S(2)}) collective-permute-start(bf16[2048,128]{1,0:T(8,128)(2,1)S(1)} %collective-permute-done.9), channel_id=1, source_target_pairs={{0,96},{1,97},{2,98},{3,99},{4,100},{5,101},{6,102},{7,103},{8,104... | collective-permute-start | bytes 1572872 | tf_op jit(solution)/shard_map/ppermute | solution.py:167
  80.9 5.2 %collective-permute-start.10 = (bf16[4096,128]{1,0:T(8,128)(2,1)S(1)}, bf16[4096,128]{1,0:T(8,128)(2,1)S(1)}, u32[]{:S(2)}, u32[]{:S(2)}) collective-permute-start(bf16[4096,128]{1,0:T(8,128)(2,1)S(1)} %collective-permute-done), channel_id=1, source_target_pairs={{0,1},{1,0},{2,3},{3,2},{4,5},{5,4},{6,7},{7,6},{8,9},{9,8},{10,11... | collective-permute-start | bytes 3145736 | tf_op jit(solution)/shard_map/ppermute | solution.py:167
  82.8 3.8 %collective-permute-start.11 = (bf16[4096,128]{1,0:T(8,128)(2,1)S(1)}, bf16[4096,128]{1,0:T(8,128)(2,1)S(1)}, u32[]{:S(2)}, u32[]{:S(2)}) collective-permute-start(bf16[4096,128]{1,0:T(8,128)(2,1)S(1)} %collective-permute-done.1), channel_id=1, source_target_pairs={{0,1},{1,0},{2,3},{3,2},{4,5},{5,4},{6,7},{7,6},{8,9},{9,8},{10,11... | collective-permute-start | bytes 3145736 | tf_op jit(solution)/shard_map/ppermute | solution.py:167
  85.2 2.4 %collective-permute-start.14 = (bf16[2048,128]{1,0:T(8,128)(2,1)S(1)}, bf16[2048,128]{1,0:T(8,128)(2,1)S(1)}, u32[]{:S(2)}, u32[]{:S(2)}) collective-permute-start(bf16[2048,128]{1,0:T(8,128)(2,1)S(1)} %collective-permute-done.2), channel_id=1, source_target_pairs={{0,1},{1,0},{2,3},{3,2},{4,5},{5,4},{6,7},{7,6},{8,9},{9,8},{10,11... | collective-permute-start | bytes 1572872 | tf_op jit(solution)/shard_map/ppermute | solution.py:167
  86.0 2.3 %collective-permute-start.15 = (bf16[2048,128]{1,0:T(8,128)(2,1)S(1)}, bf16[2048,128]{1,0:T(8,128)(2,1)S(1)}, u32[]{:S(2)}, u32[]{:S(2)}) collective-permute-start(bf16[2048,128]{1,0:T(8,128)(2,1)S(1)} %collective-permute-done.3), channel_id=1, source_target_pairs={{0,1},{1,0},{2,3},{3,2},{4,5},{5,4},{6,7},{7,6},{8,9},{9,8},{10,11... | collective-permute-start | bytes 1572872 | tf_op jit(solution)/shard_map/ppermute | solution.py:167

commit v8 on v5

--- a/solution.py
+++ b/solution.py
@@ -16,8 +16,9 @@
 Y, XL, Z, XH, CORE = range(5)
 BF16, F32 = jnp.bfloat16, jnp.float32
 ROWS = 1024
-GROUP = 8
-KC = 32
+GROUP = 16
+KC = 64
+OUT_BINS = 8
 XH_BIT = 2
 SENT = 2 * CB
 HALF_ROWS = F * 2 * CB
@@ -193,51 +194,72 @@
 
 
 def product_kernel(wid, *refs):
-    rows, cols, (out, b) = refs[:16], refs[16:24], refs[24:]
+    blocks, (out, b, made, sent) = refs[:-4], refs[-4:]
+    sides = [
+        (block, half * F) for block in blocks for half in range(block.shape[0] // F)
+    ]
+    rows, cols = sides[:16], sides[16:]
+    chunks = KC // OUT_BINS
     offsets = [pl.multiple_of(at, CB) for at in block_offsets(wid[0])]
-    for block, offset in zip(cols, offsets[16:]):
-        re, im = block[:, 0:CB, :], block[:, CB : 2 * CB, :]
-        b[:, pl.ds(offset, CB), 0:NW] = re
-        b[:, pl.ds(offset, CB), NW : 2 * NW] = im
-        b[:, pl.ds(128 + offset, CB), 0:NW] = -im
-        b[:, pl.ds(128 + offset, CB), NW : 2 * NW] = re
     factor = 1.0 / math.sqrt(NW)
-    for k in range(KC):
-        halves = [
-            jnp.concatenate([row[k, 0:CB, :], row[k, CB : 2 * CB, :]], axis=1) for row in rows
-        ]
-        o = lax.dot_general(
-            jnp.concatenate(halves, axis=0),
-            b[k],
-            (((1,), (1,)), ((), ())),
-            preferred_element_type=F32,
+
+    def send(slot, at):
+        first = pl.multiple_of(at * KC + slot * OUT_BINS, OUT_BINS)
+        return pltpu.make_async_copy(
+            made.at[slot], out.at[:, pl.ds(first, OUT_BINS)], sent.at[slot]
         )
-        o = o * factor
-        for index, offset in enumerate(offsets[:16]):
-            part = o[index * CB : (index + 1) * CB]
-            out[0, k, pl.ds(offset, CB), :] = part[:, :128]
-            out[1, k, pl.ds(offset, CB), :] = part[:, 128:]
+
+    def some_bins(step, carry):
+        first = step * KC
+        for slot in range(chunks):
+            for (block, base), offset in zip(cols, offsets[16:]):
+                held = block[pl.ds(base + first + slot * OUT_BINS, OUT_BINS)]
+                re, im = held[:, 0:CB, :], held[:, CB : 2 * CB, :]
+                b[slot, :, pl.ds(offset, CB), 0:NW] = re
+                b[slot, :, pl.ds(offset, CB), NW : 2 * NW] = im
+                b[slot, :, pl.ds(128 + offset, CB), 0:NW] = -im
+                b[slot, :, pl.ds(128 + offset, CB), NW : 2 * NW] = re
+            for bin_index in range(OUT_BINS):
+                k = slot * OUT_BINS + bin_index
+                parts = []
+                for block, base in rows:
+                    held = block[base + first + k]
+                    parts.append(jnp.concatenate([held[0:CB], held[CB : 2 * CB]], axis=1))
+                o = lax.dot_general(
+                    jnp.concatenate(parts, axis=0),
+                    b[slot, bin_index],
+                    (((1,), (1,)), ((), ())),
+                    preferred_element_type=F32,
+                )
+                o = o * factor
+                for index, offset in enumerate(offsets[:16]):
+                    part = o[index * CB : (index + 1) * CB]
+                    made[slot, 0, bin_index, pl.ds(offset, CB), :] = part[:, :128]
+                    made[slot, 1, bin_index, pl.ds(offset, CB), :] = part[:, 128:]
+            send(slot, step).start()
+        return carry
+
+    some_bins(0, 0)
+    for slot in range(chunks):
+        send(slot, F // KC - 1).wait()
 
 
 def product(wid, blocks):
-    steps = F // KC
-    arrays, specs = [], []
-    for block in blocks:
-        for half in range(block.shape[0] // HALF_ROWS):
-            arrays.append(block.reshape(-1, 2 * CB, NW))
-            index_map = lambda i, m, half=half: (i + half * steps, 0, 0)
-            specs.append(pl.BlockSpec((KC, 2 * CB, NW), index_map))
+    arrays = [block.reshape(-1, 2 * CB, NW) for block in blocks]
     return pl.pallas_call(
         product_kernel,
-        grid_spec=pltpu.PrefetchScalarGridSpec(
-            num_scalar_prefetch=1,
-            grid=(steps,),
-            in_specs=specs,
-            out_specs=pl.BlockSpec((2, KC, 256, 128), lambda i, m: (0, i, 0, 0)),
-            scratch_shapes=[pltpu.VMEM((KC, 256, 256), BF16)],
-        ),
+        in_specs=[
+            pl.BlockSpec(memory_space=pltpu.SMEM),
+            *[pl.BlockSpec(memory_space=pltpu.VMEM) for _ in arrays],
+        ],
+        out_specs=pl.BlockSpec(memory_space=pl.ANY),
+        scratch_shapes=[
+            pltpu.VMEM((KC // OUT_BINS, OUT_BINS, 256, 256), BF16),
+            pltpu.VMEM((KC // OUT_BINS, 2, OUT_BINS, 256, 128), F32),
+            pltpu.SemaphoreType.DMA((KC // OUT_BINS,)),
+        ],
         out_shape=jax.ShapeDtypeStruct((2, F, 256, 128), F32),
-        compiler_params=pltpu.CompilerParams(vmem_limit_bytes=58 << 20),
+        compiler_params=pltpu.CompilerParams(vmem_limit_bytes=36 << 20),
         name="product",
     )(wid, *arrays)
 

time: 101 us -> 95.6 us (0.947)
  Pallas kernels: 22.4 us -> 17.9 us
  local copies, waits for them, and re-layouts: 2.03 us -> 0.07 us
  waiting for transfers between devices: 31.9 us -> 33.5 us
    pallas_call x1, Pallas kernels: 11.2 us -> 6.83 us  [product(): pl.pallas_call(product_kernel, in_specs=[pl.BlockSpec(memory_space=pltpu....]
    unnamed x36 -> x0, local copies, waits for them, and re-layouts: 1.96 us -> none
    ppermute x16, waiting for transfers between devices: 31.9 us -> 33.5 us  [shift(): lax.ppermute(x, AXES, [(int(a), int(b)) for a, b in zip(ids.ravel(), to.r...]
  transfers between devices with their start and end apart: 16 -> 16, of which waited for: 8 -> 9; matrix products, arithmetic and copies ran while one was open for 0% -> 0% of each run, Pallas kernels for 0% -> 0%
where the time goes in v8:
time: 95.6 us; the launch traced here: 95.3 us
  waiting for transfers between devices  33.5 us (35%)
  blocking collectives  30.7 us (32%)
  Pallas kernels  17.9 us (19%)
  starting transfers between devices  13 us (14%)
    ppermute x16, waiting for transfers between devices, shift(): lax.ppermute(x, AXES, [(int(a), int(b)) for a, b in zip(ids.ravel(), to.r...  33.5 us
    all_to_all x1, blocking collectives, body(): lax.all_to_all(spectra.reshape(NW, SENT, 2 * F), AXES, split_axis=0, conc...  30.7 us
    ppermute x16, starting transfers between devices, shift(): lax.ppermute(x, AXES, [(int(a), int(b)) for a, b in zip(ids.ravel(), to.r...  13 us
    pallas_call x1, Pallas kernels, whiten(): pl.pallas_call(whiten_kernel, grid_spec=pltpu.PrefetchScalarGridSpec(num_...  8.53 us
    pallas_call x1, Pallas kernels, product(): pl.pallas_call(product_kernel, in_specs=[pl.BlockSpec(memory_space=pltpu....  6.83 us
    pallas_call x1, Pallas kernels, turn(): pl.pallas_call(turn_kernel, in_specs=[pl.BlockSpec(memory_space=pltpu.VME...  2.54 us
  transfers between devices with their start and end apart: 16, of which 9 were waited for; matrix products, arithmetic and copies ran while one was open for 0% of the time, Pallas kernels for 0%

profile of v8, /device:TPU:1, one launch (start us, length us, event | category | flops | bytes accessed | tf_op | source)
XLA Modules:
  0.0 95.3 jit_solution(12839912984395566736)
XLA Ops:
  0.0 8.5 %whiten.1 = bf16[4096,128]{1,0:T(8,128)(2,1)} custom-call(s32[2048]{0:T(1024)} %order.1, s32[4]{0:T(128)} %slab.1, s32[1]{0:T(128)} %bitcast.wid, bf16[1,2048,512]{2,1,0:T(8,128)(2,1)} %raw.1, s32[16,128]{1,0:T(8,128)} %bitcast.42, bf16[512,128]{1,0:T(8,128)(2,1)} %constant.13.clone.dft), custom_call_target="tpu_custom_call" | custom-call | tf_op jit(solution)/shard_map/whiten/pallas_call | solution.py:108
  8.5 30.7 %all_to_all.5 = bf16[128,32,128]{2,1,0:T(8,128)(2,1)S(1)} all-to-all(bf16[128,32,128]{2,1,0:T(8,128)(2,1)} %bitcast.41), channel_id=1, replica_groups=mesh['src'=8,'rcv'=16] {'src','rcv'}, dimensions={0} | all-to-all | bytes 2097152 | tf_op jit(solution)/shard_map/all_to_all | solution.py:271
  39.2 2.5 %turn.1 = (bf16[4096,128]{1,0:T(8,128)(2,1)S(1)}, bf16[2048,128]{1,0:T(8,128)(2,1)S(1)}) custom-call(bf16[4096,128]{1,0:T(8,128)(2,1)S(1)} %bitcast.22), custom_call_target="tpu_custom_call" | custom-call | tf_op jit(solution)/shard_map/turn/pallas_call | solution.py:150
  41.8 0.8 collective-permute-start.1
  42.5 0.8 collective-permute-start
  43.3 0.0 collective-permute-start.7
  43.3 0.4 collective-permute-start.5
  43.7 2.3 %collective-permute-start.6 = (bf16[2048,128]{1,0:T(8,128)(2,1)S(1)}, bf16[2048,128]{1,0:T(8,128)(2,1)S(1)}, u32[]{:S(2)}, u32[]{:S(2)}) collective-permute-start(bf16[2048,128]{1,0:T(8,128)(2,1)S(1)} %get-tuple-element.12), channel_id=1, source_target_pairs={{0,96},{1,97},{2,98},{3,99},{4,100},{5,101},{6,102},{7,103},{8,104... | collective-permute-start | bytes 1572872 | tf_op jit(solution)/shard_map/ppermute | solution.py:167
  46.0 9.3 %collective-permute-done.7 = bf16[2048,128]{1,0:T(8,128)(2,1)S(1)} collective-permute-done((bf16[2048,128]{1,0:T(8,128)(2,1)S(1)}, bf16[2048,128]{1,0:T(8,128)(2,1)S(1)}, u32[]{:S(2)}, u32[]{:S(2)}) %collective-permute-start.7) | collective-permute-done | bytes 524320 | tf_op jit(solution)/shard_map/ppermute | solution.py:167
  55.3 0.2 collective-permute-start.9
  55.5 0.5 collective-permute-done.5
  56.0 0.8 collective-permute-start.8
  56.8 8.9 %collective-permute-done.1 = bf16[4096,128]{1,0:T(8,128)(2,1)S(1)} collective-permute-done((bf16[4096,128]{1,0:T(8,128)(2,1)S(1)}, bf16[4096,128]{1,0:T(8,128)(2,1)S(1)}, u32[]{:S(2)}, u32[]{:S(2)}) %collective-permute-start.1) | collective-permute-done | bytes 1048608 | tf_op jit(solution)/shard_map/ppermute | solution.py:167
  65.7 0.0 collective-permute-start.12
  65.7 2.1 %collective-permute-done = bf16[4096,128]{1,0:T(8,128)(2,1)S(1)} collective-permute-done((bf16[4096,128]{1,0:T(8,128)(2,1)S(1)}, bf16[4096,128]{1,0:T(8,128)(2,1)S(1)}, u32[]{:S(2)}, u32[]{:S(2)}) %collective-permute-start) | collective-permute-done | bytes 1048608 | tf_op jit(solution)/shard_map/ppermute | solution.py:167
  67.8 0.8 collective-permute-start.3
  68.7 0.0 collective-permute-done.6
  68.7 1.8 %collective-permute-start.4 = (bf16[4096,128]{1,0:T(8,128)(2,1)S(1)}, bf16[4096,128]{1,0:T(8,128)(2,1)S(1)}, u32[]{:S(2)}, u32[]{:S(2)}) collective-permute-start(bf16[4096,128]{1,0:T(8,128)(2,1)S(1)} %get-tuple-element.11), channel_id=1, source_target_pairs={{0,1},{1,0},{2,3},{3,2},{4,5},{5,4},{6,7},{7,6},{8,9},{9,8},{10,11... | collective-permute-start | bytes 3145736 | tf_op jit(solution)/shard_map/ppermute | solution.py:167
  70.5 0.7 collective-permute-start.2
  71.2 0.0 collective-permute-done.8
  71.2 1.7 %collective-permute-start.13 = (bf16[2048,128]{1,0:T(8,128)(2,1)S(1)}, bf16[2048,128]{1,0:T(8,128)(2,1)S(1)}, u32[]{:S(2)}, u32[]{:S(2)}) collective-permute-start(bf16[2048,128]{1,0:T(8,128)(2,1)S(1)} %collective-permute-done.9), channel_id=1, source_target_pairs={{0,96},{1,97},{2,98},{3,99},{4,100},{5,101},{6,102},{7,103},{8,104... | collective-permute-start | bytes 1572872 | tf_op jit(solution)/shard_map/ppermute | solution.py:167
  72.9 8.0 %collective-permute-done.12 = bf16[2048,128]{1,0:T(8,128)(2,1)S(1)} collective-permute-done((bf16[2048,128]{1,0:T(8,128)(2,1)S(1)}, bf16[2048,128]{1,0:T(8,128)(2,1)S(1)}, u32[]{:S(2)}, u32[]{:S(2)}) %collective-permute-start.12) | collective-permute-done | bytes 524320 | tf_op jit(solution)/shard_map/ppermute | solution.py:167
  80.9 1.9 %collective-permute-start.10 = (bf16[4096,128]{1,0:T(8,128)(2,1)S(1)}, bf16[4096,128]{1,0:T(8,128)(2,1)S(1)}, u32[]{:S(2)}, u32[]{:S(2)}) collective-permute-start(bf16[4096,128]{1,0:T(8,128)(2,1)S(1)} %collective-permute-done), channel_id=1, source_target_pairs={{0,1},{1,0},{2,3},{3,2},{4,5},{5,4},{6,7},{7,6},{8,9},{9,8},{10,11... | collective-permute-start | bytes 3145736 | tf_op jit(solution)/shard_map/ppermute | solution.py:167
  82.8 0.0 collective-permute-done.3
  82.8 0.0 collective-permute-start.11
  82.8 2.4 %collective-permute-done.2 = bf16[2048,128]{1,0:T(8,128)(2,1)S(1)} collective-permute-done((bf16[2048,128]{1,0:T(8,128)(2,1)S(1)}, bf16[2048,128]{1,0:T(8,128)(2,1)S(1)}, u32[]{:S(2)}, u32[]{:S(2)}) %collective-permute-start.2) | collective-permute-done | bytes 524320 | tf_op jit(solution)/shard_map/ppermute | solution.py:167
  85.2 0.9 collective-permute-start.14
  86.0 0.0 collective-permute-start.15
  86.1 0.5 collective-permute-done.11
  86.6 1.0 %collective-permute-done.14 = bf16[2048,128]{1,0:T(8,128)(2,1)S(1)} collective-permute-done((bf16[2048,128]{1,0:T(8,128)(2,1)S(1)}, bf16[2048,128]{1,0:T(8,128)(2,1)S(1)}, u32[]{:S(2)}, u32[]{:S(2)}) %collective-permute-start.14) | collective-permute-done | bytes 524320 | tf_op jit(solution)/shard_map/ppermute | solution.py:167
  87.6 0.7 collective-permute-done.15
  88.3 6.8 %product.1 = f32[2,64,256,128]{3,2,1,0:T(8,128)} custom-call(s32[1]{0:T(128)} %bitcast.wid, bf16[128,32,128]{2,1,0:T(8,128)(2,1)S(1)} %bitcast.25, bf16[128,32,128]{2,1,0:T(8,128)(2,1)S(1)} %bitcast.24, bf16[128,32,128]{2,1,0:T(8,128)(2,1)S(1)} %bitcast.23, bf16[64,32,128]{2,1,0:T(8,128)(2,1)S(1)} %bitcast.37, bf16[64,32,128]{2,1,0:T(8,128)(2,1)S(1)} %bitcast.36, ...), custom_call_target="tpu_custom_call" | custom-call | tf_op jit(solution)/shard_map/product/pallas_call | solution.py:249
  (6 shorter events, 0.1 us)
Async XLA Ops:
  41.8 23.9 %collective-permute-start.1 = (bf16[4096,128]{1,0:T(8,128)(2,1)S(1)}, bf16[4096,128]{1,0:T(8,128)(2,1)S(1)}, u32[]{:S(2)}, u32[]{:S(2)}) collective-permute-start(bf16[4096,128]{1,0:T(8,128)(2,1)S(1)} %get-tuple-element.11), channel_id=1, source_target_pairs={{0,12},{1,13},{2,14},{3,15},{4,0},{5,1},{6,2},{7,3},{8,4},{9,5},{1... | collective-permute-start | bytes 3145736 | tf_op jit(solution)/shard_map/ppermute | solution.py:167
  42.5 25.3 %collective-permute-start = (bf16[4096,128]{1,0:T(8,128)(2,1)S(1)}, bf16[4096,128]{1,0:T(8,128)(2,1)S(1)}, u32[]{:S(2)}, u32[]{:S(2)}) collective-permute-start(bf16[4096,128]{1,0:T(8,128)(2,1)S(1)} %get-tuple-element.11), channel_id=1, source_target_pairs={{0,4},{1,5},{2,6},{3,7},{4,8},{5,9},{6,10},{7,11},{8,12},{9,13},{1... | collective-permute-start | bytes 3145736 | tf_op jit(solution)/shard_map/ppermute | solution.py:167
  43.3 12.0 %collective-permute-start.7 = (bf16[2048,128]{1,0:T(8,128)(2,1)S(1)}, bf16[2048,128]{1,0:T(8,128)(2,1)S(1)}, u32[]{:S(2)}, u32[]{:S(2)}) collective-permute-start(bf16[2048,128]{1,0:T(8,128)(2,1)S(1)} %get-tuple-element.12), channel_id=1, source_target_pairs={{0,16},{1,17},{2,18},{3,19},{4,20},{5,21},{6,22},{7,23},{8,24},{9,... | collective-permute-start | bytes 1572872 | tf_op jit(solution)/shard_map/ppermute | solution.py:167
  43.3 12.7 %collective-permute-start.5 = (bf16[2048,128]{1,0:T(8,128)(2,1)S(1)}, bf16[2048,128]{1,0:T(8,128)(2,1)S(1)}, u32[]{:S(2)}, u32[]{:S(2)}) collective-permute-start(bf16[2048,128]{1,0:T(8,128)(2,1)S(1)} %get-tuple-element.12), channel_id=1, source_target_pairs={{0,32},{1,33},{2,34},{3,35},{4,36},{5,37},{6,38},{7,39},{8,40},{9,... | collective-permute-start | bytes 1572872 | tf_op jit(solution)/shard_map/ppermute | solution.py:167
  43.7 25.0 %collective-permute-start.6 = (bf16[2048,128]{1,0:T(8,128)(2,1)S(1)}, bf16[2048,128]{1,0:T(8,128)(2,1)S(1)}, u32[]{:S(2)}, u32[]{:S(2)}) collective-permute-start(bf16[2048,128]{1,0:T(8,128)(2,1)S(1)} %get-tuple-element.12), channel_id=1, source_target_pairs={{0,96},{1,97},{2,98},{3,99},{4,100},{5,101},{6,102},{7,103},{8,104... | collective-permute-start | bytes 1572872 | tf_op jit(solution)/shard_map/ppermute | solution.py:167
  55.3 15.1 %collective-permute-start.9 = (bf16[2048,128]{1,0:T(8,128)(2,1)S(1)}, bf16[2048,128]{1,0:T(8,128)(2,1)S(1)}, u32[]{:S(2)}, u32[]{:S(2)}) collective-permute-start(bf16[2048,128]{1,0:T(8,128)(2,1)S(1)} %collective-permute-done.7), channel_id=1, source_target_pairs={{0,96},{1,97},{2,98},{3,99},{4,100},{5,101},{6,102},{7,103},{8,104... | collective-permute-start | bytes 1572872 | tf_op jit(solution)/shard_map/ppermute | solution.py:167
  56.0 15.2 %collective-permute-start.8 = (bf16[2048,128]{1,0:T(8,128)(2,1)S(1)}, bf16[2048,128]{1,0:T(8,128)(2,1)S(1)}, u32[]{:S(2)}, u32[]{:S(2)}) collective-permute-start(bf16[2048,128]{1,0:T(8,128)(2,1)S(1)} %collective-permute-done.7), channel_id=1, source_target_pairs={{0,32},{1,33},{2,34},{3,35},{4,36},{5,37},{6,38},{7,39},{8,40},{9,... | collective-permute-start | bytes 1572872 | tf_op jit(solution)/shard_map/ppermute | solution.py:167
  65.7 15.2 %collective-permute-start.12 = (bf16[2048,128]{1,0:T(8,128)(2,1)S(1)}, bf16[2048,128]{1,0:T(8,128)(2,1)S(1)}, u32[]{:S(2)}, u32[]{:S(2)}) collective-permute-start(bf16[2048,128]{1,0:T(8,128)(2,1)S(1)} %collective-permute-done.5), channel_id=1, source_target_pairs={{0,32},{1,33},{2,34},{3,35},{4,36},{5,37},{6,38},{7,39},{8,40},{9,... | collective-permute-start | bytes 1572872 | tf_op jit(solution)/shard_map/ppermute | solution.py:167
  67.8 15.0 %collective-permute-start.3 = (bf16[2048,128]{1,0:T(8,128)(2,1)S(1)}, bf16[2048,128]{1,0:T(8,128)(2,1)S(1)}, u32[]{:S(2)}, u32[]{:S(2)}) collective-permute-start(bf16[2048,128]{1,0:T(8,128)(2,1)S(1)} %slice.9), channel_id=1, source_target_pairs={{0,12},{1,13},{2,14},{3,15},{4,0},{5,1},{6,2},{7,3},{8,4},{9,5},{1... | collective-permute-start | bytes 1572872 | tf_op jit(solution)/shard_map/ppermute | solution.py:167
  68.7 17.4 %collective-permute-start.4 = (bf16[4096,128]{1,0:T(8,128)(2,1)S(1)}, bf16[4096,128]{1,0:T(8,128)(2,1)S(1)}, u32[]{:S(2)}, u32[]{:S(2)}) collective-permute-start(bf16[4096,128]{1,0:T(8,128)(2,1)S(1)} %get-tuple-element.11), channel_id=1, source_target_pairs={{0,1},{1,0},{2,3},{3,2},{4,5},{5,4},{6,7},{7,6},{8,9},{9,8},{10,11... | collective-permute-start | bytes 3145736 | tf_op jit(solution)/shard_map/ppermute | solution.py:167
  70.5 14.7 %collective-permute-start.2 = (bf16[2048,128]{1,0:T(8,128)(2,1)S(1)}, bf16[2048,128]{1,0:T(8,128)(2,1)S(1)}, u32[]{:S(2)}, u32[]{:S(2)}) collective-permute-start(bf16[2048,128]{1,0:T(8,128)(2,1)S(1)} %slice.8), channel_id=1, source_target_pairs={{0,4},{1,5},{2,6},{3,7},{4,8},{5,9},{6,10},{7,11},{8,12},{9,13},{1... | collective-permute-start | bytes 1572872 | tf_op jit(solution)/shard_map/ppermute | solution.py:167
  71.2 14.0 %collective-permute-start.13 = (bf16[2048,128]{1,0:T(8,128)(2,1)S(1)}, bf16[2048,128]{1,0:T(8,128)(2,1)S(1)}, u32[]{:S(2)}, u32[]{:S(2)}) collective-permute-start(bf16[2048,128]{1,0:T(8,128)(2,1)S(1)} %collective-permute-done.9), channel_id=1, source_target_pairs={{0,96},{1,97},{2,98},{3,99},{4,100},{5,101},{6,102},{7,103},{8,104... | collective-permute-start | bytes 1572872 | tf_op jit(solution)/shard_map/ppermute | solution.py:167
  80.9 5.2 %collective-permute-start.10 = (bf16[4096,128]{1,0:T(8,128)(2,1)S(1)}, bf16[4096,128]{1,0:T(8,128)(2,1)S(1)}, u32[]{:S(2)}, u32[]{:S(2)}) collective-permute-start(bf16[4096,128]{1,0:T(8,128)(2,1)S(1)} %collective-permute-done), channel_id=1, source_target_pairs={{0,1},{1,0},{2,3},{3,2},{4,5},{5,4},{6,7},{7,6},{8,9},{9,8},{10,11... | collective-permute-start | bytes 3145736 | tf_op jit(solution)/shard_map/ppermute | solution.py:167
  82.8 3.8 %collective-permute-start.11 = (bf16[4096,128]{1,0:T(8,128)(2,1)S(1)}, bf16[4096,128]{1,0:T(8,128)(2,1)S(1)}, u32[]{:S(2)}, u32[]{:S(2)}) collective-permute-start(bf16[4096,128]{1,0:T(8,128)(2,1)S(1)} %collective-permute-done.1), channel_id=1, source_target_pairs={{0,1},{1,0},{2,3},{3,2},{4,5},{5,4},{6,7},{7,6},{8,9},{9,8},{10,11... | collective-permute-start | bytes 3145736 | tf_op jit(solution)/shard_map/ppermute | solution.py:167
  85.2 2.4 %collective-permute-start.14 = (bf16[2048,128]{1,0:T(8,128)(2,1)S(1)}, bf16[2048,128]{1,0:T(8,128)(2,1)S(1)}, u32[]{:S(2)}, u32[]{:S(2)}) collective-permute-start(bf16[2048,128]{1,0:T(8,128)(2,1)S(1)} %collective-permute-done.2), channel_id=1, source_target_pairs={{0,1},{1,0},{2,3},{3,2},{4,5},{5,4},{6,7},{7,6},{8,9},{9,8},{10,11... | collective-permute-start | bytes 1572872 | tf_op jit(solution)/shard_map/ppermute | solution.py:167
  86.0 2.3 %collective-permute-start.15 = (bf16[2048,128]{1,0:T(8,128)(2,1)S(1)}, bf16[2048,128]{1,0:T(8,128)(2,1)S(1)}, u32[]{:S(2)}, u32[]{:S(2)}) collective-permute-start(bf16[2048,128]{1,0:T(8,128)(2,1)S(1)} %collective-permute-done.3), channel_id=1, source_target_pairs={{0,1},{1,0},{2,3},{3,2},{4,5},{5,4},{6,7},{7,6},{8,9},{9,8},{10,11... | collective-permute-start | bytes 1572872 | tf_op jit(solution)/shard_map/ppermute | solution.py:167

commit v9 on v8

--- a/solution.py
+++ b/solution.py
@@ -137,28 +137,27 @@
     return turned[...].astype(BF16)
 
 
-def turn_kernel(received, pair, own, wide, turned):
-    wide[...] = received[...].astype(F32)
-    for slot in range(2):
-        block = turn_block(wide, slot * CB, SENT, turned)
-        pair[pl.ds(slot * HALF_ROWS, HALF_ROWS), :] = block
-        if slot == 0:
-            own[...] = block
-
-
-def turn(received):
+def turn_own_kernel(received, own, wide, turned):
+    wide[...] = received[:, 0:CB, :].astype(F32).reshape(wide.shape)
+    own[...] = turn_block(wide, 0, CB, turned)
+
+
+def turn_pair_kernel(received, own, pair, wide, turned):
+    wide[...] = received[:, CB : 2 * CB, :].astype(F32).reshape(wide.shape)
+    pair[0:HALF_ROWS, :] = own[...]
+    pair[HALF_ROWS:, :] = turn_block(wide, 0, CB, turned)
+
+
+def turn(kernel, rows, *operands):
     return pl.pallas_call(
-        turn_kernel,
-        in_specs=[pl.BlockSpec(memory_space=pltpu.VMEM)],
-        out_specs=[pl.BlockSpec(memory_space=pltpu.VMEM)] * 2,
-        out_shape=[
-            jax.ShapeDtypeStruct((2 * HALF_ROWS, NW), BF16),
-            jax.ShapeDtypeStruct((HALF_ROWS, NW), BF16),
-        ],
-        scratch_shapes=[pltpu.VMEM((NW * SENT, 2 * F), F32), pltpu.VMEM((HALF_ROWS, NW), F32)],
+        kernel,
+        in_specs=[pl.BlockSpec(memory_space=pltpu.VMEM) for _ in operands],
+        out_specs=pl.BlockSpec(memory_space=pltpu.VMEM),
+        out_shape=jax.ShapeDtypeStruct((rows, NW), BF16),
+        scratch_shapes=[pltpu.VMEM((NW * CB, 2 * F), F32), pltpu.VMEM((HALF_ROWS, NW), F32)],
         compiler_params=pltpu.CompilerParams(vmem_limit_bytes=24 << 20),
         name="turn",
-    )(received)
+    )(*operands)
 
 
 def shift(x, axis, amount):
@@ -271,7 +270,8 @@
     received = lax.all_to_all(
         spectra.reshape(NW, SENT, 2 * F), AXES, split_axis=0, concat_axis=0, tiled=True
     )
-    pair, own = turn(received.reshape(NW * SENT, 2 * F))
+    own = turn(turn_own_kernel, HALF_ROWS, received)
+    pair = turn(turn_pair_kernel, 2 * HALF_ROWS, received, own)
     rows, others, cols = gather_rings(pair, own)
     return product(wid, rows + others + cols)
 

time: 95.6 us -> 95.1 us (level)
    pallas_call x1 -> x2, Pallas kernels: 2.54 us -> 2.06 us  [turn(): pl.pallas_call(kernel, in_specs=[pl.BlockSpec(memory_space=pltpu.VMEM) fo...]
where the time goes in v9:
time: 95.1 us; the launch traced here: 94.9 us
  waiting for transfers between devices  33.5 us (35%)
  blocking collectives  30.7 us (32%)
  Pallas kernels  17.4 us (18%)
  starting transfers between devices  13 us (14%)
    ppermute x16, waiting for transfers between devices, shift(): lax.ppermute(x, AXES, [(int(a), int(b)) for a, b in zip(ids.ravel(), to.r...  33.5 us
    all_to_all x1, blocking collectives, body(): lax.all_to_all(spectra.reshape(NW, SENT, 2 * F), AXES, split_axis=0, conc...  30.7 us
    ppermute x16, starting transfers between devices, shift(): lax.ppermute(x, AXES, [(int(a), int(b)) for a, b in zip(ids.ravel(), to.r...  13 us
    pallas_call x1, Pallas kernels, whiten(): pl.pallas_call(whiten_kernel, grid_spec=pltpu.PrefetchScalarGridSpec(num_...  8.53 us
    pallas_call x1, Pallas kernels, product(): pl.pallas_call(product_kernel, in_specs=[pl.BlockSpec(memory_space=pltpu....  6.83 us
    pallas_call x2, Pallas kernels, turn(): pl.pallas_call(kernel, in_specs=[pl.BlockSpec(memory_space=pltpu.VMEM) fo...  2.06 us
  transfers between devices with their start and end apart: 16, of which 9 were waited for; matrix products, arithmetic and copies ran while one was open for 0% of the time, Pallas kernels for 0%

profile of v9, /device:TPU:1, one launch (start us, length us, event | category | flops | bytes accessed | tf_op | source)
XLA Modules:
  0.0 94.9 jit_solution(810489168872960400)
XLA Ops:
  0.0 8.5 %whiten.1 = bf16[4096,128]{1,0:T(8,128)(2,1)} custom-call(s32[2048]{0:T(1024)} %order.1, s32[4]{0:T(128)} %slab.1, s32[1]{0:T(128)} %bitcast.wid, bf16[1,2048,512]{2,1,0:T(8,128)(2,1)} %raw.1, s32[16,128]{1,0:T(8,128)} %bitcast.40, bf16[512,128]{1,0:T(8,128)(2,1)} %constant.13.clone.dft), custom_call_target="tpu_custom_call" | custom-call | tf_op jit(solution)/shard_map/whiten/pallas_call | solution.py:108
  8.5 30.7 %all_to_all.5.received = bf16[128,32,128]{2,1,0:T(8,128)(2,1)S(1)} all-to-all(bf16[128,32,128]{2,1,0:T(8,128)(2,1)} %bitcast.39), channel_id=1, replica_groups=mesh['src'=8,'rcv'=16] {'src','rcv'}, dimensions={0} | all-to-all | bytes 2097152 | tf_op jit(solution)/shard_map/all_to_all | solution.py:270
  39.2 1.0 %turn.2.own = bf16[2048,128]{1,0:T(8,128)(2,1)S(1)} custom-call(bf16[128,32,128]{2,1,0:T(8,128)(2,1)S(1)} %all_to_all.5.received), custom_call_target="tpu_custom_call" | custom-call | tf_op jit(solution)/shard_map/turn/pallas_call | solution.py:152
  40.3 1.0 %turn.3 = bf16[4096,128]{1,0:T(8,128)(2,1)S(1)} custom-call(bf16[128,32,128]{2,1,0:T(8,128)(2,1)S(1)} %all_to_all.5.received, bf16[2048,128]{1,0:T(8,128)(2,1)S(1)} %turn.2.own), custom_call_target="tpu_custom_call" | custom-call | tf_op jit(solution)/shard_map/turn/pallas_call | solution.py:152
  41.3 0.8 collective-permute-start.1
  42.1 0.8 collective-permute-start
  42.8 0.0 collective-permute-start.7
  42.9 0.4 collective-permute-start.5
  43.2 2.3 %collective-permute-start.6 = (bf16[2048,128]{1,0:T(8,128)(2,1)S(1)}, bf16[2048,128]{1,0:T(8,128)(2,1)S(1)}, u32[]{:S(2)}, u32[]{:S(2)}) collective-permute-start(bf16[2048,128]{1,0:T(8,128)(2,1)S(1)} %turn.2.own), channel_id=1, source_target_pairs={{0,96},{1,97},{2,98},{3,99},{4,100},{5,101},{6,102},{7,103},{8,104... | collective-permute-start | bytes 1572872 | tf_op jit(solution)/shard_map/ppermute | solution.py:166
  45.5 9.3 %collective-permute-done.7 = bf16[2048,128]{1,0:T(8,128)(2,1)S(1)} collective-permute-done((bf16[2048,128]{1,0:T(8,128)(2,1)S(1)}, bf16[2048,128]{1,0:T(8,128)(2,1)S(1)}, u32[]{:S(2)}, u32[]{:S(2)}) %collective-permute-start.7) | collective-permute-done | bytes 524320 | tf_op jit(solution)/shard_map/ppermute | solution.py:166
  54.9 0.2 collective-permute-start.9
  55.1 0.5 collective-permute-done.5
  55.6 0.8 collective-permute-start.8
  56.3 8.9 %collective-permute-done.1 = bf16[4096,128]{1,0:T(8,128)(2,1)S(1)} collective-permute-done((bf16[4096,128]{1,0:T(8,128)(2,1)S(1)}, bf16[4096,128]{1,0:T(8,128)(2,1)S(1)}, u32[]{:S(2)}, u32[]{:S(2)}) %collective-permute-start.1) | collective-permute-done | bytes 1048608 | tf_op jit(solution)/shard_map/ppermute | solution.py:166
  65.3 2.1 %collective-permute-done = bf16[4096,128]{1,0:T(8,128)(2,1)S(1)} collective-permute-done((bf16[4096,128]{1,0:T(8,128)(2,1)S(1)}, bf16[4096,128]{1,0:T(8,128)(2,1)S(1)}, u32[]{:S(2)}, u32[]{:S(2)}) %collective-permute-start) | collective-permute-done | bytes 1048608 | tf_op jit(solution)/shard_map/ppermute | solution.py:166
  67.4 0.8 collective-permute-start.3
  68.2 1.8 %collective-permute-start.4 = (bf16[4096,128]{1,0:T(8,128)(2,1)S(1)}, bf16[4096,128]{1,0:T(8,128)(2,1)S(1)}, u32[]{:S(2)}, u32[]{:S(2)}) collective-permute-start(bf16[4096,128]{1,0:T(8,128)(2,1)S(1)} %turn.3), channel_id=1, source_target_pairs={{0,1},{1,0},{2,3},{3,2},{4,5},{5,4},{6,7},{7,6},{8,9},{9,8},{10,11... | collective-permute-start | bytes 3145736 | tf_op jit(solution)/shard_map/ppermute | solution.py:166
  70.0 0.0 collective-permute-done.9
  70.0 0.7 collective-permute-start.2
  70.7 0.0 collective-permute-done.8
  70.7 1.7 %collective-permute-start.13 = (bf16[2048,128]{1,0:T(8,128)(2,1)S(1)}, bf16[2048,128]{1,0:T(8,128)(2,1)S(1)}, u32[]{:S(2)}, u32[]{:S(2)}) collective-permute-start(bf16[2048,128]{1,0:T(8,128)(2,1)S(1)} %collective-permute-done.9), channel_id=1, source_target_pairs={{0,96},{1,97},{2,98},{3,99},{4,100},{5,101},{6,102},{7,103},{8,104... | collective-permute-start | bytes 1572872 | tf_op jit(solution)/shard_map/ppermute | solution.py:166
  72.4 8.0 %collective-permute-done.12 = bf16[2048,128]{1,0:T(8,128)(2,1)S(1)} collective-permute-done((bf16[2048,128]{1,0:T(8,128)(2,1)S(1)}, bf16[2048,128]{1,0:T(8,128)(2,1)S(1)}, u32[]{:S(2)}, u32[]{:S(2)}) %collective-permute-start.12) | collective-permute-done | bytes 524320 | tf_op jit(solution)/shard_map/ppermute | solution.py:166
  80.4 1.9 %collective-permute-start.10 = (bf16[4096,128]{1,0:T(8,128)(2,1)S(1)}, bf16[4096,128]{1,0:T(8,128)(2,1)S(1)}, u32[]{:S(2)}, u32[]{:S(2)}) collective-permute-start(bf16[4096,128]{1,0:T(8,128)(2,1)S(1)} %collective-permute-done), channel_id=1, source_target_pairs={{0,1},{1,0},{2,3},{3,2},{4,5},{5,4},{6,7},{7,6},{8,9},{9,8},{10,11... | collective-permute-start | bytes 3145736 | tf_op jit(solution)/shard_map/ppermute | solution.py:166
  82.3 0.0 collective-permute-start.11
  82.3 2.4 %collective-permute-done.2 = bf16[2048,128]{1,0:T(8,128)(2,1)S(1)} collective-permute-done((bf16[2048,128]{1,0:T(8,128)(2,1)S(1)}, bf16[2048,128]{1,0:T(8,128)(2,1)S(1)}, u32[]{:S(2)}, u32[]{:S(2)}) %collective-permute-start.2) | collective-permute-done | bytes 524320 | tf_op jit(solution)/shard_map/ppermute | solution.py:166
  84.7 0.9 collective-permute-start.14
  85.6 0.0 collective-permute-start.15
  85.6 0.0 collective-permute-done.4
  85.6 0.5 collective-permute-done.11
  86.1 1.0 %collective-permute-done.14 = bf16[2048,128]{1,0:T(8,128)(2,1)S(1)} collective-permute-done((bf16[2048,128]{1,0:T(8,128)(2,1)S(1)}, bf16[2048,128]{1,0:T(8,128)(2,1)S(1)}, u32[]{:S(2)}, u32[]{:S(2)}) %collective-permute-start.14) | collective-permute-done | bytes 524320 | tf_op jit(solution)/shard_map/ppermute | solution.py:166
  87.1 0.7 collective-permute-done.15
  87.9 6.8 %product.1 = f32[2,64,256,128]{3,2,1,0:T(8,128)} custom-call(s32[1]{0:T(128)} %bitcast.wid, bf16[128,32,128]{2,1,0:T(8,128)(2,1)S(1)} %bitcast.22, bf16[128,32,128]{2,1,0:T(8,128)(2,1)S(1)} %bitcast.24, bf16[128,32,128]{2,1,0:T(8,128)(2,1)S(1)} %bitcast.23, bf16[64,32,128]{2,1,0:T(8,128)(2,1)S(1)} %bitcast.35, bf16[64,32,128]{2,1,0:T(8,128)(2,1)S(1)} %bitcast.34, ...), custom_call_target="tpu_custom_call" | custom-call | tf_op jit(solution)/shard_map/product/pallas_call | solution.py:248
  (7 shorter events, 0.1 us)
Async XLA Ops:
  41.3 23.9 %collective-permute-start.1 = (bf16[4096,128]{1,0:T(8,128)(2,1)S(1)}, bf16[4096,128]{1,0:T(8,128)(2,1)S(1)}, u32[]{:S(2)}, u32[]{:S(2)}) collective-permute-start(bf16[4096,128]{1,0:T(8,128)(2,1)S(1)} %turn.3), channel_id=1, source_target_pairs={{0,12},{1,13},{2,14},{3,15},{4,0},{5,1},{6,2},{7,3},{8,4},{9,5},{1... | collective-permute-start | bytes 3145736 | tf_op jit(solution)/shard_map/ppermute | solution.py:166
  42.1 25.3 %collective-permute-start = (bf16[4096,128]{1,0:T(8,128)(2,1)S(1)}, bf16[4096,128]{1,0:T(8,128)(2,1)S(1)}, u32[]{:S(2)}, u32[]{:S(2)}) collective-permute-start(bf16[4096,128]{1,0:T(8,128)(2,1)S(1)} %turn.3), channel_id=1, source_target_pairs={{0,4},{1,5},{2,6},{3,7},{4,8},{5,9},{6,10},{7,11},{8,12},{9,13},{1... | collective-permute-start | bytes 3145736 | tf_op jit(solution)/shard_map/ppermute | solution.py:166
  42.8 12.0 %collective-permute-start.7 = (bf16[2048,128]{1,0:T(8,128)(2,1)S(1)}, bf16[2048,128]{1,0:T(8,128)(2,1)S(1)}, u32[]{:S(2)}, u32[]{:S(2)}) collective-permute-start(bf16[2048,128]{1,0:T(8,128)(2,1)S(1)} %turn.2.own), channel_id=1, source_target_pairs={{0,16},{1,17},{2,18},{3,19},{4,20},{5,21},{6,22},{7,23},{8,24},{9,... | collective-permute-start | bytes 1572872 | tf_op jit(solution)/shard_map/ppermute | solution.py:166
  42.9 12.7 %collective-permute-start.5 = (bf16[2048,128]{1,0:T(8,128)(2,1)S(1)}, bf16[2048,128]{1,0:T(8,128)(2,1)S(1)}, u32[]{:S(2)}, u32[]{:S(2)}) collective-permute-start(bf16[2048,128]{1,0:T(8,128)(2,1)S(1)} %turn.2.own), channel_id=1, source_target_pairs={{0,32},{1,33},{2,34},{3,35},{4,36},{5,37},{6,38},{7,39},{8,40},{9,... | collective-permute-start | bytes 1572872 | tf_op jit(solution)/shard_map/ppermute | solution.py:166
  43.2 25.0 %collective-permute-start.6 = (bf16[2048,128]{1,0:T(8,128)(2,1)S(1)}, bf16[2048,128]{1,0:T(8,128)(2,1)S(1)}, u32[]{:S(2)}, u32[]{:S(2)}) collective-permute-start(bf16[2048,128]{1,0:T(8,128)(2,1)S(1)} %turn.2.own), channel_id=1, source_target_pairs={{0,96},{1,97},{2,98},{3,99},{4,100},{5,101},{6,102},{7,103},{8,104... | collective-permute-start | bytes 1572872 | tf_op jit(solution)/shard_map/ppermute | solution.py:166
  54.9 15.1 %collective-permute-start.9 = (bf16[2048,128]{1,0:T(8,128)(2,1)S(1)}, bf16[2048,128]{1,0:T(8,128)(2,1)S(1)}, u32[]{:S(2)}, u32[]{:S(2)}) collective-permute-start(bf16[2048,128]{1,0:T(8,128)(2,1)S(1)} %collective-permute-done.7), channel_id=1, source_target_pairs={{0,96},{1,97},{2,98},{3,99},{4,100},{5,101},{6,102},{7,103},{8,104... | collective-permute-start | bytes 1572872 | tf_op jit(solution)/shard_map/ppermute | solution.py:166
  55.6 15.2 %collective-permute-start.8 = (bf16[2048,128]{1,0:T(8,128)(2,1)S(1)}, bf16[2048,128]{1,0:T(8,128)(2,1)S(1)}, u32[]{:S(2)}, u32[]{:S(2)}) collective-permute-start(bf16[2048,128]{1,0:T(8,128)(2,1)S(1)} %collective-permute-done.7), channel_id=1, source_target_pairs={{0,32},{1,33},{2,34},{3,35},{4,36},{5,37},{6,38},{7,39},{8,40},{9,... | collective-permute-start | bytes 1572872 | tf_op jit(solution)/shard_map/ppermute | solution.py:166
  65.2 15.2 %collective-permute-start.12 = (bf16[2048,128]{1,0:T(8,128)(2,1)S(1)}, bf16[2048,128]{1,0:T(8,128)(2,1)S(1)}, u32[]{:S(2)}, u32[]{:S(2)}) collective-permute-start(bf16[2048,128]{1,0:T(8,128)(2,1)S(1)} %collective-permute-done.5), channel_id=1, source_target_pairs={{0,32},{1,33},{2,34},{3,35},{4,36},{5,37},{6,38},{7,39},{8,40},{9,... | collective-permute-start | bytes 1572872 | tf_op jit(solution)/shard_map/ppermute | solution.py:166
  67.4 15.0 %collective-permute-start.3 = (bf16[2048,128]{1,0:T(8,128)(2,1)S(1)}, bf16[2048,128]{1,0:T(8,128)(2,1)S(1)}, u32[]{:S(2)}, u32[]{:S(2)}) collective-permute-start(bf16[2048,128]{1,0:T(8,128)(2,1)S(1)} %slice.9), channel_id=1, source_target_pairs={{0,12},{1,13},{2,14},{3,15},{4,0},{5,1},{6,2},{7,3},{8,4},{9,5},{1... | collective-permute-start | bytes 1572872 | tf_op jit(solution)/shard_map/ppermute | solution.py:166
  68.2 17.4 %collective-permute-start.4 = (bf16[4096,128]{1,0:T(8,128)(2,1)S(1)}, bf16[4096,128]{1,0:T(8,128)(2,1)S(1)}, u32[]{:S(2)}, u32[]{:S(2)}) collective-permute-start(bf16[4096,128]{1,0:T(8,128)(2,1)S(1)} %turn.3), channel_id=1, source_target_pairs={{0,1},{1,0},{2,3},{3,2},{4,5},{5,4},{6,7},{7,6},{8,9},{9,8},{10,11... | collective-permute-start | bytes 3145736 | tf_op jit(solution)/shard_map/ppermute | solution.py:166
  70.0 14.7 %collective-permute-start.2 = (bf16[2048,128]{1,0:T(8,128)(2,1)S(1)}, bf16[2048,128]{1,0:T(8,128)(2,1)S(1)}, u32[]{:S(2)}, u32[]{:S(2)}) collective-permute-start(bf16[2048,128]{1,0:T(8,128)(2,1)S(1)} %slice.8), channel_id=1, source_target_pairs={{0,4},{1,5},{2,6},{3,7},{4,8},{5,9},{6,10},{7,11},{8,12},{9,13},{1... | collective-permute-start | bytes 1572872 | tf_op jit(solution)/shard_map/ppermute | solution.py:166
  70.7 14.0 %collective-permute-start.13 = (bf16[2048,128]{1,0:T(8,128)(2,1)S(1)}, bf16[2048,128]{1,0:T(8,128)(2,1)S(1)}, u32[]{:S(2)}, u32[]{:S(2)}) collective-permute-start(bf16[2048,128]{1,0:T(8,128)(2,1)S(1)} %collective-permute-done.9), channel_id=1, source_target_pairs={{0,96},{1,97},{2,98},{3,99},{4,100},{5,101},{6,102},{7,103},{8,104... | collective-permute-start | bytes 1572872 | tf_op jit(solution)/shard_map/ppermute | solution.py:166
  80.4 5.2 %collective-permute-start.10 = (bf16[4096,128]{1,0:T(8,128)(2,1)S(1)}, bf16[4096,128]{1,0:T(8,128)(2,1)S(1)}, u32[]{:S(2)}, u32[]{:S(2)}) collective-permute-start(bf16[4096,128]{1,0:T(8,128)(2,1)S(1)} %collective-permute-done), channel_id=1, source_target_pairs={{0,1},{1,0},{2,3},{3,2},{4,5},{5,4},{6,7},{7,6},{8,9},{9,8},{10,11... | collective-permute-start | bytes 3145736 | tf_op jit(solution)/shard_map/ppermute | solution.py:166
  82.3 3.8 %collective-permute-start.11 = (bf16[4096,128]{1,0:T(8,128)(2,1)S(1)}, bf16[4096,128]{1,0:T(8,128)(2,1)S(1)}, u32[]{:S(2)}, u32[]{:S(2)}) collective-permute-start(bf16[4096,128]{1,0:T(8,128)(2,1)S(1)} %collective-permute-done.1), channel_id=1, source_target_pairs={{0,1},{1,0},{2,3},{3,2},{4,5},{5,4},{6,7},{7,6},{8,9},{9,8},{10,11... | collective-permute-start | bytes 3145736 | tf_op jit(solution)/shard_map/ppermute | solution.py:166
  84.7 2.4 %collective-permute-start.14 = (bf16[2048,128]{1,0:T(8,128)(2,1)S(1)}, bf16[2048,128]{1,0:T(8,128)(2,1)S(1)}, u32[]{:S(2)}, u32[]{:S(2)}) collective-permute-start(bf16[2048,128]{1,0:T(8,128)(2,1)S(1)} %collective-permute-done.2), channel_id=1, source_target_pairs={{0,1},{1,0},{2,3},{3,2},{4,5},{5,4},{6,7},{7,6},{8,9},{9,8},{10,11... | collective-permute-start | bytes 1572872 | tf_op jit(solution)/shard_map/ppermute | solution.py:166
  85.6 2.3 %collective-permute-start.15 = (bf16[2048,128]{1,0:T(8,128)(2,1)S(1)}, bf16[2048,128]{1,0:T(8,128)(2,1)S(1)}, u32[]{:S(2)}, u32[]{:S(2)}) collective-permute-start(bf16[2048,128]{1,0:T(8,128)(2,1)S(1)} %collective-permute-done.3), channel_id=1, source_target_pairs={{0,1},{1,0},{2,3},{3,2},{4,5},{5,4},{6,7},{7,6},{8,9},{9,8},{10,11... | collective-permute-start | bytes 1572872 | tf_op jit(solution)/shard_map/ppermute | solution.py:166
